TPU v7x, 32 devices: a whole 2x2x4 slice. The times are simulated.
32 devices in a mesh: row: 4 (over y, core), col: 8 (over z, x).
Axes of the slice: x: 2, y: 2, z: 4, core: 2. Of those that a mesh axis runs over, the one named last changes fastest.
Arguments:
- tokens: bfloat16 [2, 2048, 1024], P(None, 'col', 'row'), may hold values from -6 to 6
- streams: bfloat16 [2, 3, 2048, 1024], P(None, None, 'col', 'row'), may hold values from -6 to 6
- cotangent: bfloat16 [2, 3, 2048, 1024], P(None, None, 'col', 'row'), may hold values from -6 to 6
- block_ids: int32 [2, 4, 512], P(None, 'row'), may hold values from 0 to 3, never falling along the last dimension, each value on 1 to 256 neighbouring positions
- bucket_ids: int32 [1023], replicated, may hold values from 0 to 31
- w_qkv: bfloat16 [1024, 3, 1024], P('row', None, 'col'), may hold values from -0.1875 to 0.1875
- enc_table: float32 [16, 32], P('col'), may hold values from -4 to 4
- w_out: bfloat16 [1024, 1024], P('col', 'row'), may hold values from -1.5 to 1.5
- attention_norm_gain: float32 [1024], P('row'), may hold values from 0.5 to 1.5
- attn_bias: float32 [1024], P('row'), may hold values from -3 to 3
- w_up: bfloat16 [1024, 4096], P('row', 'col'), may hold values from -0.1875 to 0.1875
- w_down: bfloat16 [4096, 1024], P('col', 'row'), may hold values from -0.125 to 0.125
- ffn_gain: float32 [1024], P('row'), may hold values from 0.5 to 1.5
- ffn_bias: float32 [1024], P('row'), may hold values from -3 to 3
- w_query: bfloat16 [1024, 1024], P('row', 'col'), may hold values from -0.1875 to 0.1875
- w_keyval: bfloat16 [1024, 2, 1024], P('row', None, 'col'), may hold values from -0.1875 to 0.1875
- cross_table: float32 [16, 32], P('col'), may hold values from -4 to 4
- w_cross_out: bfloat16 [1024, 1024], P('col', 'row'), may hold values from -1.5 to 1.5
- cross_gain: float32 [1024], P('row'), may hold values from 0.5 to 1.5
- cross_bias: float32 [1024], P('row'), may hold values from -3 to 3
Outputs:
- output: float32 [2, 3, 2048, 1024], P(None, None, 'col', 'row')
- grad_tokens: float32 [2, 2048, 1024], P(None, 'col', 'row')
- grad_streams: float32 [2, 3, 2048, 1024], P(None, None, 'col', 'row')
- gradient_query_key_value_weight: float32 [1024, 3, 1024], P('row', None, 'col')
- grad_enc_table: float32 [16, 32], P('col')
- grad_w_out: float32 [1024, 1024], P('col', 'row')
- grad_attn_gain: float32 [1024], P('row')
- grad_attn_bias: float32 [1024], P('row')
- grad_w_up: float32 [1024, 4096], P('row', 'col')
- grad_w_down: float32 [4096, 1024], P('col', 'row')
- grad_ffn_gain: float32 [1024], P('row')
- grad_ffn_bias: float32 [1024], P('row')
- grad_w_query: float32 [1024, 1024], P('row', 'col')
- grad_w_keyval: float32 [1024, 2, 1024], P('row', None, 'col')
- grad_cross_table: float32 [16, 32], P('col')
- grad_w_cross_out: float32 [1024, 1024], P('col', 'row')
- grad_cross_gain: float32 [1024], P('row')
- grad_cross_bias: float32 [1024], P('row')
Inputs may be any that keep to these rules, and one draw needn't show every extreme that they name: `block_ids`: within a sequence the ids never fall, and one id holds 1 to 256 positions.
All inputs are finite; a program needn't handle non-finite values.
Results may differ from a plain program's by a relative error of at most 0.023.
Values may be sent and summed in bfloat16 or wider, within the bound.
A program may use at most 384 MiB of HBM per device.

v0:
```python
import jax
import jax.numpy as jnp
from jax import lax
from jax.sharding import PartitionSpec as P

D = 1024


epsilon = 1e-05
neg_fill = -1e30
highest = lax.Precision.HIGHEST


def gather_cols(local_rows):
    return lax.all_gather(local_rows, "col", axis=1, tiled=True)


def gather_rows(local_rows):
    return lax.all_gather(local_rows, "row", axis=1, tiled=True)


def product(matmul_operand, weight_matrix):
    return jnp.einsum(
        "ray,yw->raw", matmul_operand, weight_matrix, preferred_element_type=jnp.float32
    )


def rows_product(operand_full, matrix):
    return lax.psum_scatter(product(operand_full, matrix), "row", scatter_dimension=1, tiled=True)


def cols_product(operand_full, matrix):
    return lax.psum_scatter(product(operand_full, matrix), "col", scatter_dimension=1, tiled=True)


def weight_grad(matmul_operand, upstream_gradient):
    return jnp.einsum(
        "bpt,bpr->tr", matmul_operand, upstream_gradient, preferred_element_type=jnp.float32
    )


def gelu_exact(argument):
    return jax.nn.gelu(argument, approximate=False)


def norm_forward(residual, gain_vec, bias_vec):
    local_sum = jnp.sum(residual, axis=-1)
    average = lax.psum(local_sum, "row") / D
    centered = residual - average[..., None]
    spread = lax.psum(jnp.sum(centered * centered, axis=-1), "row") / D
    inv_std = lax.rsqrt(spread + epsilon)
    normed = centered * inv_std[..., None]
    return (normed * gain_vec + bias_vec, normed, inv_std)


def norm_back(out_grad, normed, inv_std, gain_vec):
    scaled_grad = out_grad * gain_vec
    first_moment, second_moment = lax.psum(
        (jnp.sum(scaled_grad, axis=-1), jnp.sum(scaled_grad * normed, axis=-1)), "row"
    )
    resid_grad = inv_std[..., None] * (
        scaled_grad - first_moment[..., None] / D - normed * (second_moment[..., None] / D)
    )
    return (resid_grad, jnp.sum(out_grad * normed, axis=(0, 1)), jnp.sum(out_grad, axis=(0, 1)))


def bucket_onehot(bucket_ids, bucket_count):
    return (bucket_ids[None, :] == jnp.arange(bucket_count, dtype=jnp.int32)[:, None]).astype(
        jnp.float32
    )


def block_logits(query_blk, key_rows, offsets, segment, first_row):
    row_count = query_blk.shape[2]
    length = key_rows.shape[1]
    score_scale = query_blk.shape[-1] ** (-0.5)
    raw_scores = jnp.einsum(
        "snqhd,nkhd->snhqk", query_blk, key_rows, preferred_element_type=jnp.float32
    )
    places = jnp.arange(length, dtype=jnp.int32)
    query_pos = first_row + jnp.arange(row_count, dtype=jnp.int32)
    offset_index = places[None, :] - query_pos[:, None] + (length - 1)
    pos_bias = jnp.take(offsets, offset_index, axis=1)
    visible = segment[:, first_row : first_row + row_count, None] >= segment[:, None, :]
    return jnp.where(
        visible[None, :, None], raw_scores * score_scale + pos_bias[None, None], neg_fill
    )


def attend(queries, key_rows, value_rows, segment, offsets):
    score_logits = block_logits(queries, key_rows, offsets, segment, 0)
    row_max = jnp.max(score_logits, axis=-1, keepdims=True)
    log_total = row_max + jnp.log(jnp.sum(jnp.exp(score_logits - row_max), axis=-1, keepdims=True))
    weights = jnp.exp(score_logits - log_total).astype(jnp.bfloat16)
    mixed_parts = jnp.einsum(
        "snhqk,nkhd->snqhd", weights, value_rows, preferred_element_type=jnp.float32
    )
    lse_parts = log_total[..., 0]
    return (mixed_parts, lse_parts)


def diagonal_sums(summand):
    head_count, row_count, length = summand.shape
    flipped = summand[:, ::-1, :]
    padded = jnp.concatenate(
        [flipped, jnp.zeros((head_count, row_count, row_count), summand.dtype)], axis=2
    )
    flattened = padded.reshape(head_count, row_count * (length + row_count))[
        :, : row_count * (length + row_count - 1)
    ]
    return jnp.sum(flattened.reshape(head_count, row_count, length + row_count - 1), axis=1)


def attend_back(queries, key_rows, value_rows, segment, offsets, onehot, log_totals, mix_grad):
    length = key_rows.shape[1]
    block_rows = min(512, length)
    score_scale = queries.shape[-1] ** (-0.5)
    offset_grad = jnp.zeros(offsets.shape, jnp.float32)
    score_logits = block_logits(queries, key_rows, offsets, segment, 0)
    probability = jnp.exp(score_logits - log_totals[:, :, :, 0:block_rows, None])
    prob_grad = jnp.einsum(
        "snqhd,nkhd->snhqk", mix_grad, value_rows, preferred_element_type=jnp.float32
    )
    logit_grad = probability * (
        prob_grad - jnp.sum(probability * prob_grad, axis=-1, keepdims=True)
    )
    scaled = (logit_grad * score_scale).astype(jnp.bfloat16)
    query_parts = jnp.einsum(
        "snhqk,nkhd->snqhd", scaled, key_rows, preferred_element_type=jnp.float32
    )
    key_grad = jnp.einsum("snhqk,snqhd->nkhd", scaled, queries, preferred_element_type=jnp.float32)
    value_grad = jnp.einsum(
        "snhqk,snqhd->nkhd",
        probability.astype(jnp.bfloat16),
        mix_grad,
        preferred_element_type=jnp.float32,
    )
    low_end = length - block_rows
    offset_grad = offset_grad.at[:, low_end : low_end + length + block_rows - 1].add(
        diagonal_sums(jnp.sum(logit_grad, axis=(0, 1)))
    )
    table_grad = jnp.dot(offset_grad, onehot.T, precision=highest)
    return (query_parts, key_grad, value_grad, table_grad)


def on_device(
    tokens,
    streams,
    cotangent,
    block_ids,
    bucket_ids,
    w_qkv,
    enc_table,
    w_out,
    attention_norm_gain,
    attn_bias,
    w_up,
    w_down,
    ffn_gain,
    ffn_bias,
    w_query,
    w_keyval,
    cross_table,
    w_cross_out,
    cross_gain,
    cross_bias,
):
    micro_count = tokens.shape[0]
    stream_count = streams.shape[1]
    seq_rows = block_ids.shape[1]
    length = block_ids.shape[2]
    head_count = enc_table.shape[0]
    bucket_count = enc_table.shape[1]
    row_width = w_qkv.shape[0]
    col_width = w_qkv.shape[2]
    head_dim = col_width // head_count
    row_tokens = seq_rows * length
    qkv_matrix = w_qkv.reshape(row_width, 3 * col_width)
    keyval_matrix = w_keyval.reshape(row_width, 2 * col_width)
    onehot = bucket_onehot(bucket_ids, bucket_count)
    enc_offsets = jnp.dot(enc_table, onehot, precision=highest)
    cross_offsets = jnp.dot(cross_table, onehot, precision=highest)
    qkv_acc = jnp.zeros((row_width, 3 * col_width), jnp.float32)
    out_acc = jnp.zeros(w_out.shape, jnp.float32)
    up_acc = jnp.zeros(w_up.shape, jnp.float32)
    down_acc = jnp.zeros(w_down.shape, jnp.float32)
    query_acc = jnp.zeros(w_query.shape, jnp.float32)
    keyval_acc = jnp.zeros((row_width, 2 * col_width), jnp.float32)
    cross_out_acc = jnp.zeros(w_cross_out.shape, jnp.float32)
    enc_table_acc = jnp.zeros(enc_table.shape, jnp.float32)
    cross_table_acc = jnp.zeros(cross_table.shape, jnp.float32)
    norm_accs = [jnp.zeros((row_width,), jnp.float32) for place_holder in range(6)]
    outputs = []
    token_grads = []
    stream_grads = []
    for micro in range(micro_count):
        segment = block_ids[micro]
        x_in = tokens[micro][None]
        y_in = streams[micro]
        x_full = gather_cols(x_in)
        qkv = (
            rows_product(x_full, qkv_matrix)
            .astype(jnp.bfloat16)
            .reshape(seq_rows, length, 3, head_count, head_dim)
        )
        enc_query = qkv[:, :, 0][None]
        enc_key = qkv[:, :, 1]
        encoder_value_rows = qkv[:, :, 2]
        enc_mixed, enc_lse = attend(enc_query, enc_key, encoder_value_rows, segment, enc_offsets)
        enc_mix = enc_mixed.reshape(1, row_tokens, col_width).astype(jnp.bfloat16)
        mix_full = gather_rows(enc_mix)
        attn_branch = cols_product(mix_full, w_out)
        hidden, normed_one, inv_one = norm_forward(
            x_in.astype(jnp.float32) + attn_branch, attention_norm_gain, attn_bias
        )
        hidden_low = hidden.astype(jnp.bfloat16)
        hidden_full = gather_cols(hidden_low)
        pre_act = rows_product(hidden_full, w_up)
        act_value, gelu_pull = jax.vjp(gelu_exact, pre_act)
        act_low = act_value.astype(jnp.bfloat16)
        act_full = gather_rows(act_low)
        ffn_branch = cols_product(act_full, w_down)
        encoded, normed_two, inv_two = norm_forward(hidden + ffn_branch, ffn_gain, ffn_bias)
        encoded_low = encoded.astype(jnp.bfloat16)
        enc_full = gather_cols(encoded_low)
        keyval = (
            rows_product(enc_full, keyval_matrix)
            .astype(jnp.bfloat16)
            .reshape(seq_rows, length, 2, head_count, head_dim)
        )
        cross_key = keyval[:, :, 0]
        cross_value = keyval[:, :, 1]
        stream_full = gather_cols(y_in)
        cross_query = (
            rows_product(stream_full, w_query)
            .astype(jnp.bfloat16)
            .reshape(stream_count, seq_rows, length, head_count, head_dim)
        )
        cross_mixed, cross_lse = attend(cross_query, cross_key, cross_value, segment, cross_offsets)
        cross_mix = cross_mixed.reshape(stream_count, row_tokens, col_width).astype(jnp.bfloat16)
        cross_full = gather_rows(cross_mix)
        cross_branch = cols_product(cross_full, w_cross_out)
        result, normed_three, inv_three = norm_forward(
            y_in.astype(jnp.float32) + cross_branch, cross_gain, cross_bias
        )
        outputs.append(result)
        grad_three, gain_part, bias_part = norm_back(
            cotangent[micro].astype(jnp.float32), normed_three, inv_three, cross_gain
        )
        norm_accs[4] = norm_accs[4] + gain_part
        norm_accs[5] = norm_accs[5] + bias_part
        branch_full = gather_cols(grad_three.astype(jnp.bfloat16))
        cross_out_acc = cross_out_acc + weight_grad(cross_full, branch_full)
        cross_mix_grad = (
            rows_product(branch_full, w_cross_out.T)
            .astype(jnp.bfloat16)
            .reshape(stream_count, seq_rows, length, head_count, head_dim)
        )
        query_grad, key_grad, value_grad, table_grad = attend_back(
            cross_query,
            cross_key,
            cross_value,
            segment,
            cross_offsets,
            onehot,
            cross_lse,
            cross_mix_grad,
        )
        cross_table_acc = cross_table_acc + table_grad
        query_low = query_grad.reshape(stream_count, row_tokens, col_width).astype(jnp.bfloat16)
        keyval_low = (
            jnp.stack(
                [
                    key_grad.reshape(row_tokens, col_width),
                    value_grad.reshape(row_tokens, col_width),
                ],
                axis=1,
            )
            .reshape(1, row_tokens, 2 * col_width)
            .astype(jnp.bfloat16)
        )
        query_full = gather_rows(query_low)
        query_acc = query_acc + weight_grad(stream_full, query_full)
        stream_grads.append(grad_three + cols_product(query_full, w_query.T))
        keyval_full = gather_rows(keyval_low)
        keyval_acc = keyval_acc + weight_grad(enc_full, keyval_full)
        encoded_grad = cols_product(keyval_full, keyval_matrix.T)
        grad_two, gain_part, bias_part = norm_back(encoded_grad, normed_two, inv_two, ffn_gain)
        norm_accs[2] = norm_accs[2] + gain_part
        norm_accs[3] = norm_accs[3] + bias_part
        feedforward_full_output = gather_cols(grad_two.astype(jnp.bfloat16))
        down_acc = down_acc + weight_grad(act_full, feedforward_full_output)
        act_grad = rows_product(feedforward_full_output, w_down.T)
        pre_low = gelu_pull(act_grad)[0].astype(jnp.bfloat16)
        pre_full = gather_rows(pre_low)
        up_acc = up_acc + weight_grad(hidden_full, pre_full)
        hidden_grad = grad_two + cols_product(pre_full, w_up.T)
        grad_one, gain_part, bias_part = norm_back(
            hidden_grad, normed_one, inv_one, attention_norm_gain
        )
        norm_accs[0] = norm_accs[0] + gain_part
        norm_accs[1] = norm_accs[1] + bias_part
        attn_full = gather_cols(grad_one.astype(jnp.bfloat16))
        out_acc = out_acc + weight_grad(mix_full, attn_full)
        enc_mix_grad = (
            rows_product(attn_full, w_out.T)
            .astype(jnp.bfloat16)
            .reshape(1, seq_rows, length, head_count, head_dim)
        )
        enc_qgrad, enc_kgrad, enc_vgrad, table_grad = attend_back(
            enc_query,
            enc_key,
            encoder_value_rows,
            segment,
            enc_offsets,
            onehot,
            enc_lse,
            enc_mix_grad,
        )
        enc_table_acc = enc_table_acc + table_grad
        qkv_low = (
            jnp.stack(
                [
                    enc_qgrad.reshape(row_tokens, col_width),
                    enc_kgrad.reshape(row_tokens, col_width),
                    enc_vgrad.reshape(row_tokens, col_width),
                ],
                axis=1,
            )
            .reshape(1, row_tokens, 3 * col_width)
            .astype(jnp.bfloat16)
        )
        qkv_full = gather_rows(qkv_low)
        qkv_acc = qkv_acc + weight_grad(x_full, qkv_full)
        token_grads.append((grad_one + cols_product(qkv_full, qkv_matrix.T))[0])
    norm_stack = jnp.stack(norm_accs)
    table_stack = jnp.stack([enc_table_acc, cross_table_acc])
    norm_sums = lax.psum(norm_stack, "col")
    table_sums = lax.psum(table_stack, "row")
    return (
        jnp.stack(outputs),
        jnp.stack(token_grads),
        jnp.stack(stream_grads),
        qkv_acc.reshape(row_width, 3, col_width),
        table_sums[0],
        out_acc,
        norm_sums[0],
        norm_sums[1],
        up_acc,
        down_acc,
        norm_sums[2],
        norm_sums[3],
        query_acc,
        keyval_acc.reshape(row_width, 2, col_width),
        table_sums[1],
        cross_out_acc,
        norm_sums[4],
        norm_sums[5],
    )


def solution(mesh):
    placed = (
        P(None, "col", "row"),
        P(None, None, "col", "row"),
        P(None, None, "col", "row"),
        P(None, "row", None),
        P(),
        P("row", None, "col"),
        P("col", None),
        P("col", "row"),
        P("row"),
        P("row"),
        P("row", "col"),
        P("col", "row"),
        P("row"),
        P("row"),
        P("row", "col"),
        P("row", None, "col"),
        P("col", None),
        P("col", "row"),
        P("row"),
        P("row"),
    )
    return jax.shard_map(
        on_device,
        mesh=mesh,
        in_specs=placed,
        out_specs=(
            P(None, None, "col", "row"),
            P(None, "col", "row"),
            P(None, None, "col", "row"),
            P("row", None, "col"),
            P("col", None),
            P("col", "row"),
            P("row"),
            P("row"),
            P("row", "col"),
            P("col", "row"),
            P("row"),
            P("row"),
            P("row", "col"),
            P("row", None, "col"),
            P("col", None),
            P("col", "row"),
            P("row"),
            P("row"),
        ),
        check_vma=False,
    )
```

profile of v0, /device:TPU:0, one launch (start us, length us, event | category | flops | bytes accessed | tf_op | source)
XLA Modules:
  0.0 4433.7 jit_solution(9951330898816761110)
XLA Ops:
  10.9 42.8 all-gather.29.cloned.1.call-done
  58.7 36.6 all-gather.39.cloned.1.call-done
  99.1 865.6 %gather_fusion = f32[262144,2]{1,0:T(8,128)} fusion(f32[2,1023]{0,1:T(8,128)S(1)} %copy.203, s32[262144]{0:T(1024)S(1)} %broadcast_clamp_fusion), kind=kCustom, calls=%fused_computation.clone | custom fusion | bytes 5242880 | tf_op jit(solution)/shard_map/jit(_take)/gather | solution.py:83
  964.7 70.1 %copy.205 = f32[512,512,2]{0,1,2:T(8,128)S(1)} copy(f32[512,512,2]{2,1,0:T(8,128)} %bitcast.12) | data formatting | bytes 4194304 | tf_op jit(solution)/shard_map/jit(_take)/gather | solution.py:83
  1064.5 51.2 %reduce-scatter.31.cloned.1.call-done = f32[1,256,256]{2,1,0:T(8,128)} async-done(((f32[1,2048,256]{2,1,0:T(8,128)}), f32[1,256,256]{2,1,0:T(8,128)}) %reduce-scatter.31.cloned.1.call-update) | async-done | bytes 262160 | tf_op jit(solution)/shard_map/reduce_scatter | solution.py:33
  1115.6 70.1 %reduce-scatter.45.cloned.1.call-done = f32[1,256,256]{2,1,0:T(8,128)} async-done(((f32[1,2048,256]{2,1,0:T(8,128)}), f32[1,256,256]{2,1,0:T(8,128)}) %reduce-scatter.45.cloned.1.call-update) | async-done | bytes 262160 | tf_op jit(solution)/shard_map/reduce_scatter | solution.py:33
  1200.4 38.7 all-gather.31.cloned.1.call-done
  1243.2 43.2 reduce-scatter.33.cloned.1.call-done
  1290.6 22.7 all-gather.33.cloned.1.call-done
  1317.1 68.0 %reduce-scatter.35.cloned.1.call-done = f32[1,256,256]{2,1,0:T(8,128)} async-done(((f32[1,2048,256]{2,1,0:T(8,128)}), f32[1,256,256]{2,1,0:T(8,128)}) %reduce-scatter.35.cloned.1.call-update) | async-done | bytes 262160 | tf_op jit(solution)/shard_map/reduce_scatter | solution.py:33
  1387.0 40.1 all-gather.41.cloned.1.call-done
  1431.1 43.4 reduce-scatter.47.cloned.1.call-done
  1478.7 22.7 all-gather.43.cloned.1.call-done
  1507.2 65.7 %reduce-scatter.49.cloned.1.call-done = f32[1,256,256]{2,1,0:T(8,128)} async-done(((f32[1,2048,256]{2,1,0:T(8,128)}), f32[1,256,256]{2,1,0:T(8,128)}) %reduce-scatter.49.cloned.1.call-update) | async-done | bytes 262160 | tf_op jit(solution)/shard_map/reduce_scatter | solution.py:33
  1589.0 46.0 %all-gather.77.cloned.1.call-done = bf16[1,3,2048,256]{3,2,1,0:T(8,128)(2,1)} async-done(((bf16[1,3,256,256]{3,2,1,0:T(8,128)(2,1)}), bf16[1,3,2048,256]{3,2,1,0:T(8,128)(2,1)}) %all-gather.77.cloned.1.call-update) | async-done | bytes 3145744 | tf_op jit(solution)/shard_map/all_gather | solution.py:15
  1639.8 36.6 all-gather.35.cloned.1.call-done
  1679.6 58.8 %all-gather.79.cloned.1.call-done = bf16[1,3,2048,256]{3,2,1,0:T(8,128)(2,1)} async-done(((bf16[1,3,256,256]{3,2,1,0:T(8,128)(2,1)}), bf16[1,3,2048,256]{3,2,1,0:T(8,128)(2,1)}) %all-gather.79.cloned.1.call-update) | async-done | bytes 3145744 | tf_op jit(solution)/shard_map/all_gather | solution.py:15
  1743.0 36.7 all-gather.45.cloned.1.call-done
  1783.9 865.6 %gather_fusion.1 = f32[262144,2]{1,0:T(8,128)} fusion(f32[2,1023]{0,1:T(8,128)S(1)} %copy.211, s32[262144]{0:T(1024)S(1)} %copy-done.23), kind=kCustom, calls=%fused_computation.1.clone | custom fusion | bytes 5242880 | tf_op jit(solution)/shard_map/jit(_take)/gather | solution.py:83
  2649.5 71.1 %copy.212 = f32[512,512,2]{0,1,2:T(8,128)} copy(f32[512,512,2]{2,1,0:T(8,128)} %bitcast.48) | data formatting | bytes 4194304 | tf_op jit(solution)/shard_map/jit(_take)/gather | solution.py:83
  2756.8 16.7 all-gather.47.cloned.1.call-done
  2778.7 116.8 %reduce-scatter.41.cloned.1.call-done = f32[3,256,256]{2,1,0:T(8,128)} async-done(((f32[3,2048,256]{2,1,0:T(8,128)}), f32[3,256,256]{2,1,0:T(8,128)}) %reduce-scatter.41.cloned.1.call-update) | async-done | bytes 786448 | tf_op jit(solution)/shard_map/reduce_scatter | solution.py:33
  2895.5 121.1 %reduce-scatter.55.cloned.1.call-done = f32[3,256,256]{2,1,0:T(8,128)} async-done(((f32[3,2048,256]{2,1,0:T(8,128)}), f32[3,256,256]{2,1,0:T(8,128)}) %reduce-scatter.55.cloned.1.call-update) | async-done | bytes 786448 | tf_op jit(solution)/shard_map/reduce_scatter | solution.py:33
  3046.1 59.0 %all-gather.49.cloned.1.call-done = bf16[3,2048,256]{2,1,0:T(8,128)(2,1)} async-done(((bf16[3,256,256]{2,1,0:T(8,128)(2,1)}), bf16[3,2048,256]{2,1,0:T(8,128)(2,1)}) %all-gather.49.cloned.1.call-update) | async-done | bytes 3145744 | tf_op jit(solution)/shard_map/all_gather | solution.py:15
  3109.7 57.4 %all-gather.61.cloned.1.call-done = bf16[3,2048,256]{2,1,0:T(8,128)(2,1)} async-done(((bf16[3,256,256]{2,1,0:T(8,128)(2,1)}), bf16[3,2048,256]{2,1,0:T(8,128)(2,1)}) %all-gather.61.cloned.1.call-update) | async-done | bytes 3145744 | tf_op jit(solution)/shard_map/all_gather | solution.py:15
  3171.7 34.6 reduce-scatter.57.cloned.1.call-done
  3218.6 28.1 reduce-scatter.69.cloned.1.call-done
  3277.4 15.6 all-gather.63.cloned.1.call-done
  3296.1 67.9 %reduce-scatter.59.cloned.1.call-done = f32[1,256,256]{2,1,0:T(8,128)} async-done(((f32[1,2048,256]{2,1,0:T(8,128)}), f32[1,256,256]{2,1,0:T(8,128)}) %reduce-scatter.59.cloned.1.call-update) | async-done | bytes 262160 | tf_op jit(solution)/shard_map/reduce_scatter | solution.py:33
  3364.0 70.4 %reduce-scatter.71.cloned.1.call-done = f32[1,256,256]{2,1,0:T(8,128)} async-done(((f32[1,2048,256]{2,1,0:T(8,128)}), f32[1,256,256]{2,1,0:T(8,128)}) %reduce-scatter.71.cloned.1.call-update) | async-done | bytes 262160 | tf_op jit(solution)/shard_map/reduce_scatter | solution.py:33
  3445.0 38.9 all-gather.53.cloned.1.call-done
  3488.0 37.4 all-gather.65.cloned.1.call-done
  3529.4 41.7 reduce-scatter.61.cloned.1.call-done
  3573.6 44.7 %reduce-scatter.73.cloned.1.call-done = f32[1,512,512]{2,1,0:T(8,128)} async-done(((f32[1,2048,512]{2,1,0:T(8,128)}), f32[1,512,512]{2,1,0:T(8,128)}) %reduce-scatter.73.cloned.1.call-update) | async-done | bytes 1048592 | tf_op jit(solution)/shard_map/reduce_scatter | solution.py:29
  3621.5 21.4 all-gather.55.cloned.1.call-done
  3646.6 21.0 all-gather.67.cloned.1.call-done
  3671.5 67.5 %reduce-scatter.63.cloned.1.call-done = f32[1,256,256]{2,1,0:T(8,128)} async-done(((f32[1,2048,256]{2,1,0:T(8,128)}), f32[1,256,256]{2,1,0:T(8,128)}) %reduce-scatter.63.cloned.1.call-update) | async-done | bytes 262160 | tf_op jit(solution)/shard_map/reduce_scatter | solution.py:33
  3739.0 70.4 %reduce-scatter.75.cloned.1.call-done = f32[1,256,256]{2,1,0:T(8,128)} async-done(((f32[1,2048,256]{2,1,0:T(8,128)}), f32[1,256,256]{2,1,0:T(8,128)}) %reduce-scatter.75.cloned.1.call-update) | async-done | bytes 262160 | tf_op jit(solution)/shard_map/reduce_scatter | solution.py:33
  3819.3 38.7 all-gather.69.cloned.1.call-done
  3860.7 38.9 all-gather.57.cloned.1.call-done
  3911.6 14.7 reduce-scatter.77.cloned.1.call-done
  3936.1 18.2 reduce-scatter.65.cloned.1.call-done
  3981.1 16.6 all-gather.73.cloned.1.call-done
  4002.9 16.5 all-gather.71.cloned.1.call-done
  4111.1 51.9 %reduce-scatter.83.cloned.1.call-done = f32[3,256,256]{2,1,0:T(8,128)} async-done(((f32[3,2048,256]{2,1,0:T(8,128)}), f32[3,256,256]{2,1,0:T(8,128)}) %reduce-scatter.83.cloned.1.call-update) | async-done | bytes 786448 | tf_op jit(solution)/shard_map/reduce_scatter | solution.py:33
  4163.1 121.2 %reduce-scatter.81.cloned.1.call-done = f32[3,256,256]{2,1,0:T(8,128)} async-done(((f32[3,2048,256]{2,1,0:T(8,128)}), f32[3,256,256]{2,1,0:T(8,128)}) %reduce-scatter.81.cloned.1.call-update) | async-done | bytes 786448 | tf_op jit(solution)/shard_map/reduce_scatter | solution.py:33
  4294.3 20.4 psum.207
  4397.2 27.6 reduce-scatter.67.cloned.1.call-done
  (653 shorter events, 525.7 us)
Async XLA Ops:
  9.0 86.3 %all-gather.39.cloned.1.call-start = ((), (), s32[]{:S(2)}) async-start(), calls=%async_computation.40 | async-start | bytes 1179648 | tf_op jit(solution)/shard_map/all_gather | solution.py:15
  9.7 1025.3 %reduce-scatter.29.cloned.1.call-start = ((), (), s32[]{:S(2)}) async-start(), calls=%async_computation.29 | async-start | bytes 3932160 | tf_op jit(solution)/shard_map/reduce_scatter | solution.py:29
  57.3 992.5 %reduce-scatter.43.cloned.1.call-start = ((), (), s32[]{:S(2)}) async-start(), calls=%async_computation.41 | async-start | bytes 3932160 | tf_op jit(solution)/shard_map/reduce_scatter | solution.py:29
  98.9 1016.8 %reduce-scatter.31.cloned.1.call-start = ((), (), s32[]{:S(2)}) async-start(), calls=%async_computation.30 | async-start | bytes 2359296 | tf_op jit(solution)/shard_map/reduce_scatter | solution.py:33
  1049.5 136.2 %reduce-scatter.45.cloned.1.call-start = ((), (), s32[]{:S(2)}) async-start(), calls=%async_computation.42 | async-start | bytes 2359296 | tf_op jit(solution)/shard_map/reduce_scatter | solution.py:33
  1064.4 174.6 %all-gather.31.cloned.1.call-start = ((), (), s32[]{:S(2)}) async-start(), calls=%async_computation.31 | async-start | bytes 1179648 | tf_op jit(solution)/shard_map/all_gather | solution.py:15
  1200.3 86.1 %reduce-scatter.33.cloned.1.call-start = ((), (), s32[]{:S(2)}) async-start(), calls=%async_computation.32 | async-start | bytes 5242880 | tf_op jit(solution)/shard_map/reduce_scatter | solution.py:29
  1290.6 94.4 %reduce-scatter.35.cloned.1.call-start = ((), (), s32[]{:S(2)}) async-start(), calls=%async_computation.34 | async-start | bytes 2359296 | tf_op jit(solution)/shard_map/reduce_scatter | solution.py:33
  1317.0 110.1 %all-gather.41.cloned.1.call-start = ((), (), s32[]{:S(2)}) async-start(), calls=%async_computation.43 | async-start | bytes 1179648 | tf_op jit(solution)/shard_map/all_gather | solution.py:15
  1387.0 87.5 %reduce-scatter.47.cloned.1.call-start = ((), (), s32[]{:S(2)}) async-start(), calls=%async_computation.44 | async-start | bytes 5242880 | tf_op jit(solution)/shard_map/reduce_scatter | solution.py:29
  1478.7 94.3 %reduce-scatter.49.cloned.1.call-start = ((), (), s32[]{:S(2)}) async-start(), calls=%async_computation.46 | async-start | bytes 2359296 | tf_op jit(solution)/shard_map/reduce_scatter | solution.py:33
  1505.1 129.9 %all-gather.77.cloned.1.call-start = ((), (), s32[]{:S(2)}) async-start(), calls=%async_computation.80 | async-start | bytes 3538944 | tf_op jit(solution)/shard_map/all_gather | solution.py:15
  1507.1 169.3 %all-gather.35.cloned.1.call-start = ((), (), s32[]{:S(2)}) async-start(), calls=%async_computation.35 | async-start | bytes 1179648 | tf_op jit(solution)/shard_map/all_gather | solution.py:15
  1587.8 150.5 %all-gather.79.cloned.1.call-start = ((), (), s32[]{:S(2)}) async-start(), calls=%async_computation.81 | async-start | bytes 3538944 | tf_op jit(solution)/shard_map/all_gather | solution.py:15
  1588.4 191.3 %all-gather.45.cloned.1.call-start = ((), (), s32[]{:S(2)}) async-start(), calls=%async_computation.47 | async-start | bytes 1179648 | tf_op jit(solution)/shard_map/all_gather | solution.py:15
  1589.0 1133.6 %reduce-scatter.39.cloned.1.call-start = ((), (), s32[]{:S(2)}) async-start(), calls=%async_computation.37 | async-start | bytes 3932160 | tf_op jit(solution)/shard_map/reduce_scatter | solution.py:29
  1639.8 1085.0 %reduce-scatter.37.cloned.1.call-start = ((), (), s32[]{:S(2)}) async-start(), calls=%async_computation.36 | async-start | bytes 2621440 | tf_op jit(solution)/shard_map/reduce_scatter | solution.py:29
  1679.5 1053.8 %reduce-scatter.53.cloned.1.call-start = ((), (), s32[]{:S(2)}) async-start(), calls=%async_computation.49 | async-start | bytes 3932160 | tf_op jit(solution)/shard_map/reduce_scatter | solution.py:29
  1742.9 992.5 %reduce-scatter.51.cloned.1.call-start = ((), (), s32[]{:S(2)}) async-start(), calls=%async_computation.48 | async-start | bytes 2621440 | tf_op jit(solution)/shard_map/reduce_scatter | solution.py:29
  1782.7 969.1 %all-gather.37.cloned.1.call-start = ((), (), s32[]{:S(2)}) async-start(), calls=%async_computation.38 | async-start | bytes 1966080 | tf_op jit(solution)/shard_map/all_gather | solution.py:19
  2744.0 151.5 %reduce-scatter.41.cloned.1.call-start = ((), (), s32[]{:S(2)}) async-start(), calls=%async_computation.39 | async-start | bytes 7077888 | tf_op jit(solution)/shard_map/reduce_scatter | solution.py:33
  2756.8 259.8 %reduce-scatter.55.cloned.1.call-start = ((), (), s32[]{:S(2)}) async-start(), calls=%async_computation.51 | async-start | bytes 7077888 | tf_op jit(solution)/shard_map/reduce_scatter | solution.py:33
  2778.6 326.5 %all-gather.49.cloned.1.call-start = ((), (), s32[]{:S(2)}) async-start(), calls=%async_computation.52 | async-start | bytes 3538944 | tf_op jit(solution)/shard_map/all_gather | solution.py:15
  3045.3 121.7 %all-gather.61.cloned.1.call-start = ((), (), s32[]{:S(2)}) async-start(), calls=%async_computation.64 | async-start | bytes 3538944 | tf_op jit(solution)/shard_map/all_gather | solution.py:15
  3046.1 160.1 %reduce-scatter.57.cloned.1.call-start = ((), (), s32[]{:S(2)}) async-start(), calls=%async_computation.53 | async-start | bytes 3932160 | tf_op jit(solution)/shard_map/reduce_scatter | solution.py:29
  3109.7 137.1 %reduce-scatter.69.cloned.1.call-start = ((), (), s32[]{:S(2)}) async-start(), calls=%async_computation.65 | async-start | bytes 3932160 | tf_op jit(solution)/shard_map/reduce_scatter | solution.py:29
  3171.6 102.5 %all-gather.51.cloned.1.call-start = ((), (), s32[]{:S(2)}) async-start(), calls=%async_computation.54 | async-start | bytes 1310720 | tf_op jit(solution)/shard_map/all_gather | solution.py:19
  3268.7 95.3 %reduce-scatter.59.cloned.1.call-start = ((), (), s32[]{:S(2)}) async-start(), calls=%async_computation.55 | async-start | bytes 2359296 | tf_op jit(solution)/shard_map/reduce_scatter | solution.py:33
  3277.3 157.1 %reduce-scatter.71.cloned.1.call-start = ((), (), s32[]{:S(2)}) async-start(), calls=%async_computation.67 | async-start | bytes 2359296 | tf_op jit(solution)/shard_map/reduce_scatter | solution.py:33
  3296.0 187.9 %all-gather.53.cloned.1.call-start = ((), (), s32[]{:S(2)}) async-start(), calls=%async_computation.56 | async-start | bytes 1179648 | tf_op jit(solution)/shard_map/all_gather | solution.py:15
  3444.4 81.0 %all-gather.65.cloned.1.call-start = ((), (), s32[]{:S(2)}) async-start(), calls=%async_computation.68 | async-start | bytes 1179648 | tf_op jit(solution)/shard_map/all_gather | solution.py:15
  3444.9 126.1 %reduce-scatter.61.cloned.1.call-start = ((), (), s32[]{:S(2)}) async-start(), calls=%async_computation.57 | async-start | bytes 5242880 | tf_op jit(solution)/shard_map/reduce_scatter | solution.py:29
  3487.9 130.4 %reduce-scatter.73.cloned.1.call-start = ((), (), s32[]{:S(2)}) async-start(), calls=%async_computation.69 | async-start | bytes 5242880 | tf_op jit(solution)/shard_map/reduce_scatter | solution.py:29
  3529.4 113.5 %all-gather.55.cloned.1.call-start = ((), (), s32[]{:S(2)}) async-start(), calls=%async_computation.58 | async-start | bytes 2621440 | tf_op jit(solution)/shard_map/all_gather | solution.py:19
  3573.6 94.1 %all-gather.67.cloned.1.call-start = ((), (), s32[]{:S(2)}) async-start(), calls=%async_computation.70 | async-start | bytes 2621440 | tf_op jit(solution)/shard_map/all_gather | solution.py:19
  3621.4 117.6 %reduce-scatter.63.cloned.1.call-start = ((), (), s32[]{:S(2)}) async-start(), calls=%async_computation.59 | async-start | bytes 2359296 | tf_op jit(solution)/shard_map/reduce_scatter | solution.py:33
  3646.6 162.9 %reduce-scatter.75.cloned.1.call-start = ((), (), s32[]{:S(2)}) async-start(), calls=%async_computation.71 | async-start | bytes 2359296 | tf_op jit(solution)/shard_map/reduce_scatter | solution.py:33
  3671.4 186.6 %all-gather.69.cloned.1.call-start = ((), (), s32[]{:S(2)}) async-start(), calls=%async_computation.72 | async-start | bytes 1179648 | tf_op jit(solution)/shard_map/all_gather | solution.py:15
  3818.5 81.2 %all-gather.57.cloned.1.call-start = ((), (), s32[]{:S(2)}) async-start(), calls=%async_computation.60 | async-start | bytes 1179648 | tf_op jit(solution)/shard_map/all_gather | solution.py:15
  3819.2 107.0 %reduce-scatter.77.cloned.1.call-start = ((), (), s32[]{:S(2)}) async-start(), calls=%async_computation.73 | async-start | bytes 1310720 | tf_op jit(solution)/shard_map/reduce_scatter | solution.py:29
  3860.7 93.7 %reduce-scatter.65.cloned.1.call-start = ((), (), s32[]{:S(2)}) async-start(), calls=%async_computation.61 | async-start | bytes 1310720 | tf_op jit(solution)/shard_map/reduce_scatter | solution.py:29
  3905.9 91.8 %all-gather.73.cloned.1.call-start = ((), (), s32[]{:S(2)}) async-start(), calls=%async_computation.76 | async-start | bytes 1966080 | tf_op jit(solution)/shard_map/all_gather | solution.py:19
  3911.5 107.9 %all-gather.71.cloned.1.call-start = ((), (), s32[]{:S(2)}) async-start(), calls=%async_computation.74 | async-start | bytes 1966080 | tf_op jit(solution)/shard_map/all_gather | solution.py:19
  3935.9 166.0 %all-gather.59.cloned.1.call-start = ((), (), s32[]{:S(2)}) async-start(), calls=%async_computation.62 | async-start | bytes 1966080 | tf_op jit(solution)/shard_map/all_gather | solution.py:19
  3963.2 199.9 %reduce-scatter.83.cloned.1.call-start = ((), (), s32[]{:S(2)}) async-start(), calls=%async_computation.79 | async-start | bytes 7077888 | tf_op jit(solution)/shard_map/reduce_scatter | solution.py:33
  3981.1 303.2 %reduce-scatter.81.cloned.1.call-start = ((), (), s32[]{:S(2)}) async-start(), calls=%async_computation.77 | async-start | bytes 7077888 | tf_op jit(solution)/shard_map/reduce_scatter | solution.py:33
  4002.8 393.4 %reduce-scatter.79.cloned.1.call-start = ((), (), s32[]{:S(2)}) async-start(), calls=%async_computation.75 | async-start | bytes 2359296 | tf_op jit(solution)/shard_map/reduce_scatter | solution.py:33
  4023.0 401.9 %reduce-scatter.67.cloned.1.call-start = ((), (), s32[]{:S(2)}) async-start(), calls=%async_computation.63 | async-start | bytes 2359296 | tf_op jit(solution)/shard_map/reduce_scatter | solution.py:33
  (155 other events, 12369.6 us)
Sparse Core Ops, SparseCore 0:
  10.7 42.8 all-gather.28
  56.3 38.8 all-gather.38
  97.8 36.7 reduce-scatter.28
  137.1 37.9 reduce-scatter.42
  1049.6 65.9 reduce-scatter.30
  1119.0 66.6 reduce-scatter.44
  1200.4 38.5 all-gather.30
  1243.1 43.2 reduce-scatter.32
  1290.7 22.5 all-gather.32
  1317.1 67.8 reduce-scatter.34
  1388.0 39.1 all-gather.40
  1431.2 43.2 reduce-scatter.46
  1478.8 22.5 all-gather.42
  1505.2 67.6 reduce-scatter.48
  1575.5 59.4 all-gather.76
  1637.6 38.7 all-gather.34
  1679.0 59.2 all-gather.78
  1740.9 38.7 all-gather.44
  1782.2 36.7 reduce-scatter.38
  1821.5 31.3 reduce-scatter.36
  1855.5 37.9 reduce-scatter.52
  1896.1 31.3 reduce-scatter.50
  2753.8 19.6 all-gather.46
  2777.1 118.3 reduce-scatter.40
  2899.0 117.5 reduce-scatter.54
  3045.5 59.6 all-gather.48
  3107.9 59.1 all-gather.60
  3169.6 36.5 reduce-scatter.56
  3208.8 37.9 reduce-scatter.68
  3296.4 67.5 reduce-scatter.58
  3367.5 66.8 reduce-scatter.70
  3444.5 39.3 all-gather.52
  3486.4 38.8 all-gather.64
  3527.8 43.2 reduce-scatter.60
  3573.8 44.4 reduce-scatter.72
  3620.3 22.5 all-gather.54
  3645.0 22.5 all-gather.66
  3671.2 67.7 reduce-scatter.62
  3742.6 66.8 reduce-scatter.74
  3818.6 39.3 all-gather.68
  3860.7 38.8 all-gather.56
  3902.6 23.6 reduce-scatter.76
  3929.4 24.9 reduce-scatter.64
  3999.7 19.6 all-gather.70
  4044.7 118.3 reduce-scatter.82
  4166.7 117.5 reduce-scatter.80
  4287.6 66.8 reduce-scatter.78
  4358.1 66.6 reduce-scatter.66
  (6 shorter events, 110.5 us)
where the time goes:
time: 4450 us; the launch traced here: 4430 us
  local copies, waits for them, and re-layouts  2030 us (46%)
  waiting for transfers between devices  2030 us (46%)
  matrix products  166 us (4%)
  blocking collectives  99.6 us (2%)
  other arithmetic  89.6 us (2%)
    gather x4, local copies, waits for them, and re-layouts, block_logits(): pos_bias = jnp.take(offsets, offset_index, axis=1)  1870 us
    reduce_scatter x14, waiting for transfers between devices, cols_product(): lax.psum_scatter(product(operand_full, matrix), 'col', scatter_dimension=...  970 us
    all_gather x14, waiting for transfers between devices, gather_cols(): return lax.all_gather(local_rows, 'col', axis=1, tiled=True)  607 us
    reduce_scatter x14, waiting for transfers between devices, rows_product(): lax.psum_scatter(product(operand_full, matrix), 'row', scatter_dimension=...  269 us
    all_gather x12, waiting for transfers between devices, gather_rows(): return lax.all_gather(local_rows, 'row', axis=1, tiled=True)  179 us
    dot_general x28, matrix products, product(): jnp.einsum('ray,yw->raw', matmul_operand, weight_matrix, preferred_elemen...  104 us
  transfers between devices with their start and end apart: 54, of which 46 were waited for; matrix products, arithmetic and copies ran while one was open for 50% of the time, Pallas kernels for 0%

commit v1 on v0

--- a/solution.py
+++ b/solution.py
@@ -1,9 +1,14 @@
+import functools
 import jax
 import jax.numpy as jnp
 from jax import lax
+from jax.experimental import pallas as pl
+from jax.experimental.pallas import tpu as pltpu
 from jax.sharding import PartitionSpec as P
 
 D = 1024
+F32 = jnp.float32
+BF = jnp.bfloat16
 
 
 epsilon = 1e-05
@@ -143,7 +148,7 @@
     return (query_parts, key_grad, value_grad, table_grad)
 
 
-def on_device(
+def on_device_general(
     tokens,
     streams,
     cotangent,
@@ -359,52 +364,384 @@
     )
 
 
+def mm(a,b):
+    return jnp.dot(a,b,preferred_element_type=F32)
+def mm_nt(a,b):
+    return lax.dot_general(a,b,(((1,),(1,)),((),())),preferred_element_type=F32)
+
+def fwd_kernel(streams, length, width, off_ref, segq_ref, segk_ref, q_ref, k_ref, v_ref, mix_ref, lse_ref, t_ref):
+    chunks = 2*length//width - 1
+    top = length - width
+    for c in range(chunks):
+        lo = (chunks-1-c)*width
+        w = off_ref[0, :, lo:lo+2*width]
+        rolled = pltpu.roll(jnp.broadcast_to(w,(width,2*width)), 0, 1, stride=1, stride_axis=0)
+        t_ref[0, c*width:(c+1)*width, :] = rolled[:, width:]
+    keys = k_ref[0].T
+    values = v_ref[0]
+    scale = k_ref.shape[1]**-0.5
+    panels = length//width
+    for p in range(panels):
+        bias = t_ref[0, top-p*width:top-p*width+length, :]
+        shown = segk_ref[...] <= segq_ref[:, p*width:(p+1)*width]
+        for s in range(streams):
+            lo = s*length+p*width
+            logits = mm(keys, q_ref[0, :, lo:lo+width])*scale + bias
+            logits = jnp.where(shown, logits, neg_fill)
+            m = jnp.max(logits, axis=0, keepdims=True)
+            e = jnp.exp(logits-m)
+            total = jnp.sum(e, axis=0, keepdims=True)
+            lse_ref[0, :, lo:lo+width] = m + jnp.log(total)
+            prob = (e*(1.0/total)).astype(BF)
+            mix_ref[0, :, lo:lo+width] = mm(values, prob).astype(BF)
+
+def bwd_kernel(streams, length, width, t_ref, segq_ref, segk_ref, q_ref, k_ref, v_ref, lse_ref, dmix_ref, dq_ref, dk_ref, dv_ref, doff_ref, g_scr, dk_scr, dv_scr):
+    chunks = 2*length//width - 1
+    top = length - width
+    keysT = k_ref[0]
+    keys = keysT.T
+    values = v_ref[0].T
+    scale = k_ref.shape[1]**-0.5
+    panels = length//width
+    g_scr[...] = jnp.zeros_like(g_scr)
+    dk_scr[...] = jnp.zeros_like(dk_scr)
+    dv_scr[...] = jnp.zeros_like(dv_scr)
+    for p in range(panels):
+        rows = slice(top-p*width, top-p*width+length)
+        shown = segk_ref[...] <= segq_ref[:, p*width:(p+1)*width]
+        for s in range(streams):
+            lo = s*length+p*width
+            qs = q_ref[0, :, lo:lo+width]
+            dm = dmix_ref[0, :, lo:lo+width]
+            logits = mm(keys, qs)*scale + t_ref[0, rows, :]
+            prob = jnp.where(shown, jnp.exp(logits - lse_ref[0, :, lo:lo+width]), 0.0)
+            dprob = mm(values, dm)
+            delta = jnp.sum(prob*dprob, axis=0, keepdims=True)
+            dlog = prob*(dprob-delta)
+            g_scr[rows, :] += dlog
+            g = (dlog*scale).astype(BF)
+            dq_ref[0, :, lo:lo+width] = mm(keysT, g).astype(BF)
+            dk_scr[...] += mm_nt(qs, g)
+            dv_scr[...] += mm_nt(dm, prob.astype(BF))
+    dk_ref[0] = dk_scr[...].astype(BF)
+    dv_ref[0] = dv_scr[...].astype(BF)
+    doff_ref[...] = jnp.zeros_like(doff_ref)
+    sub = lax.broadcasted_iota(jnp.int32, (8, 2*width), 0)
+    for c in range(chunks):
+        acc = jnp.zeros((8, 2*width), F32)
+        for i in range(width//8):
+            piece = g_scr[c*width+8*i:c*width+8*i+8, :]
+            padded = jnp.concatenate([jnp.zeros((8,width),F32), piece], axis=1)
+            if i: padded = pltpu.roll(padded, 2*width-8*i, 1)
+            acc = acc + padded
+        for b in (1,2,4):
+            acc = jnp.where((sub//b)%2==1, pltpu.roll(acc, 2*width-b, 1), acc)
+        lo = (chunks-1-c)*width
+        doff_ref[0, :, lo:lo+2*width] += jnp.sum(acc, axis=0, keepdims=True)
+
+def attention(off_rev, segq, segk, q, k, v, parts, streams):
+    heads, length = k.shape[0], k.shape[2]
+    hd = 64; width=128
+    blk = lambda part,n: pl.BlockSpec((1,hd,n), lambda h: (h,part,0))
+    return pl.pallas_call(
+        functools.partial(fwd_kernel, streams, length, width),
+        grid=(heads,),
+        in_specs=[pl.BlockSpec((1,1,2*length),lambda h:(h,0,0)), pl.BlockSpec((1,length),lambda h:(0,0)), pl.BlockSpec((length,width),lambda h:(0,0)),
+                  blk(parts[0],streams*length), blk(parts[1],length), blk(parts[2],length)],
+        out_specs=[blk(0,streams*length), pl.BlockSpec((1,1,streams*length),lambda h:(h,0,0)), pl.BlockSpec((1,2*length-width,width),lambda h:(h,0,0))],
+        out_shape=[jax.ShapeDtypeStruct((heads,hd,streams*length),BF), jax.ShapeDtypeStruct((heads,1,streams*length),F32), jax.ShapeDtypeStruct((heads,2*length-width,width),F32)],
+        compiler_params=pltpu.CompilerParams(vmem_limit_bytes=48<<20),
+        name="attend",
+    )(off_rev, segq, segk, q, k, v)
+
+def attention_back(tiles, segq, segk, q, k, v, parts, lse, dmix, streams):
+    heads, length = k.shape[0], k.shape[2]
+    hd = 64; width=128
+    blk = lambda part,n: pl.BlockSpec((1,hd,n), lambda h: (h,part,0))
+    return pl.pallas_call(
+        functools.partial(bwd_kernel, streams, length, width),
+        grid=(heads,),
+        in_specs=[pl.BlockSpec((1,2*length-width,width),lambda h:(h,0,0)), pl.BlockSpec((1,length),lambda h:(0,0)), pl.BlockSpec((length,width),lambda h:(0,0)),
+                  blk(parts[0],streams*length), blk(parts[1],length), blk(parts[2],length),
+                  pl.BlockSpec((1,1,streams*length),lambda h:(h,0,0)), blk(0,streams*length)],
+        out_specs=[blk(0,streams*length), blk(0,length), blk(0,length), pl.BlockSpec((1,1,2*length),lambda h:(h,0,0))],
+        out_shape=[jax.ShapeDtypeStruct((heads,hd,streams*length),BF), jax.ShapeDtypeStruct((heads,hd,length),BF), jax.ShapeDtypeStruct((heads,hd,length),BF), jax.ShapeDtypeStruct((heads,1,2*length),F32)],
+        scratch_shapes=[pltpu.VMEM((2*length-width,width),F32), pltpu.VMEM((hd,length),F32), pltpu.VMEM((hd,length),F32)],
+        compiler_params=pltpu.CompilerParams(vmem_limit_bytes=48<<20),
+        name="attend_back",
+    )(tiles, segq, segk, q, k, v, lse, dmix)
+
+
+def send(value, pairs):
+    return lax.ppermute(value, ("row", "col"), pairs)
+
+
+def device_pairs(rows, cols):
+    seqs = cols // 2
+    place = lambda y, k, s, h: (2 * (y % (rows // 2)) + k % 2) * cols + 2 * (s % seqs) + h % 2
+    spots = [(y, k, s, h) for y in range(rows // 2) for k in range(2) for s in range(seqs) for h in range(2)]
+    move = lambda dy, dk, ds, dh: [(place(y, k, s, h), place(y + dy, k + dk, s + ds, h + dh)) for y, k, s, h in spots]
+    return {
+        "core": move(0, 1, 0, 0),
+        "half": move(0, 0, 0, 1),
+        "micro": move(1, 0, 0, 0),
+        "seq": [move(0, 0, d, 0) for d in range(seqs)],
+    }
+
+
+def pick(array, index, axis):
+    return lax.dynamic_index_in_dim(array, index, axis, keepdims=False)
+
+
+def in_order(first, mine, other, axis, join=jnp.concatenate):
+    return jnp.where(first, join([mine, other], axis=axis), join([other, mine], axis=axis))
+
+
+def layer_norm(residual, gain_vec, bias_vec):
+    centered = residual - jnp.mean(residual, axis=-1, keepdims=True)
+    inv_std = lax.rsqrt(jnp.mean(centered * centered, axis=-1, keepdims=True) + epsilon)
+    normed = centered * inv_std
+    return (normed * gain_vec + bias_vec, normed, inv_std)
+
+
+def layer_norm_back(out_grad, normed, inv_std, gain_vec):
+    scaled = out_grad * gain_vec
+    first = jnp.mean(scaled, axis=-1, keepdims=True)
+    second = jnp.mean(scaled * normed, axis=-1, keepdims=True)
+    lead = tuple(range(out_grad.ndim - 1))
+    return (
+        inv_std * (scaled - first - normed * second),
+        jnp.sum(out_grad * normed, axis=lead),
+        jnp.sum(out_grad, axis=lead),
+    )
+
+
+def dot_f32(spec, left, right):
+    return jnp.einsum(spec, left, right, preferred_element_type=F32)
+
+
+def on_device(
+    rows,
+    cols,
+    tokens,
+    streams,
+    cotangent,
+    block_ids,
+    bucket_ids,
+    w_qkv,
+    enc_table,
+    w_out,
+    attention_norm_gain,
+    attn_bias,
+    w_up,
+    w_down,
+    ffn_gain,
+    ffn_bias,
+    w_query,
+    w_keyval,
+    cross_table,
+    w_cross_out,
+    cross_gain,
+    cross_bias,
+):
+    pairs = device_pairs(rows, cols)
+    seqs = cols // 2
+    row, col = lax.axis_index("row"), lax.axis_index("col")
+    y, k, seq, half = row // 2, row % 2, col // 2, col % 2
+    low_core, low_half, low_y = k == 0, half == 0, y == 0
+    stream_count = streams.shape[1]
+    tok = tokens.shape[1]
+    own = tok // 2
+    feat = tokens.shape[2]
+    length = block_ids.shape[2]
+    head_dim = w_qkv.shape[2] // 2
+    ff = w_up.shape[1] // 2
+    table_heads, bucket_count = enc_table.shape
+
+    norm_params = jnp.stack([attention_norm_gain, attn_bias, ffn_gain, ffn_bias, cross_gain, cross_bias])
+    norm_params = lax.all_gather(norm_params, "row", axis=1, tiled=True)
+    norm_params = jnp.where(low_y, norm_params, jnp.roll(norm_params, D // 2, axis=1))
+    gain1, bias1, gain2, bias2, gain3, bias3 = norm_params
+    segment = pick(pick(lax.all_gather(block_ids, "row", axis=1, tiled=True), y, 0), seq, 0)
+    segq = segment[None]
+    segk = jnp.broadcast_to(segment[:, None], (length, 128))
+    tables = lax.all_gather(jnp.stack([enc_table, cross_table]), "col", axis=0)
+    slot_col = 2 * ((seq - jnp.arange(seqs)) % seqs) + half
+    own_tables = pick(jnp.take(tables, slot_col, axis=0), k, 2)
+    reversed_ids = jnp.concatenate([jnp.full((1,), -1, jnp.int32), bucket_ids[::-1]])
+    onehot = bucket_onehot(reversed_ids, bucket_count)
+    offsets = jnp.einsum("htb,bo->tho", own_tables, onehot, precision=highest)[:, :, None, :]
+
+    def relayout(array):
+        count = array.shape[1]
+        both = jnp.concatenate([pick(array, y, 0), send(pick(array, 1 - y, 0), pairs["micro"])], axis=-1)
+        blocks = both.reshape(count, 2, own, 2, 1, feat)
+        other = send(pick(blocks, 1 - k, 1), pairs["core"])
+        return in_order(low_core, pick(blocks, k, 1), other, 3).reshape(count, own, D)
+
+    def relayout_back(array, link_type):
+        count = array.shape[0]
+        blocks = array.reshape(count, own, 2, 2, feat)
+        other = send(pick(blocks, 1 - k, 3), pairs["core"])
+        both = in_order(low_core, pick(blocks, k, 3), other, 1).reshape(count, tok, 2, feat)
+        other = send(both[:, :, 1].astype(link_type), pairs["micro"]).astype(F32)
+        return in_order(low_y, both[:, :, 0], other, 0, jnp.stack)
+
+    def gather_tokens(array):
+        count = array.shape[0]
+        pair = in_order(low_half, array, send(array, pairs["half"]), 1, jnp.stack)
+        return in_order(low_core, pair, send(pair, pairs["core"]), 2, jnp.stack).reshape(count, 2 * tok, D)
+
+    def scatter_tokens(partial):
+        count = partial.shape[0]
+        blocks = partial.reshape(count, 2, 2, own, D)
+        other = send(pick(blocks, 1 - k, 2).astype(BF), pairs["core"])
+        blocks = pick(blocks, k, 2) + other.astype(F32)
+        other = send(pick(blocks, 1 - half, 1).astype(BF), pairs["half"])
+        return pick(blocks, half, 1) + other.astype(F32)
+
+    def gather_weights(shards):
+        base = in_order(low_core, pick(shards, k, 0), send(pick(shards, 1 - k, 0), pairs["core"]), 1)
+        slots = jnp.stack([base] + [send(base, pairs["seq"][d]) for d in range(1, seqs)])
+        return jnp.concatenate([slots, send(slots, pairs["micro"])], axis=2)
+
+    def scatter_weights(grad):
+        part = grad[:, :, : D // 2] + send(grad[:, :, D // 2 :].astype(BF), pairs["micro"]).astype(F32)
+        low = part.astype(BF)
+        total = part[0]
+        for d in range(1, seqs):
+            total = total + send(low[d], pairs["seq"][seqs - d]).astype(F32)
+        blocks = total.reshape(-1, 2, feat)
+        other = send(pick(blocks, 1 - k, 1), pairs["core"])
+        return in_order(low_core, pick(blocks, k, 1), other, 0, jnp.stack)
+
+    def columns(weight, parts):
+        return weight.reshape(feat, parts, 2, -1).transpose(2, 1, 3, 0).reshape(2, -1, feat)
+
+    def columns_back(array, parts):
+        return array.reshape(2, parts, -1, feat).transpose(3, 1, 0, 2).reshape(feat, parts, -1)
+
+    halves = lambda weight: weight.reshape(2, -1, feat)
+    hd3, hd2 = 3 * head_dim, 2 * head_dim
+    first = gather_weights(jnp.concatenate([columns(w_qkv, 3), halves(w_out)], axis=1))
+    x_own = relayout(tokens[:, None])
+    x_full = gather_tokens(x_own)[0]
+    up = gather_weights(columns(w_up, 1))
+    down = gather_weights(halves(w_down))
+    last = gather_weights(jnp.concatenate([columns(w_keyval, 2), columns(w_query, 1), halves(w_cross_out)], axis=1))
+    y_own = relayout(streams)
+    y_full = gather_tokens(y_own).reshape(stream_count * length, D)
+    c_own = relayout(cotangent)
+    m_qkv, m_out = first[:, :hd3], first[:, hd3:].reshape(-1, D)
+    m_kv, m_q, m_co = last[:, :hd2], last[:, hd2:hd3], last[:, hd3:].reshape(-1, D)
+    up, down = up.reshape(-1, D), down.reshape(-1, D)
+
+    qkv = dot_f32("snr,tr->snt", m_qkv, x_full).astype(BF)
+    mix, lse, tiles = attention(offsets[0], segq, segk, qkv, qkv, qkv, (0, 1, 2), 1)
+    mix_flat = mix.reshape(-1, length)
+    branch = scatter_tokens(dot_f32("et,er->tr", mix_flat, m_out)[None])[0]
+    hidden, normed1, inv1 = layer_norm(x_own[0].astype(F32) + branch, gain1, bias1)
+    hidden_full = gather_tokens(hidden.astype(BF)[None])[0]
+    pre = dot_f32("fr,tr->ft", up, hidden_full)
+    act, gelu_pull = jax.vjp(gelu_exact, pre)
+    act = act.astype(BF)
+    branch = scatter_tokens(dot_f32("ft,fr->tr", act, down)[None])[0]
+    encoded, normed2, inv2 = layer_norm(hidden + branch, gain2, bias2)
+    enc_full = gather_tokens(encoded.astype(BF)[None])[0]
+    kv = dot_f32("snr,tr->snt", m_kv, enc_full).astype(BF)
+    query = dot_f32("snr,tr->snt", m_q, y_full).astype(BF)
+    cmix, clse, ctiles = attention(offsets[1], segq, segk, query, kv, kv, (0, 0, 1), stream_count)
+    cmix_flat = cmix.reshape(-1, stream_count * length)
+    branch = scatter_tokens(dot_f32("et,er->tr", cmix_flat, m_co).reshape(stream_count, length, D))
+    result, normed3, inv3 = layer_norm(y_own.astype(F32) + branch, gain3, bias3)
+    output = relayout_back(result, BF)
+
+    d3, gain3_grad, bias3_grad = layer_norm_back(c_own.astype(F32), normed3, inv3, gain3)
+    d3_full = gather_tokens(d3.astype(BF)).reshape(stream_count * length, D)
+    dcmix = dot_f32("er,tr->et", m_co, d3_full).astype(BF).reshape(cmix.shape)
+    g_co = dot_f32("et,tr->er", cmix_flat, d3_full)
+    dquery, dkc, dvc, doff_cross = attention_back(
+        ctiles, segq, segk, query, kv, kv, (0, 0, 1), clse, dcmix, stream_count
+    )
+    dkv = jnp.concatenate([dkc, dvc], axis=1)
+    d_enc = scatter_tokens(dot_f32("snt,snr->tr", dkv, m_kv)[None])[0]
+    d2, gain2_grad, bias2_grad = layer_norm_back(d_enc, normed2, inv2, gain2)
+    d2_full = gather_tokens(d2.astype(BF)[None])[0]
+    g_q = dot_f32("snt,tr->snr", dquery, y_full)
+    g_kv = dot_f32("snt,tr->snr", dkv, enc_full)
+    g_last = scatter_weights(
+        jnp.concatenate([g_kv, g_q, g_co.reshape(seqs, head_dim, D)], axis=1)
+    )
+    dy = scatter_tokens(dot_f32("snt,snr->tr", dquery, m_q).reshape(stream_count, length, D))
+    grad_streams = relayout_back(d3 + dy, BF)
+    dact = dot_f32("fr,tr->ft", down, d2_full)
+    dpre = gelu_pull(dact)[0].astype(BF)
+    g_down = scatter_weights(dot_f32("ft,tr->fr", act, d2_full).reshape(seqs, ff, D))
+    d_hid = d2 + scatter_tokens(dot_f32("ft,fr->tr", dpre, up)[None])[0]
+    d1, gain1_grad, bias1_grad = layer_norm_back(d_hid, normed1, inv1, gain1)
+    d1_full = gather_tokens(d1.astype(BF)[None])[0]
+    g_up = scatter_weights(dot_f32("ft,tr->fr", dpre, hidden_full).reshape(seqs, ff, D))
+    dmix = dot_f32("er,tr->et", m_out, d1_full).astype(BF).reshape(mix.shape)
+    g_out = dot_f32("et,tr->er", mix_flat, d1_full)
+    dq, dk, dv, doff_enc = attention_back(tiles, segq, segk, qkv, qkv, qkv, (0, 1, 2), lse, dmix, 1)
+    dqkv = jnp.concatenate([dq, dk, dv], axis=1)
+    g_qkv = dot_f32("snt,tr->snr", dqkv, x_full)
+    g_first = scatter_weights(jnp.concatenate([g_qkv, g_out.reshape(seqs, head_dim, D)], axis=1))
+    dx = scatter_tokens(dot_f32("snt,snr->tr", dqkv, m_qkv)[None])[0]
+    grad_tokens = relayout_back((d1 + dx)[None], BF)[:, 0]
+
+    norm_grads = jnp.stack([gain1_grad, bias1_grad, gain2_grad, bias2_grad, gain3_grad, bias3_grad])
+    norm_grads = jnp.where(low_y, norm_grads, jnp.roll(norm_grads, D // 2, axis=1))
+    table_grads = jnp.einsum(
+        "tho,bo->thb", jnp.stack([doff_enc[:, 0], doff_cross[:, 0]]), onehot, precision=highest
+    )
+    heads = 2 * slot_col + k
+    spread = (heads[:, None] == jnp.arange(table_heads * cols)[None, :]).astype(F32)
+    table_grads = jnp.einsum("thb,hg->tgb", table_grads, spread, precision=highest)
+    small = jnp.concatenate([norm_grads.reshape(-1, 128), table_grads.reshape(-1, 128)])
+    small = lax.psum(small, ("row", "col"))
+    count = norm_grads.size // 128
+    norm_sums = lax.dynamic_slice_in_dim(small[:count].reshape(6, D), row * feat, feat, axis=1)
+    table_sums = small[count:].reshape(2, table_heads * cols, bucket_count)
+    table_sums = lax.dynamic_slice_in_dim(table_sums, col * table_heads, table_heads, axis=1)
+    return (
+        output,
+        grad_tokens,
+        grad_streams,
+        columns_back(g_first[:, :hd3], 3),
+        table_sums[0],
+        g_first[:, hd3:].reshape(w_out.shape),
+        norm_sums[0],
+        norm_sums[1],
+        columns_back(g_up, 1).reshape(w_up.shape),
+        g_down.reshape(w_down.shape),
+        norm_sums[2],
+        norm_sums[3],
+        columns_back(g_last[:, hd2:hd3], 1).reshape(w_query.shape),
+        columns_back(g_last[:, :hd2], 2),
+        table_sums[1],
+        g_last[:, hd3:].reshape(w_cross_out.shape),
+        norm_sums[4],
+        norm_sums[5],
+    )
+
+
 def solution(mesh):
-    placed = (
-        P(None, "col", "row"),
-        P(None, None, "col", "row"),
-        P(None, None, "col", "row"),
-        P(None, "row", None),
-        P(),
-        P("row", None, "col"),
-        P("col", None),
-        P("col", "row"),
-        P("row"),
-        P("row"),
-        P("row", "col"),
-        P("col", "row"),
-        P("row"),
-        P("row"),
-        P("row", "col"),
-        P("row", None, "col"),
-        P("col", None),
-        P("col", "row"),
-        P("row"),
-        P("row"),
-    )
-    return jax.shard_map(
-        on_device,
-        mesh=mesh,
-        in_specs=placed,
-        out_specs=(
-            P(None, None, "col", "row"),
-            P(None, "col", "row"),
-            P(None, None, "col", "row"),
-            P("row", None, "col"),
-            P("col", None),
-            P("col", "row"),
-            P("row"),
-            P("row"),
-            P("row", "col"),
-            P("col", "row"),
-            P("row"),
-            P("row"),
-            P("row", "col"),
-            P("row", None, "col"),
-            P("col", None),
-            P("col", "row"),
-            P("row"),
-            P("row"),
-        ),
-        check_vma=False,
-    )
+    whole_row, half_col = mesh.shape["row"], mesh.shape["col"]
+    weights = (P("row", None, "col"), P("col", None), P("col", "row"), P("row"), P("row"), P("row", "col"), P("col", "row"), P("row"), P("row"), P("row", "col"), P("row", None, "col"), P("col", None), P("col", "row"), P("row"), P("row"))
+
+    def run(tokens, *rest):
+        micro_count = tokens.shape[0]
+        if whole_row == 2 * micro_count:
+            device_fn = functools.partial(on_device, whole_row, half_col)
+        else:
+            device_fn = on_device_general
+        return jax.shard_map(
+            device_fn,
+            mesh=mesh,
+            in_specs=(P(None, "col", "row"), P(None, None, "col", "row"), P(None, None, "col", "row"), P(None, "row", None), P()) + weights,
+            out_specs=(P(None, None, "col", "row"), P(None, "col", "row"), P(None, None, "col", "row")) + weights,
+            check_vma=False,
+        )(tokens, *rest)
+
+    return run

time: 4450 us -> 721 us (0.16)
  local copies, waits for them, and re-layouts: 2030 us -> 114 us
  waiting for transfers between devices: 2030 us -> 232 us
  matrix products: 166 us -> 34.8 us
  starting transfers between devices: 3.43 us -> 85.4 us
  Pallas kernels: 0 us -> 50.9 us
    gather x4 -> x1, local copies, waits for them, and re-layouts: 1870 us -> 0.57 us  [on_device(): own_tables = pick(jnp.take(tables, slot_col, axis=0), k, 2)]
    reduce_scatter x28 -> x0, waiting for transfers between devices: 1240 us -> none  [the longest x14 970 us: cols_product(): lax.psum_scatter(product(operand_full, matrix), 'col', scatter_dimension=...]
    all_gather x26 -> x0, waiting for transfers between devices: 785 us -> none  [the longest x14 607 us: gather_cols(): return lax.all_gather(local_rows, 'col', axis=1, tiled=True)]
    ppermute x0 -> x80, waiting for transfers between devices: none -> 232 us  [send(): return lax.ppermute(value, ('row', 'col'), pairs)]
    dot_general x72 -> x24, matrix products: 166 us -> 34.8 us  [the longest x21 34.1 us: dot_f32(): return jnp.einsum(spec, left, right, preferred_element_type=F32)]
    ppermute x0 -> x80, starting transfers between devices: none -> 85.4 us  [send(): return lax.ppermute(value, ('row', 'col'), pairs)]
    pallas_call x0 -> x4, Pallas kernels: none -> 50.9 us  [the longest x2 27.6 us: attention_back(): pl.pallas_call(functools.partial(bwd_kernel, streams, length, width), gri...]
    psum x11 -> x1, blocking collectives: 85.2 us -> 37.2 us  [on_device(): small = lax.psum(small, ('row', 'col'))]
  transfers between devices with their start and end apart: 54 -> 80, of which waited for: 46 -> 27; matrix products, arithmetic and copies ran while one was open for 50% -> 32% of each run, Pallas kernels for 0% -> 2%
where the time goes in v1:
time: 721 us; the launch traced here: 711 us
  waiting for transfers between devices  232 us (32%)
  other arithmetic  117 us (16%)
  local copies, waits for them, and re-layouts  114 us (16%)
  starting transfers between devices  85.4 us (12%)
  blocking collectives  73.9 us (10%)
  Pallas kernels  50.9 us (7%)
  matrix products  34.8 us (5%)
    ppermute x80, waiting for transfers between devices, send(): return lax.ppermute(value, ('row', 'col'), pairs)  232 us
    ppermute x80, starting transfers between devices, send(): return lax.ppermute(value, ('row', 'col'), pairs)  85.4 us
    select_n x39, other arithmetic, in_order(): jnp.where(first, join([mine, other], axis=axis), join([other, mine], axis...  42 us
    psum x1, blocking collectives, on_device(): small = lax.psum(small, ('row', 'col'))  37.2 us
    dot_general x21, matrix products, dot_f32(): return jnp.einsum(spec, left, right, preferred_element_type=F32)  34.1 us
    pallas_call x2, Pallas kernels, attention_back(): pl.pallas_call(functools.partial(bwd_kernel, streams, length, width), gri...  27.6 us
    all_gather x1, blocking collectives, on_device(): tables = lax.all_gather(jnp.stack([enc_table, cross_table]), 'col', axis=0)  26.3 us
    unnamed x275, local copies, waits for them, and re-layouts  26.1 us
  transfers between devices with their start and end apart: 80, of which 27 were waited for; matrix products, arithmetic and copies ran while one was open for 32% of the time, Pallas kernels for 2%

profile of v1, /device:TPU:0, one launch (start us, length us, event | category | flops | bytes accessed | tf_op | source)
XLA Modules:
  0.0 711.5 jit_solution(517873062648305823)
XLA Ops:
  2.0 3.0 collective-permute-start.9
  8.5 26.3 %all-gather = f32[16,2,32]{2,1,0:T(2,128)S(1)} all-gather(f32[2,2,32]{2,1,0:T(2,128)S(1)} %pad_maximum_fusion.24), channel_id=2, replica_groups=mesh['row'=4,'col'=8] {'col'}, dimensions={0}, use_global_device_ids=true | all-gather | bytes 4608 | tf_op jit(solution)/shard_map/all_gather | solution.py:568
  36.4 5.2 all_gather.15
  43.4 5.2 all_gather.14
  49.6 3.6 collective-permute-start.14
  55.6 5.1 collective-permute-done.12
  60.6 10.5 %collective-permute-done.13 = bf16[256,512]{1,0:T(8,128)(2,1)S(1)} collective-permute-done((bf16[256,512]{1,0:T(8,128)(2,1)}, bf16[256,512]{1,0:T(8,128)(2,1)S(1)}, u32[]{:S(2)}, u32[]{:S(2)}) %collective-permute-start.13) | collective-permute-done | bytes 262176 | tf_op jit(solution)/shard_map/ppermute | solution.py:476
  74.5 3.2 collective-permute-done.16
  81.3 3.1 collective-permute-start.21
  85.5 3.3 collective-permute-start.22
  90.4 6.8 collective-permute-done.15
  97.2 5.8 collective-permute-start.23
  106.0 6.1 attend.2
  128.4 3.3 collective-permute-start.30
  136.0 12.7 %collective-permute-start.5 = (bf16[256,512]{1,0:T(8,128)(2,1)S(1)}, bf16[256,512]{1,0:T(8,128)(2,1)S(1)}, u32[]{:S(2)}, u32[]{:S(2)}) collective-permute-start(bf16[256,512]{1,0:T(8,128)(2,1)S(1)} %copy-done.108), channel_id=1, source_target_pairs={{0,6},{1,7},{2,0},{3,1},{4,2},{5,3},{6,4},{7,5},{8,14},{9,15},{10,... | collective-permute-start | bytes 786440 | tf_op jit(solution)/shard_map/ppermute | solution.py:476
  154.9 11.3 %collective-permute-done.4 = bf16[256,512]{1,0:T(8,128)(2,1)S(1)} collective-permute-done((bf16[256,512]{1,0:T(8,128)(2,1)S(1)}, bf16[256,512]{1,0:T(8,128)(2,1)S(1)}, u32[]{:S(2)}, u32[]{:S(2)}) %collective-permute-start.4) | collective-permute-done | bytes 262176 | tf_op jit(solution)/shard_map/ppermute | solution.py:476
  179.3 5.4 collective-permute-done.24
  186.4 20.8 %collective-permute-done.31 = bf16[4,256,512]{2,1,0:T(8,128)(2,1)} collective-permute-done((bf16[4,256,512]{2,1,0:T(8,128)(2,1)}, bf16[4,256,512]{2,1,0:T(8,128)(2,1)}, u32[]{:S(2)}, u32[]{:S(2)}) %collective-permute-start.31) | collective-permute-done | bytes 1048608 | tf_op jit(solution)/shard_map/ppermute | solution.py:476
  211.7 7.2 %fusion.13 = (bf16[512,1024]{0,1:T(8,128)(2,1)}, f32[512,1024]{0,1:T(8,128)}, f32[1024,512]{1,0:T(8,128)}) fusion(bf16[1024,1024]{1,0:T(8,128)(2,1)S(1)} %bitcast.683, bf16[512,1024]{1,0:T(8,128)(2,1)S(1)} %bitcast.638), kind=kOutput, calls=%fused_computation.45 | convolution fusion | flops 1107820544 | bytes 8388608 | tf_op jit(solution)/shard_map/fr,tr->ft/dot_general | solution.py:520
  221.1 3.2 fusion.136
  236.1 14.1 %collective-permute-done.7 = bf16[3,128,1024]{2,1,0:T(8,128)(2,1)} collective-permute-done((bf16[3,128,1024]{2,1,0:T(8,128)(2,1)}, bf16[3,128,1024]{2,1,0:T(8,128)(2,1)}, u32[]{:S(2)}, u32[]{:S(2)}) %collective-permute-start.7) | collective-permute-done | bytes 786464 | tf_op jit(solution)/shard_map/ppermute | solution.py:476
  259.8 3.2 collective-permute-done.34
  267.0 17.2 %attend.3 = (bf16[4,64,1536]{2,1,0:T(8,128)(2,1)S(1)}, f32[4,1,1536]{2,1,0:T(1,128)S(1)}, f32[4,896,128]{2,1,0:T(8,128)S(1)}) custom-call(f32[4,1,1024]{2,1,0:T(1,128)S(1)} %get-tuple-element.211.off_ref, s32[1,512]{1,0:T(1,128)S(1)} %fusion.187.segq_ref, s32[512,128]{1,0:T(8,128)S(1)} %broadcast_in_dim.17.segk_ref, ...), custom_call_target="tpu_custom_call" | custom-call | tf_op jit(solution)/shard_map/attend/pallas_call | solution.py:446
  294.0 10.6 %collective-permute-done.40 = bf16[3,256,256]{2,1,0:T(8,128)(2,1)S(1)} collective-permute-done((bf16[3,256,256]{2,1,0:T(8,128)(2,1)S(1)}, bf16[3,256,256]{2,1,0:T(8,128)(2,1)S(1)}, u32[]{:S(2)}, u32[]{:S(2)}) %collective-permute-start.40) | collective-permute-done | bytes 393248 | tf_op jit(solution)/shard_map/ppermute | solution.py:476
  305.5 2.9 reshape.3335
  311.6 2.9 bitcast_add_fusion.1
  323.3 3.7 reshape.3356
  328.7 8.8 %collective-permute-done.37 = bf16[3,128,1024]{2,1,0:T(8,128)(2,1)} collective-permute-done((bf16[3,128,1024]{2,1,0:T(8,128)(2,1)}, bf16[3,128,1024]{2,1,0:T(8,128)(2,1)}, u32[]{:S(2)}, u32[]{:S(2)}) %collective-permute-start.37) | collective-permute-done | bytes 786464 | tf_op jit(solution)/shard_map/ppermute | solution.py:476
  342.0 18.6 %collective-permute-done.42 = bf16[3,128,1024]{2,1,0:T(8,128)(2,1)S(1)} collective-permute-done((bf16[3,128,1024]{2,1,0:T(8,128)(2,1)S(1)}, bf16[3,128,1024]{2,1,0:T(8,128)(2,1)S(1)}, u32[]{:S(2)}, u32[]{:S(2)}) %collective-permute-start.42) | collective-permute-done | bytes 786464 | tf_op jit(solution)/shard_map/ppermute | solution.py:476
  371.6 20.0 %attend_back.2 = (bf16[4,64,1536]{2,1,0:T(8,128)(2,1)S(1)}, bf16[4,64,512]{2,1,0:T(8,128)(2,1)S(1)}, bf16[4,64,512]{2,1,0:T(8,128)(2,1)S(1)}, f32[4,1,1024]{2,1,0:T(1,128)S(1)}) custom-call(f32[4,896,128]{2,1,0:T(8,128)S(1)} %copy-done.3, s32[1,512]{1,0:T(1,128)S(1)} %fusion.187.segq_ref, s32[512,128]{1,0:T(8,128)S(1)} %broadcast_in_dim.17.segk_ref, ...), custom_call_target="tpu_custom_call" | custom-call | tf_op jit(solution)/shard_map/attend_back/pallas_call | solution.py:461
  401.8 5.3 collective-permute-done.45
  407.6 15.9 %collective-permute-done.75 = bf16[4,256,512]{2,1,0:T(8,128)(2,1)S(1)} collective-permute-done((bf16[4,256,512]{2,1,0:T(8,128)(2,1)S(1)}, bf16[4,256,512]{2,1,0:T(8,128)(2,1)S(1)}, u32[]{:S(2)}, u32[]{:S(2)}) %collective-permute-start.75) | collective-permute-done | bytes 1048608 | tf_op jit(solution)/shard_map/ppermute | solution.py:476
  424.8 7.4 %collective-permute-start.77 = (bf16[256,512]{1,0:T(8,128)(2,1)S(1)}, bf16[256,512]{1,0:T(8,128)(2,1)S(1)}, u32[]{:S(2)}, u32[]{:S(2)}) collective-permute-start(bf16[256,512]{1,0:T(8,128)(2,1)S(1)} %get-tuple-element.151), channel_id=1, source_target_pairs={{0,4},{1,5},{2,6},{3,7},{4,0},{5,1},{6,2},{7,3},{8,12},{9,13},{10,... | collective-permute-start | bytes 786440 | tf_op jit(solution)/shard_map/ppermute | solution.py:476
  436.9 18.1 %collective-permute-done.77 = bf16[256,512]{1,0:T(8,128)(2,1)S(1)} collective-permute-done((bf16[256,512]{1,0:T(8,128)(2,1)S(1)}, bf16[256,512]{1,0:T(8,128)(2,1)S(1)}, u32[]{:S(2)}, u32[]{:S(2)}) %collective-permute-start.77) | collective-permute-done | bytes 262176 | tf_op jit(solution)/shard_map/ppermute | solution.py:476
  461.4 5.8 multiply_convert_fusion
  482.5 3.0 bitcast_add_fusion
  496.9 3.0 fusion.139
  509.8 3.5 fusion.34
  513.4 3.0 reshape.3339
  533.2 17.7 %collective-permute-done.70 = bf16[4,256,512]{2,1,0:T(8,128)(2,1)} collective-permute-done((bf16[4,256,512]{2,1,0:T(8,128)(2,1)}, bf16[4,256,512]{2,1,0:T(8,128)(2,1)}, u32[]{:S(2)}, u32[]{:S(2)}) %collective-permute-start.70) | collective-permute-done | bytes 1048608 | tf_op jit(solution)/shard_map/ppermute | solution.py:476
  552.7 3.9 collective-permute-start.71
  556.6 5.4 collective-permute-done.68
  562.3 4.6 collective-permute-done.71
  567.4 15.0 %collective-permute-done.72 = bf16[256,512]{1,0:T(8,128)(2,1)S(1)} collective-permute-done((bf16[256,512]{1,0:T(8,128)(2,1)S(1)}, bf16[256,512]{1,0:T(8,128)(2,1)S(1)}, u32[]{:S(2)}, u32[]{:S(2)}) %collective-permute-start.72) | collective-permute-done | bytes 262176 | tf_op jit(solution)/shard_map/ppermute | solution.py:476
  601.5 7.6 %attend_back.3 = (bf16[4,64,512]{2,1,0:T(8,128)(2,1)S(1)}, bf16[4,64,512]{2,1,0:T(8,128)(2,1)S(1)}, bf16[4,64,512]{2,1,0:T(8,128)(2,1)S(1)}, f32[4,1,1024]{2,1,0:T(1,128)S(1)}) custom-call(f32[4,896,128]{2,1,0:T(8,128)S(1)} %copy-done.1, s32[1,512]{1,0:T(1,128)S(1)} %fusion.187.segq_ref, s32[512,128]{1,0:T(8,128)S(1)} %broadcast_in_dim.17.segk_ref, ...), custom_call_target="tpu_custom_call" | custom-call | tf_op jit(solution)/shard_map/attend_back/pallas_call | solution.py:461
  614.8 37.2 %psum.7 = f32[56,128]{1,0:T(8,128)S(1)} all-reduce(f32[56,128]{1,0:T(8,128)S(1)} %pad_maximum_fusion.23), channel_id=1, replica_groups=mesh['row'=4,'col'=8] {'row','col'}, use_global_device_ids=true, to_apply=%region_18.19 | all-reduce | flops 7168 | bytes 57344 | tf_op jit(solution)/shard_map/psum | solution.py:702
  669.4 5.4 collective-permute-done.53
  690.4 16.5 %collective-permute-done.62 = bf16[256,512]{1,0:T(8,128)(2,1)S(1)} collective-permute-done((bf16[256,512]{1,0:T(8,128)(2,1)S(1)}, bf16[256,512]{1,0:T(8,128)(2,1)S(1)}, u32[]{:S(2)}, u32[]{:S(2)}) %collective-permute-start.62) | collective-permute-done | bytes 262176 | tf_op jit(solution)/shard_map/ppermute | solution.py:476
  (664 shorter events, 276.6 us)
Async XLA Ops:
  2.0 51.2 %collective-permute-start.9 = (bf16[1,256,256]{2,1,0:T(8,128)(2,1)S(1)}, bf16[1,256,256]{2,1,0:T(8,128)(2,1)S(1)}, u32[]{:S(2)}, u32[]{:S(2)}) collective-permute-start(bf16[1,256,256]{2,1,0:T(8,128)(2,1)S(1)} %get-tuple-element.193), channel_id=1, source_target_pairs={{0,16},{1,17},{2,18},{3,19},{4,20},{5,21},{6,22},{7,23},{8,24},{9,... | collective-permute-start | bytes 393224 | tf_op jit(solution)/shard_map/ppermute | solution.py:476
  7.0 41.6 %collective-permute-start.11 = (bf16[256,256]{1,0:T(8,128)(2,1)S(1)}, bf16[256,256]{1,0:T(8,128)(2,1)S(1)}, u32[]{:S(2)}, u32[]{:S(2)}) collective-permute-start(bf16[256,256]{1,0:T(8,128)(2,1)S(1)} %get-tuple-element.189), channel_id=1, source_target_pairs={{0,8},{1,9},{2,10},{3,11},{4,12},{5,13},{6,14},{7,15},{8,0},{9,1},... | collective-permute-start | bytes 393224 | tf_op jit(solution)/shard_map/ppermute | solution.py:476
  7.9 71.6 %collective-permute-start.20 = (bf16[256,256]{1,0:T(8,128)(2,1)}, bf16[256,256]{1,0:T(8,128)(2,1)S(1)}, u32[]{:S(2)}, u32[]{:S(2)}) collective-permute-start(bf16[256,256]{1,0:T(8,128)(2,1)} %get-tuple-element.186), channel_id=1, source_target_pairs={{0,8},{1,9},{2,10},{3,11},{4,12},{5,13},{6,14},{7,15},{8,0},{9,1},... | collective-permute-start | bytes 393224 | tf_op jit(solution)/shard_map/ppermute | solution.py:476
  49.6 21.5 %collective-permute-start.13 = (bf16[256,512]{1,0:T(8,128)(2,1)}, bf16[256,512]{1,0:T(8,128)(2,1)S(1)}, u32[]{:S(2)}, u32[]{:S(2)}) collective-permute-start(bf16[256,512]{1,0:T(8,128)(2,1)} %maximum_select_fusion.30), channel_id=1, source_target_pairs={{0,4},{1,5},{2,6},{3,7},{4,0},{5,1},{6,2},{7,3},{8,12},{9,13},{10,... | collective-permute-start | bytes 786440 | tf_op jit(solution)/shard_map/ppermute | solution.py:476
  49.6 23.0 %collective-permute-start.14 = (bf16[256,512]{1,0:T(8,128)(2,1)}, bf16[256,512]{1,0:T(8,128)(2,1)S(1)}, u32[]{:S(2)}, u32[]{:S(2)}) collective-permute-start(bf16[256,512]{1,0:T(8,128)(2,1)} %maximum_select_fusion.30), channel_id=1, source_target_pairs={{0,6},{1,7},{2,0},{3,1},{4,2},{5,3},{6,4},{7,5},{8,14},{9,15},{10,... | collective-permute-start | bytes 786440 | tf_op jit(solution)/shard_map/ppermute | solution.py:476
  54.9 62.4 %collective-permute-start.27 = (bf16[256,256]{1,0:T(8,128)(2,1)}, bf16[256,256]{1,0:T(8,128)(2,1)}, u32[]{:S(2)}, u32[]{:S(2)}) collective-permute-start(bf16[256,256]{1,0:T(8,128)(2,1)} %get-tuple-element.184), channel_id=1, source_target_pairs={{0,8},{1,9},{2,10},{3,11},{4,12},{5,13},{6,14},{7,15},{8,0},{9,1},... | collective-permute-start | bytes 393224 | tf_op jit(solution)/shard_map/ppermute | solution.py:476
  60.6 60.3 %collective-permute-start.2 = (bf16[256,256]{1,0:T(8,128)(2,1)}, bf16[256,256]{1,0:T(8,128)(2,1)}, u32[]{:S(2)}, u32[]{:S(2)}) collective-permute-start(bf16[256,256]{1,0:T(8,128)(2,1)} %get-tuple-element.195), channel_id=1, source_target_pairs={{0,8},{1,9},{2,10},{3,11},{4,12},{5,13},{6,14},{7,15},{8,0},{9,1},... | collective-permute-start | bytes 393224 | tf_op jit(solution)/shard_map/ppermute | solution.py:476
  73.7 23.5 %collective-permute-start.15 = (bf16[4,256,512]{2,1,0:T(8,128)(2,1)}, bf16[4,256,512]{2,1,0:T(8,128)(2,1)}, u32[]{:S(2)}, u32[]{:S(2)}) collective-permute-start(bf16[4,256,512]{2,1,0:T(8,128)(2,1)} %pad_maximum_fusion.11), channel_id=1, source_target_pairs={{0,16},{1,17},{2,18},{3,19},{4,20},{5,21},{6,22},{7,23},{8,24},{9,... | collective-permute-start | bytes 3145736 | tf_op jit(solution)/shard_map/ppermute | solution.py:476
  81.3 46.5 %collective-permute-start.21 = (bf16[256,512]{1,0:T(8,128)(2,1)}, bf16[256,512]{1,0:T(8,128)(2,1)}, u32[]{:S(2)}, u32[]{:S(2)}) collective-permute-start(bf16[256,512]{1,0:T(8,128)(2,1)} %maximum_select_fusion.32), channel_id=1, source_target_pairs={{0,2},{1,3},{2,4},{3,5},{4,6},{5,7},{6,0},{7,1},{8,10},{9,11},{10,... | collective-permute-start | bytes 786440 | tf_op jit(solution)/shard_map/ppermute | solution.py:476
  85.5 42.9 %collective-permute-start.22 = (bf16[256,512]{1,0:T(8,128)(2,1)}, bf16[256,512]{1,0:T(8,128)(2,1)}, u32[]{:S(2)}, u32[]{:S(2)}) collective-permute-start(bf16[256,512]{1,0:T(8,128)(2,1)} %maximum_select_fusion.32), channel_id=1, source_target_pairs={{0,4},{1,5},{2,6},{3,7},{4,0},{5,1},{6,2},{7,3},{8,12},{9,13},{10,... | collective-permute-start | bytes 786440 | tf_op jit(solution)/shard_map/ppermute | solution.py:476
  97.2 34.5 %collective-permute-start.23 = (bf16[256,512]{1,0:T(8,128)(2,1)}, bf16[256,512]{1,0:T(8,128)(2,1)}, u32[]{:S(2)}, u32[]{:S(2)}) collective-permute-start(bf16[256,512]{1,0:T(8,128)(2,1)} %maximum_select_fusion.32), channel_id=1, source_target_pairs={{0,6},{1,7},{2,0},{3,1},{4,2},{5,3},{6,4},{7,5},{8,14},{9,15},{10,... | collective-permute-start | bytes 786440 | tf_op jit(solution)/shard_map/ppermute | solution.py:476
  127.8 22.2 %collective-permute-start.29 = (bf16[256,512]{1,0:T(8,128)(2,1)}, bf16[256,512]{1,0:T(8,128)(2,1)S(1)}, u32[]{:S(2)}, u32[]{:S(2)}) collective-permute-start(bf16[256,512]{1,0:T(8,128)(2,1)} %maximum_select_fusion.34), channel_id=1, source_target_pairs={{0,4},{1,5},{2,6},{3,7},{4,0},{5,1},{6,2},{7,3},{8,12},{9,13},{10,... | collective-permute-start | bytes 786440 | tf_op jit(solution)/shard_map/ppermute | solution.py:476
  128.4 22.2 %collective-permute-start.30 = (bf16[256,512]{1,0:T(8,128)(2,1)}, bf16[256,512]{1,0:T(8,128)(2,1)S(1)}, u32[]{:S(2)}, u32[]{:S(2)}) collective-permute-start(bf16[256,512]{1,0:T(8,128)(2,1)} %maximum_select_fusion.34), channel_id=1, source_target_pairs={{0,6},{1,7},{2,0},{3,1},{4,2},{5,3},{6,4},{7,5},{8,14},{9,15},{10,... | collective-permute-start | bytes 786440 | tf_op jit(solution)/shard_map/ppermute | solution.py:476
  131.7 21.6 %collective-permute-start.3 = (bf16[256,512]{1,0:T(8,128)(2,1)}, bf16[256,512]{1,0:T(8,128)(2,1)S(1)}, u32[]{:S(2)}, u32[]{:S(2)}) collective-permute-start(bf16[256,512]{1,0:T(8,128)(2,1)} %maximum_select_fusion.27), channel_id=1, source_target_pairs={{0,2},{1,3},{2,4},{3,5},{4,6},{5,7},{6,0},{7,1},{8,10},{9,11},{10,... | collective-permute-start | bytes 786440 | tf_op jit(solution)/shard_map/ppermute | solution.py:476
  134.6 31.6 %collective-permute-start.4 = (bf16[256,512]{1,0:T(8,128)(2,1)S(1)}, bf16[256,512]{1,0:T(8,128)(2,1)S(1)}, u32[]{:S(2)}, u32[]{:S(2)}) collective-permute-start(bf16[256,512]{1,0:T(8,128)(2,1)S(1)} %copy-done.108), channel_id=1, source_target_pairs={{0,4},{1,5},{2,6},{3,7},{4,0},{5,1},{6,2},{7,3},{8,12},{9,13},{10,... | collective-permute-start | bytes 786440 | tf_op jit(solution)/shard_map/ppermute | solution.py:476
  136.0 30.6 %collective-permute-start.5 = (bf16[256,512]{1,0:T(8,128)(2,1)S(1)}, bf16[256,512]{1,0:T(8,128)(2,1)S(1)}, u32[]{:S(2)}, u32[]{:S(2)}) collective-permute-start(bf16[256,512]{1,0:T(8,128)(2,1)S(1)} %copy-done.108), channel_id=1, source_target_pairs={{0,6},{1,7},{2,0},{3,1},{4,2},{5,3},{6,4},{7,5},{8,14},{9,15},{10,... | collective-permute-start | bytes 786440 | tf_op jit(solution)/shard_map/ppermute | solution.py:476
  150.0 21.2 %collective-permute-start = (bf16[3,256,256]{2,1,0:T(8,128)(2,1)S(1)}, bf16[3,256,256]{2,1,0:T(8,128)(2,1)S(1)}, u32[]{:S(2)}, u32[]{:S(2)}) collective-permute-start(bf16[3,256,256]{2,1,0:T(8,128)(2,1)S(1)} %copy-done.107), channel_id=1, source_target_pairs={{0,16},{1,17},{2,18},{3,19},{4,20},{5,21},{6,22},{7,23},{8,24},{9,... | collective-permute-start | bytes 1179656 | tf_op jit(solution)/shard_map/ppermute | solution.py:476
  150.6 18.7 %collective-permute-start.19 = (bf16[1,128,1024]{2,1,0:T(8,128)(2,1)S(1)}, bf16[1,128,1024]{2,1,0:T(8,128)(2,1)S(1)}, u32[]{:S(2)}, u32[]{:S(2)}) collective-permute-start(bf16[1,128,1024]{2,1,0:T(8,128)(2,1)S(1)} %fusion.86), channel_id=1, source_target_pairs={{0,1},{1,0},{2,3},{3,2},{4,5},{5,4},{6,7},{7,6},{8,9},{9,8},{10,11... | collective-permute-start | bytes 786440 | tf_op jit(solution)/shard_map/ppermute | solution.py:476
  153.3 31.4 %collective-permute-start.24 = (bf16[4,256,512]{2,1,0:T(8,128)(2,1)}, bf16[4,256,512]{2,1,0:T(8,128)(2,1)}, u32[]{:S(2)}, u32[]{:S(2)}) collective-permute-start(bf16[4,256,512]{2,1,0:T(8,128)(2,1)} %pad_maximum_fusion.12), channel_id=1, source_target_pairs={{0,16},{1,17},{2,18},{3,19},{4,20},{5,21},{6,22},{7,23},{8,24},{9,... | collective-permute-start | bytes 3145736 | tf_op jit(solution)/shard_map/ppermute | solution.py:476
  166.2 41.1 %collective-permute-start.31 = (bf16[4,256,512]{2,1,0:T(8,128)(2,1)}, bf16[4,256,512]{2,1,0:T(8,128)(2,1)}, u32[]{:S(2)}, u32[]{:S(2)}) collective-permute-start(bf16[4,256,512]{2,1,0:T(8,128)(2,1)} %pad_maximum_fusion.13), channel_id=1, source_target_pairs={{0,16},{1,17},{2,18},{3,19},{4,20},{5,21},{6,22},{7,23},{8,24},{9,... | collective-permute-start | bytes 3145736 | tf_op jit(solution)/shard_map/ppermute | solution.py:476
  167.8 84.1 %collective-permute-start.6 = (bf16[4,256,512]{2,1,0:T(8,128)(2,1)}, bf16[4,256,512]{2,1,0:T(8,128)(2,1)}, u32[]{:S(2)}, u32[]{:S(2)}) collective-permute-start(bf16[4,256,512]{2,1,0:T(8,128)(2,1)} %pad_maximum_fusion.10), channel_id=1, source_target_pairs={{0,16},{1,17},{2,18},{3,19},{4,20},{5,21},{6,22},{7,23},{8,24},{9,... | collective-permute-start | bytes 3145736 | tf_op jit(solution)/shard_map/ppermute | solution.py:476
  174.9 50.5 %collective-permute-start.1 = (bf16[3,128,2,1,256]{4,1,3,2,0:T(8,128)(2,1)}, bf16[3,128,2,1,256]{4,1,3,2,0:T(8,128)(2,1)}, u32[]{:S(2)}, u32[]{:S(2)}) collective-permute-start(bf16[3,128,2,1,256]{4,1,3,2,0:T(8,128)(2,1)} %bitcast.607), channel_id=1, source_target_pairs={{0,8},{1,9},{2,10},{3,11},{4,12},{5,13},{6,14},{7,15},{8,0},{9,1},... | collective-permute-start | bytes 1179656 | tf_op jit(solution)/shard_map/ppermute | solution.py:476
  179.3 32.1 %collective-permute-start.26 = (bf16[1,2,128,1024]{3,2,1,0:T(8,128)(2,1)S(1)}, bf16[1,2,128,1024]{3,2,1,0:T(8,128)(2,1)S(1)}, u32[]{:S(2)}, u32[]{:S(2)}) collective-permute-start(bf16[1,2,128,1024]{3,2,1,0:T(8,128)(2,1)S(1)} %bitcast_select_fusion.1), channel_id=1, source_target_pairs={{0,8},{1,9},{2,10},{3,11},{4,12},{5,13},{6,14},{7,15},{8,0},{9,1},... | collective-permute-start | bytes 1572872 | tf_op jit(solution)/shard_map/ppermute | solution.py:476
  229.4 20.7 %collective-permute-start.7 = (bf16[3,128,1024]{2,1,0:T(8,128)(2,1)}, bf16[3,128,1024]{2,1,0:T(8,128)(2,1)}, u32[]{:S(2)}, u32[]{:S(2)}) collective-permute-start(bf16[3,128,1024]{2,1,0:T(8,128)(2,1)} %select_n.757), channel_id=1, source_target_pairs={{0,1},{1,0},{2,3},{3,2},{4,5},{5,4},{6,7},{7,6},{8,9},{9,8},{10,11... | collective-permute-start | bytes 2359304 | tf_op jit(solution)/shard_map/ppermute | solution.py:476
  234.5 20.1 %collective-permute-start.33 = (bf16[1,128,1024]{2,1,0:T(8,128)(2,1)S(1)}, bf16[1,128,1024]{2,1,0:T(8,128)(2,1)S(1)}, u32[]{:S(2)}, u32[]{:S(2)}) collective-permute-start(bf16[1,128,1024]{2,1,0:T(8,128)(2,1)S(1)} %fusion.87), channel_id=1, source_target_pairs={{0,1},{1,0},{2,3},{3,2},{4,5},{5,4},{6,7},{7,6},{8,9},{9,8},{10,11... | collective-permute-start | bytes 786440 | tf_op jit(solution)/shard_map/ppermute | solution.py:476
  292.9 18.7 %collective-permute-start.36 = (bf16[3,2,128,1024]{3,2,1,0:T(8,128)(2,1)}, bf16[3,2,128,1024]{3,2,1,0:T(8,128)(2,1)}, u32[]{:S(2)}, u32[]{:S(2)}) collective-permute-start(bf16[3,2,128,1024]{3,2,1,0:T(8,128)(2,1)} %fusion.31), channel_id=1, source_target_pairs={{0,8},{1,9},{2,10},{3,11},{4,12},{5,13},{6,14},{7,15},{8,0},{9,1},... | collective-permute-start | bytes 4718600 | tf_op jit(solution)/shard_map/ppermute | solution.py:476
  317.3 20.3 %collective-permute-start.37 = (bf16[3,128,1024]{2,1,0:T(8,128)(2,1)}, bf16[3,128,1024]{2,1,0:T(8,128)(2,1)}, u32[]{:S(2)}, u32[]{:S(2)}) collective-permute-start(bf16[3,128,1024]{2,1,0:T(8,128)(2,1)} %fusion.44), channel_id=1, source_target_pairs={{0,1},{1,0},{2,3},{3,2},{4,5},{5,4},{6,7},{7,6},{8,9},{9,8},{10,11... | collective-permute-start | bytes 2359304 | tf_op jit(solution)/shard_map/ppermute | solution.py:476
  341.4 19.2 %collective-permute-start.42 = (bf16[3,128,1024]{2,1,0:T(8,128)(2,1)S(1)}, bf16[3,128,1024]{2,1,0:T(8,128)(2,1)S(1)}, u32[]{:S(2)}, u32[]{:S(2)}) collective-permute-start(bf16[3,128,1024]{2,1,0:T(8,128)(2,1)S(1)} %fusion.99), channel_id=1, source_target_pairs={{0,1},{1,0},{2,3},{3,2},{4,5},{5,4},{6,7},{7,6},{8,9},{9,8},{10,11... | collective-permute-start | bytes 2359304 | tf_op jit(solution)/shard_map/ppermute | solution.py:476
  398.0 25.5 %collective-permute-start.75 = (bf16[4,256,512]{2,1,0:T(8,128)(2,1)S(1)}, bf16[4,256,512]{2,1,0:T(8,128)(2,1)S(1)}, u32[]{:S(2)}, u32[]{:S(2)}) collective-permute-start(bf16[4,256,512]{2,1,0:T(8,128)(2,1)S(1)} %slice.359), channel_id=1, source_target_pairs={{0,16},{1,17},{2,18},{3,19},{4,20},{5,21},{6,22},{7,23},{8,24},{9,... | collective-permute-start | bytes 3145736 | tf_op jit(solution)/shard_map/ppermute | solution.py:476
  401.8 80.7 %collective-permute-start.56 = (bf16[3,2,128,1024]{3,2,0,1:T(8,128)(2,1)}, bf16[3,2,128,1024]{3,2,0,1:T(8,128)(2,1)}, u32[]{:S(2)}, u32[]{:S(2)}) collective-permute-start(bf16[3,2,128,1024]{3,2,0,1:T(8,128)(2,1)} %fusion.32), channel_id=1, source_target_pairs={{0,8},{1,9},{2,10},{3,11},{4,12},{5,13},{6,14},{7,15},{8,0},{9,1},... | collective-permute-start | bytes 4718600 | tf_op jit(solution)/shard_map/ppermute | solution.py:476
  424.8 30.2 %collective-permute-start.77 = (bf16[256,512]{1,0:T(8,128)(2,1)S(1)}, bf16[256,512]{1,0:T(8,128)(2,1)S(1)}, u32[]{:S(2)}, u32[]{:S(2)}) collective-permute-start(bf16[256,512]{1,0:T(8,128)(2,1)S(1)} %get-tuple-element.151), channel_id=1, source_target_pairs={{0,4},{1,5},{2,6},{3,7},{4,0},{5,1},{6,2},{7,3},{8,12},{9,13},{10,... | collective-permute-start | bytes 786440 | tf_op jit(solution)/shard_map/ppermute | solution.py:476
  432.2 22.8 %collective-permute-start.78 = (bf16[256,512]{1,0:T(8,128)(2,1)S(1)}, bf16[256,512]{1,0:T(8,128)(2,1)S(1)}, u32[]{:S(2)}, u32[]{:S(2)}) collective-permute-start(bf16[256,512]{1,0:T(8,128)(2,1)S(1)} %get-tuple-element.150), channel_id=1, source_target_pairs={{0,2},{1,3},{2,4},{3,5},{4,6},{5,7},{6,0},{7,1},{8,10},{9,11},{10,... | collective-permute-start | bytes 786440 | tf_op jit(solution)/shard_map/ppermute | solution.py:476
  435.4 36.4 %collective-permute-start.46 = (bf16[1,128,1024]{2,1,0:T(8,128)(2,1)}, bf16[1,128,1024]{2,1,0:T(8,128)(2,1)}, u32[]{:S(2)}, u32[]{:S(2)}) collective-permute-start(bf16[1,128,1024]{2,1,0:T(8,128)(2,1)} %get-tuple-element.129), channel_id=1, source_target_pairs={{0,1},{1,0},{2,3},{3,2},{4,5},{5,4},{6,7},{7,6},{8,9},{9,8},{10,11... | collective-permute-start | bytes 786440 | tf_op jit(solution)/shard_map/ppermute | solution.py:476
  486.6 22.8 %collective-permute-start.57 = (bf16[3,128,1024]{2,1,0:T(8,128)(2,1)}, bf16[3,128,1024]{2,1,0:T(8,128)(2,1)}, u32[]{:S(2)}, u32[]{:S(2)}) collective-permute-start(bf16[3,128,1024]{2,1,0:T(8,128)(2,1)} %fusion.45), channel_id=1, source_target_pairs={{0,1},{1,0},{2,3},{3,2},{4,5},{5,4},{6,7},{7,6},{8,9},{9,8},{10,11... | collective-permute-start | bytes 2359304 | tf_op jit(solution)/shard_map/ppermute | solution.py:476
  502.5 27.9 %collective-permute-start.65 = (bf16[4,256,512]{2,1,0:T(8,128)(2,1)}, bf16[4,256,512]{2,1,0:T(8,128)(2,1)}, u32[]{:S(2)}, u32[]{:S(2)}) collective-permute-start(bf16[4,256,512]{2,1,0:T(8,128)(2,1)} %slice.361), channel_id=1, source_target_pairs={{0,16},{1,17},{2,18},{3,19},{4,20},{5,21},{6,22},{7,23},{8,24},{9,... | collective-permute-start | bytes 3145736 | tf_op jit(solution)/shard_map/ppermute | solution.py:476
  507.1 43.8 %collective-permute-start.70 = (bf16[4,256,512]{2,1,0:T(8,128)(2,1)}, bf16[4,256,512]{2,1,0:T(8,128)(2,1)}, u32[]{:S(2)}, u32[]{:S(2)}) collective-permute-start(bf16[4,256,512]{2,1,0:T(8,128)(2,1)} %slice.360), channel_id=1, source_target_pairs={{0,16},{1,17},{2,18},{3,19},{4,20},{5,21},{6,22},{7,23},{8,24},{9,... | collective-permute-start | bytes 3145736 | tf_op jit(solution)/shard_map/ppermute | solution.py:476
  518.8 69.7 %collective-permute-start.58 = (f32[3,128,2,256]{3,1,0,2:T(8,128)}, f32[3,128,2,256]{3,1,0,2:T(8,128)}, u32[]{:S(2)}, u32[]{:S(2)}) collective-permute-start(f32[3,128,2,256]{3,1,0,2:T(8,128)} %bitcast.601), channel_id=1, source_target_pairs={{0,8},{1,9},{2,10},{3,11},{4,12},{5,13},{6,14},{7,15},{8,0},{9,1},... | collective-permute-start | bytes 2359304 | tf_op jit(solution)/shard_map/ppermute | solution.py:476
  525.2 66.3 %collective-permute-start.38 = (f32[3,128,2,256]{3,1,0,2:T(8,128)}, f32[3,128,2,256]{3,1,0,2:T(8,128)}, u32[]{:S(2)}, u32[]{:S(2)}) collective-permute-start(f32[3,128,2,256]{3,1,0,2:T(8,128)} %bitcast.603), channel_id=1, source_target_pairs={{0,8},{1,9},{2,10},{3,11},{4,12},{5,13},{6,14},{7,15},{8,0},{9,1},... | collective-permute-start | bytes 2359304 | tf_op jit(solution)/shard_map/ppermute | solution.py:476
  533.0 19.6 %collective-permute-start.66 = (bf16[256,512]{1,0:T(8,128)(2,1)S(1)}, bf16[256,512]{1,0:T(8,128)(2,1)S(1)}, u32[]{:S(2)}, u32[]{:S(2)}) collective-permute-start(bf16[256,512]{1,0:T(8,128)(2,1)S(1)} %get-tuple-element.155), channel_id=1, source_target_pairs={{0,6},{1,7},{2,0},{3,1},{4,2},{5,3},{6,4},{7,5},{8,14},{9,15},{10,... | collective-permute-start | bytes 786440 | tf_op jit(solution)/shard_map/ppermute | solution.py:476
  533.1 23.5 %collective-permute-start.67 = (bf16[256,512]{1,0:T(8,128)(2,1)S(1)}, bf16[256,512]{1,0:T(8,128)(2,1)S(1)}, u32[]{:S(2)}, u32[]{:S(2)}) collective-permute-start(bf16[256,512]{1,0:T(8,128)(2,1)S(1)} %get-tuple-element.157), channel_id=1, source_target_pairs={{0,4},{1,5},{2,6},{3,7},{4,0},{5,1},{6,2},{7,3},{8,12},{9,13},{10,... | collective-permute-start | bytes 786440 | tf_op jit(solution)/shard_map/ppermute | solution.py:476
  556.6 25.8 %collective-permute-start.72 = (bf16[256,512]{1,0:T(8,128)(2,1)S(1)}, bf16[256,512]{1,0:T(8,128)(2,1)S(1)}, u32[]{:S(2)}, u32[]{:S(2)}) collective-permute-start(bf16[256,512]{1,0:T(8,128)(2,1)S(1)} %get-tuple-element.154), channel_id=1, source_target_pairs={{0,4},{1,5},{2,6},{3,7},{4,0},{5,1},{6,2},{7,3},{8,12},{9,13},{10,... | collective-permute-start | bytes 786440 | tf_op jit(solution)/shard_map/ppermute | solution.py:476
  561.9 20.4 %collective-permute-start.73 = (bf16[256,512]{1,0:T(8,128)(2,1)S(1)}, bf16[256,512]{1,0:T(8,128)(2,1)S(1)}, u32[]{:S(2)}, u32[]{:S(2)}) collective-permute-start(bf16[256,512]{1,0:T(8,128)(2,1)S(1)} %get-tuple-element.153), channel_id=1, source_target_pairs={{0,2},{1,3},{2,4},{3,5},{4,6},{5,7},{6,0},{7,1},{8,10},{9,11},{10,... | collective-permute-start | bytes 786440 | tf_op jit(solution)/shard_map/ppermute | solution.py:476
  591.0 71.6 %collective-permute-start.59 = (bf16[3,256,256]{2,1,0:T(8,128)(2,1)}, bf16[3,256,256]{2,1,0:T(8,128)(2,1)}, u32[]{:S(2)}, u32[]{:S(2)}) collective-permute-start(bf16[3,256,256]{2,1,0:T(8,128)(2,1)} %fusion.85), channel_id=1, source_target_pairs={{0,16},{1,17},{2,18},{3,19},{4,20},{5,21},{6,22},{7,23},{8,24},{9,... | collective-permute-start | bytes 1179656 | tf_op jit(solution)/shard_map/ppermute | solution.py:476
  593.9 69.8 %collective-permute-start.39 = (bf16[3,256,256]{2,1,0:T(8,128)(2,1)}, bf16[3,256,256]{2,1,0:T(8,128)(2,1)}, u32[]{:S(2)}, u32[]{:S(2)}) collective-permute-start(bf16[3,256,256]{2,1,0:T(8,128)(2,1)} %fusion.84), channel_id=1, source_target_pairs={{0,16},{1,17},{2,18},{3,19},{4,20},{5,21},{6,22},{7,23},{8,24},{9,... | collective-permute-start | bytes 1179656 | tf_op jit(solution)/shard_map/ppermute | solution.py:476
  655.1 24.5 %collective-permute-start.60 = (bf16[4,256,512]{2,1,0:T(8,128)(2,1)}, bf16[4,256,512]{2,1,0:T(8,128)(2,1)}, u32[]{:S(2)}, u32[]{:S(2)}) collective-permute-start(bf16[4,256,512]{2,1,0:T(8,128)(2,1)} %fusion.4), channel_id=1, source_target_pairs={{0,16},{1,17},{2,18},{3,19},{4,20},{5,21},{6,22},{7,23},{8,24},{9,... | collective-permute-start | bytes 3145736 | tf_op jit(solution)/shard_map/ppermute | solution.py:476
  683.6 23.4 %collective-permute-start.62 = (bf16[256,512]{1,0:T(8,128)(2,1)S(1)}, bf16[256,512]{1,0:T(8,128)(2,1)S(1)}, u32[]{:S(2)}, u32[]{:S(2)}) collective-permute-start(bf16[256,512]{1,0:T(8,128)(2,1)S(1)} %get-tuple-element.160), channel_id=1, source_target_pairs={{0,4},{1,5},{2,6},{3,7},{4,0},{5,1},{6,2},{7,3},{8,12},{9,13},{10,... | collective-permute-start | bytes 786440 | tf_op jit(solution)/shard_map/ppermute | solution.py:476
  685.6 21.4 %collective-permute-start.63 = (bf16[256,512]{1,0:T(8,128)(2,1)S(1)}, bf16[256,512]{1,0:T(8,128)(2,1)S(1)}, u32[]{:S(2)}, u32[]{:S(2)}) collective-permute-start(bf16[256,512]{1,0:T(8,128)(2,1)S(1)} %get-tuple-element.159), channel_id=1, source_target_pairs={{0,2},{1,3},{2,4},{3,5},{4,6},{5,7},{6,0},{7,1},{8,10},{9,11},{10,... | collective-permute-start | bytes 786440 | tf_op jit(solution)/shard_map/ppermute | solution.py:476
  686.3 21.8 %collective-permute-start.55 = (bf16[1,256,256]{2,1,0:T(8,128)(2,1)S(1)}, bf16[1,256,256]{2,1,0:T(8,128)(2,1)S(1)}, u32[]{:S(2)}, u32[]{:S(2)}) collective-permute-start(bf16[1,256,256]{2,1,0:T(8,128)(2,1)S(1)} %fusion.91), channel_id=1, source_target_pairs={{0,16},{1,17},{2,18},{3,19},{4,20},{5,21},{6,22},{7,23},{8,24},{9,... | collective-permute-start | bytes 393224 | tf_op jit(solution)/shard_map/ppermute | solution.py:476
  (158 other events, 1843.9 us)

commit v2 on v1

--- a/solution.py
+++ b/solution.py
@@ -472,6 +472,462 @@
     )(tiles, segq, segk, q, k, v, lse, dmix)
 
 
+MESH = pl.DeviceIdType.MESH
+
+
+def spot():
+    row, col = lax.axis_index("row"), lax.axis_index("col")
+    return row // 2, row % 2, col // 2, col % 2
+
+
+def device(y, k, seq, half):
+    return (2 * y + k, 2 * seq + half)
+
+
+def greet(devices):
+    barrier = pltpu.get_barrier_semaphore()
+    for target in devices:
+        pl.semaphore_signal(barrier, inc=1, device_id=target, device_id_type=MESH)
+    pl.semaphore_wait(barrier, len(devices))
+
+
+def remote(source, target, send_sem, recv_sem, device_id):
+    copy = pltpu.make_async_remote_copy(
+        src_ref=source, dst_ref=target, send_sem=send_sem, recv_sem=recv_sem, device_id=device_id, device_id_type=MESH
+    )
+    copy.start()
+    return copy
+
+
+def lanes(start, size):
+    return pl.ds(pl.multiple_of(start, size), size)
+
+
+def rows_of(place):
+    y, k, seq, half = place
+    return [(dy, dk, (1 - y if dy else y), (1 - k if dk else k)) for dy, dk in ((0, 1), (1, 0), (1, 1))]
+
+
+class Spread:
+    def __init__(self, full_ref, half_sems, core_sems, place, rows):
+        self.full, self.place, self.rows = full_ref, place, rows
+        self.half_sems, self.core_sems = half_sems, core_sems
+        self.first, self.second = {}, {}
+
+    def block(self, n, piece, half, k):
+        return self.full.at[n, half, k, pl.ds(piece * self.rows, self.rows)]
+
+    def start(self, unit, n, piece):
+        y, k, seq, half = self.place
+        mine = self.block(n, piece, half, k)
+        hs, cs = self.half_sems, self.core_sems
+        self.first[unit] = (
+            remote(mine, mine, hs.at[0, unit], hs.at[1, unit], device(y, k, seq, 1 - half)),
+            remote(mine, mine, cs.at[0, unit, 0], cs.at[1, unit, 0], device(y, 1 - k, seq, half)),
+        )
+
+    def forward(self, unit, n, piece):
+        y, k, seq, half = self.place
+        self.first[unit][0].wait_recv()
+        theirs = self.block(n, piece, 1 - half, k)
+        cs = self.core_sems
+        self.second[unit] = remote(theirs, theirs, cs.at[0, unit, 1], cs.at[1, unit, 1], device(y, 1 - k, seq, half))
+
+    def finish(self, unit):
+        self.first[unit][0].wait_send()
+        self.first[unit][1].wait()
+        self.second[unit].wait()
+
+
+class Reduce:
+    def __init__(self, partial_ref, core_buf, half_send, half_buf, core_sems, half_sems, place, rows):
+        self.partial, self.core_buf, self.half_send, self.half_buf = partial_ref, core_buf, half_send, half_buf
+        self.core_sems, self.half_sems, self.place, self.rows = core_sems, half_sems, place, rows
+        self.first, self.second = {}, {}
+
+    def part(self, n, piece, half, k):
+        return (n, half, k, pl.ds(piece * self.rows, self.rows))
+
+    def start(self, unit, n, piece, away):
+        y, k, seq, half = self.place
+        side = 1 - half if away else half
+        cs = self.core_sems
+        lane = 0 if away else 1
+        self.first[unit, lane] = remote(
+            self.partial.at[self.part(n, piece, side, 1 - k)],
+            self.core_buf.at[unit, lane],
+            cs.at[0, unit, lane],
+            cs.at[1, unit, lane],
+            device(y, 1 - k, seq, half),
+        )
+
+    def pass_on(self, unit, n, piece):
+        y, k, seq, half = self.place
+        self.first[unit, 0].wait_recv()
+        away = self.partial[self.part(n, piece, 1 - half, k)].astype(F32) + self.core_buf[unit, 0].astype(F32)
+        self.half_send[unit] = away.astype(BF)
+        hs = self.half_sems
+        self.second[unit] = remote(
+            self.half_send.at[unit], self.half_buf.at[unit], hs.at[0, unit], hs.at[1, unit], device(y, k, seq, 1 - half)
+        )
+
+    def result(self, unit, n, piece):
+        y, k, seq, half = self.place
+        self.first[unit, 1].wait_recv()
+        mine = self.partial[self.part(n, piece, half, k)].astype(F32) + self.core_buf[unit, 1].astype(F32)
+        self.second[unit].wait_recv()
+        return mine + self.half_buf[unit].astype(F32)
+
+    def finish(self, unit):
+        self.first[unit, 0].wait_send()
+        self.first[unit, 1].wait_send()
+        self.second[unit].wait_send()
+
+
+class Return:
+    def __init__(self, own_ref, landing, sems, place, feat):
+        self.own, self.landing, self.sems, self.place, self.feat = own_ref, landing, sems, place, feat
+        self.copies = []
+
+    def start(self, unit, n, value):
+        y, k, seq, half = self.place
+        feat = self.feat
+        self.own[unit] = value
+        self.landing[y, n, k] = jnp.where(k == 0, value[:, :feat], value[:, feat : 2 * feat])
+        for i, (dy, dk, ty, tk) in enumerate(rows_of(self.place)):
+            self.copies.append(
+                remote(
+                    self.own.at[unit, :, lanes(tk * feat + 2 * dy * feat, feat)],
+                    self.landing.at[y, n, k],
+                    self.sems.at[0, unit, i],
+                    self.sems.at[1, unit, i],
+                    device(ty, tk, seq, half),
+                )
+            )
+
+    def finish(self):
+        for copy in self.copies:
+            copy.wait()
+
+
+def normalize(residual):
+    centered = residual - jnp.mean(residual, axis=-1, keepdims=True)
+    inv_std = lax.rsqrt(jnp.mean(centered * centered, axis=-1, keepdims=True) + epsilon)
+    return centered * inv_std, inv_std
+
+
+def normalize_back(out_grad, normed, inv_std, gain):
+    scaled = out_grad * gain
+    first = jnp.mean(scaled, axis=-1, keepdims=True)
+    second = jnp.mean(scaled * normed, axis=-1, keepdims=True)
+    return inv_std * (scaled - first - normed * second)
+
+
+def column_sum(value):
+    return jnp.sum(value, axis=0, keepdims=True)
+
+
+def exchange_kernel(kind, count, pieces, *refs):
+    place = spot()
+    y, k, seq, half = place
+    names = {
+        "forward": ("resid", "norm", "full", "out", "normed", "inv"),
+        "turn": ("resid", "norm", "cot", "full", "output", "grad", "sums", "own", "landing", "return_sems"),
+        "backward": ("resid", "norm", "normed", "inv", "full", "grad", "sums"),
+    }[kind]
+    partial, refs = refs[0], refs[1:]
+    r = dict(zip(names, refs))
+    core_buf, half_send, half_buf, rc, rh, gh, gc = refs[len(names) :]
+    rows = partial.shape[3] // pieces
+    peers = [device(y, 1 - k, seq, half), device(y, k, seq, 1 - half)]
+    if kind == "turn":
+        peers += [device(ty, tk, seq, half) for dy, dk, ty, tk in rows_of(place) if dy]
+    greet(peers)
+    units = [(n * pieces + p, n, p) for n in range(count) for p in range(pieces)]
+    reduce = Reduce(partial, core_buf, half_send, half_buf, rc, rh, place, rows)
+    spread = Spread(r["full"], gh, gc, place, rows)
+    for unit, n, p in units:
+        reduce.start(unit, n, p, True)
+    for unit, n, p in units:
+        reduce.start(unit, n, p, False)
+    if kind != "forward":
+        r["sums"][...] = jnp.zeros_like(r["sums"])
+    if kind == "turn":
+        back = Return(r["own"], r["landing"], r["return_sems"], place, partial.shape[4] // 4)
+    gain, bias = r["norm"][0:1], r["norm"][1:2]
+    for unit, n, p in units:
+        reduce.pass_on(unit, n, p)
+    for unit, n, p in units:
+        here = pl.ds(p * rows, rows)
+        branch = reduce.result(unit, n, p)
+        if kind == "forward":
+            normed, inv = normalize(r["resid"][n, here].astype(F32) + branch)
+            value = normed * gain + bias
+            r["out"][n, here] = value
+            r["normed"][n, here] = normed
+            r["inv"][n, here] = inv
+        elif kind == "turn":
+            normed, inv = normalize(r["resid"][n, here].astype(F32) + branch)
+            upstream = r["cot"][n, here].astype(F32)
+            value = normalize_back(upstream, normed, inv, gain)
+            r["grad"][n, here] = value
+        else:
+            upstream = r["resid"][n, here] + branch if r["resid"].shape[1] == partial.shape[3] else branch
+            normed = r["normed"][n, here]
+            value = normalize_back(upstream, normed, r["inv"][n, here], gain)
+            r["grad"][n, here] = value
+        r["full"][n, half, k, here] = value.astype(BF)
+        spread.start(unit, n, p)
+        if kind != "forward":
+            r["sums"][0:1] += column_sum(upstream * normed)
+            r["sums"][1:2] += column_sum(upstream)
+        if kind == "turn":
+            back.start(unit, n, (normed * gain + bias).astype(BF))
+    for unit, n, p in units:
+        spread.forward(unit, n, p)
+    for unit, n, p in units:
+        spread.finish(unit)
+        reduce.finish(unit)
+    if kind == "turn":
+        back.finish()
+        r["output"][...] = r["landing"][...].astype(F32)
+
+
+def exchange(kind, collective_id, partial, resid, norm, cot=None, normed=None, inv=None):
+    count, _, _, own, depth = partial.shape
+    pieces = 2 if count == 1 else 1
+    units, rows = count * pieces, own // pieces
+    dma = pltpu.SemaphoreType.DMA
+    shape = jax.ShapeDtypeStruct
+    full = shape((count, 2, 2, own, depth), BF)
+    grad, sums = shape((count, own, depth), F32), shape((8, depth), F32)
+    scratch = []
+    if kind == "forward":
+        args = (partial, resid, norm)
+        outs = (full, grad, grad, shape((count, own, 1), F32))
+    elif kind == "turn":
+        args = (partial, resid, norm, cot)
+        outs = (full, shape((2, count, 2, own, depth // 4), F32), grad, sums)
+        scratch = [pltpu.VMEM((units, rows, depth), BF), pltpu.VMEM((2, count, 2, own, depth // 4), BF), dma((2, units, 3))]
+    else:
+        args = (partial, resid, norm, normed, inv)
+        outs = (full, grad, sums)
+    scratch += [
+        pltpu.VMEM((units, 2, rows, depth), BF),
+        pltpu.VMEM((units, rows, depth), BF),
+        pltpu.VMEM((units, rows, depth), BF),
+        dma((2, units, 2)),
+        dma((2, units)),
+        dma((2, units)),
+        dma((2, units, 2)),
+    ]
+    return pl.pallas_call(
+        functools.partial(exchange_kernel, kind, count, pieces),
+        out_shape=outs,
+        in_specs=[pl.BlockSpec(memory_space=pltpu.VMEM)] * len(args),
+        out_specs=tuple(pl.BlockSpec(memory_space=pltpu.VMEM) for _ in outs),
+        scratch_shapes=scratch,
+        compiler_params=pltpu.CompilerParams(collective_id=collective_id, has_side_effects=True, vmem_limit_bytes=50 << 20),
+        name="exchange_" + kind,
+    )(*args)
+
+
+def inputs_kernel(seqs, tok_ref, str_ref, cot_ref, norm_ref, ids_ref, tab_ref, x_own, x_full, y_own, y_full, c_own, norm_all, ids_all, tab_all, in_send, in_recv, self_sems, xh, xc, yh, yc, small_sems, tab_sems, small_self):
+    place = spot()
+    y, k, seq, half = place
+    feat = tok_ref.shape[-1]
+    own = tok_ref.shape[-2]
+    row_peers = rows_of(place)
+    rest = [lax.rem(seq + d, seqs) for d in range(1, seqs)]
+    greet(
+        [device(ty, tk, seq, half) for dy, dk, ty, tk in row_peers]
+        + [device(y, k, seq, 1 - half)]
+        + [device(y, k, s, half) for s in rest]
+    )
+
+    def shuffle(source, target, n, index):
+        copies = [pltpu.make_async_copy(source.at[y, n, k], target.at[n, :, lanes(k * feat, feat)], self_sems.at[index])]
+        copies[0].start()
+        for i, (dy, dk, ty, tk) in enumerate(row_peers):
+            copies.append(
+                remote(
+                    source.at[ty, n, tk],
+                    target.at[n, :, lanes(k * feat + 2 * dy * feat, feat)],
+                    in_send.at[index, i],
+                    in_recv.at[index, i],
+                    device(ty, tk, seq, half),
+                )
+            )
+        return copies
+
+    count = str_ref.shape[1]
+    x_copies = shuffle(tok_ref, x_own, 0, 0)
+    small = []
+    for j, (source, target) in enumerate(((norm_ref, norm_all), (ids_ref, ids_all))):
+        slot = (lambda dy: (slice(None), lanes(k * feat + 2 * dy * feat, feat))) if j == 0 else (lambda dy: (2 * y + k,))
+        copy = pltpu.make_async_copy(source, target.at[slot(0)], small_self.at[j])
+        copy.start()
+        small.append(copy)
+        for i, (dy, dk, ty, tk) in enumerate(row_peers):
+            small.append(
+                remote(source, target.at[slot(dy)], small_sems.at[0, j, i], small_sems.at[1, j, i], device(ty, tk, seq, half))
+            )
+    copy = pltpu.make_async_copy(tab_ref, tab_all.at[0], small_self.at[2])
+    copy.start()
+    small.append(copy)
+    for d in range(1, seqs):
+        small.append(
+            remote(tab_ref, tab_all.at[d], tab_sems.at[0, d - 1], tab_sems.at[1, d - 1], device(y, k, rest[d - 1], half))
+        )
+    for copy in x_copies:
+        copy.wait()
+    x_full[0, half, k] = x_own[0]
+    x_spread = Spread(x_full, xh, xc, place, own)
+    x_spread.start(0, 0, 0)
+    y_copies = [shuffle(str_ref, y_own, n, 1 + n) for n in range(count)]
+    y_spread = Spread(y_full, yh, yc, place, own)
+    x_spread.forward(0, 0, 0)
+    for n in range(count):
+        for copy in y_copies[n]:
+            copy.wait()
+        y_full[n, half, k] = y_own[n]
+        y_spread.start(n, n, 0)
+    c_copies = [shuffle(cot_ref, c_own, n, 1 + count + n) for n in range(count)]
+    for n in range(count):
+        y_spread.forward(n, n, 0)
+    x_spread.finish(0)
+    for n in range(count):
+        y_spread.finish(n)
+        for copy in c_copies[n]:
+            copy.wait()
+    for copy in small:
+        copy.wait()
+
+
+def gather_inputs(seqs, tokens, streams, cotangent, norm, ids, table):
+    count, own, feat = streams.shape[1], streams.shape[-2], streams.shape[-1]
+    depth = 4 * feat
+    dma = pltpu.SemaphoreType.DMA
+    shape = jax.ShapeDtypeStruct
+    outs = (
+        shape((1, own, depth), BF),
+        shape((1, 2, 2, own, depth), BF),
+        shape((count, own, depth), BF),
+        shape((count, 2, 2, own, depth), BF),
+        shape((count, own, depth), BF),
+        shape((norm.shape[0], depth), F32),
+        shape((4,) + ids.shape, jnp.int32),
+        shape((seqs,) + table.shape, F32),
+    )
+    moves = 1 + 2 * count
+    return pl.pallas_call(
+        functools.partial(inputs_kernel, seqs),
+        out_shape=outs,
+        in_specs=[pl.BlockSpec(memory_space=pltpu.VMEM)] * 6,
+        out_specs=tuple(pl.BlockSpec(memory_space=pltpu.VMEM) for _ in outs),
+        scratch_shapes=[
+            dma((moves, 3)),
+            dma((moves, 3)),
+            dma((moves,)),
+            dma((2, 1)),
+            dma((2, 1, 2)),
+            dma((2, count)),
+            dma((2, count, 2)),
+            dma((2, 2, 3)),
+            dma((2, seqs - 1)),
+            dma((3,)),
+        ],
+        compiler_params=pltpu.CompilerParams(collective_id=0, has_side_effects=True, vmem_limit_bytes=50 << 20),
+        name="gather_inputs",
+    )(tokens, streams, cotangent, norm, ids, table)
+
+
+def outputs_kernel(seqs, count, part_x, part_y, d1, d3, small, tok_out, str_out, small_out, core_buf, half_send, half_buf, own, land_x, land_y, rc, rh, rs, small_buf, ss):
+    place = spot()
+    y, k, seq, half = place
+    rows = part_x.shape[3]
+    feat = part_x.shape[4] // 4
+    bits = []
+    while 1 << len(bits) < seqs:
+        bits.append(1 << len(bits))
+    flips = [device(y, k, seq + b - 2 * b * ((seq // b) % 2), half) for b in bits]
+    partners = [device(y, 1 - k, seq, half), device(y, k, seq, 1 - half), device(1 - y, k, seq, half)] + flips
+    greet(partners + [device(1 - y, 1 - k, seq, half)])
+    small_out[...] = small[...]
+
+    def add_small(stage):
+        copy = remote(small_out, small_buf.at[stage], ss.at[0, stage], ss.at[1, stage], partners[stage])
+        copy.wait()
+        small_out[...] += small_buf[stage]
+
+    class Both:
+        def __getitem__(self, index):
+            return part_x[(0,) + index[1:]] if index[0] == 0 else part_y[(index[0] - 1,) + index[1:]]
+
+        @property
+        def at(self):
+            return View()
+
+    class View:
+        def __getitem__(self, index):
+            return part_x.at[(0,) + index[1:]] if index[0] == 0 else part_y.at[(index[0] - 1,) + index[1:]]
+
+    reduce = Reduce(Both(), core_buf, half_send, half_buf, rc, rh, place, rows)
+    units = range(count + 1)
+    for unit in units:
+        reduce.start(unit, unit, 0, True)
+        reduce.start(unit, unit, 0, False)
+    for unit in units:
+        reduce.pass_on(unit, unit, 0)
+    for stage in range(len(partners)):
+        add_small(stage)
+    x_back = Return(own, land_x, rs, place, feat)
+    y_back = Return(own, land_y, rs, place, feat)
+    for unit in units:
+        branch = reduce.result(unit, unit, 0)
+        if unit == 0:
+            x_back.start(unit, 0, (d1[0] + branch).astype(BF))
+        else:
+            y_back.start(unit, unit - 1, (d3[unit - 1] + branch).astype(BF))
+    for unit in units:
+        reduce.finish(unit)
+    x_back.finish()
+    tok_out[...] = land_x[:, 0].astype(F32)
+    y_back.finish()
+    str_out[...] = land_y[...].astype(F32)
+
+
+def scatter_outputs(seqs, collective_id, part_x, part_y, d1, d3, small):
+    count, _, _, own, depth = part_y.shape
+    feat = depth // 4
+    units = count + 1
+    dma = pltpu.SemaphoreType.DMA
+    shape = jax.ShapeDtypeStruct
+    stages = 3 + (seqs - 1).bit_length()
+    outs = (shape((2, 2, own, feat), F32), shape((2, count, 2, own, feat), F32), shape(small.shape, F32))
+    return pl.pallas_call(
+        functools.partial(outputs_kernel, seqs, count),
+        out_shape=outs,
+        in_specs=[pl.BlockSpec(memory_space=pltpu.VMEM)] * 5,
+        out_specs=tuple(pl.BlockSpec(memory_space=pltpu.VMEM) for _ in outs),
+        scratch_shapes=[
+            pltpu.VMEM((units, 2, own, depth), BF),
+            pltpu.VMEM((units, own, depth), BF),
+            pltpu.VMEM((units, own, depth), BF),
+            pltpu.VMEM((units, own, depth), BF),
+            pltpu.VMEM((2, 1, 2, own, feat), BF),
+            pltpu.VMEM((2, count, 2, own, feat), BF),
+            dma((2, units, 2)),
+            dma((2, units)),
+            dma((2, units, 3)),
+            pltpu.VMEM((stages,) + small.shape, F32),
+            dma((2, stages)),
+        ],
+        compiler_params=pltpu.CompilerParams(collective_id=collective_id, has_side_effects=True, vmem_limit_bytes=50 << 20),
+        name="scatter_outputs",
+    )(part_x, part_y, d1, d3, small)
+
+
 def send(value, pairs):
     return lax.ppermute(value, ("row", "col"), pairs)
 
@@ -495,25 +951,6 @@
 
 def in_order(first, mine, other, axis, join=jnp.concatenate):
     return jnp.where(first, join([mine, other], axis=axis), join([other, mine], axis=axis))
-
-
-def layer_norm(residual, gain_vec, bias_vec):
-    centered = residual - jnp.mean(residual, axis=-1, keepdims=True)
-    inv_std = lax.rsqrt(jnp.mean(centered * centered, axis=-1, keepdims=True) + epsilon)
-    normed = centered * inv_std
-    return (normed * gain_vec + bias_vec, normed, inv_std)
-
-
-def layer_norm_back(out_grad, normed, inv_std, gain_vec):
-    scaled = out_grad * gain_vec
-    first = jnp.mean(scaled, axis=-1, keepdims=True)
-    second = jnp.mean(scaled * normed, axis=-1, keepdims=True)
-    lead = tuple(range(out_grad.ndim - 1))
-    return (
-        inv_std * (scaled - first - normed * second),
-        jnp.sum(out_grad * normed, axis=lead),
-        jnp.sum(out_grad, axis=lead),
-    )
 
 
 def dot_f32(spec, left, right):
@@ -548,7 +985,7 @@
     seqs = cols // 2
     row, col = lax.axis_index("row"), lax.axis_index("col")
     y, k, seq, half = row // 2, row % 2, col // 2, col % 2
-    low_core, low_half, low_y = k == 0, half == 0, y == 0
+    low_core, low_y = k == 0, y == 0
     stream_count = streams.shape[1]
     tok = tokens.shape[1]
     own = tok // 2
@@ -558,47 +995,27 @@
     ff = w_up.shape[1] // 2
     table_heads, bucket_count = enc_table.shape
 
-    norm_params = jnp.stack([attention_norm_gain, attn_bias, ffn_gain, ffn_bias, cross_gain, cross_bias])
-    norm_params = lax.all_gather(norm_params, "row", axis=1, tiled=True)
-    norm_params = jnp.where(low_y, norm_params, jnp.roll(norm_params, D // 2, axis=1))
-    gain1, bias1, gain2, bias2, gain3, bias3 = norm_params
-    segment = pick(pick(lax.all_gather(block_ids, "row", axis=1, tiled=True), y, 0), seq, 0)
+    norm_params = jnp.stack([attention_norm_gain, attn_bias, ffn_gain, ffn_bias, cross_gain, cross_bias] + [cross_bias] * 2)
+    table_pack = jnp.zeros((8, 128), F32).at[0].set(jnp.stack([enc_table, cross_table]).reshape(-1))
+    micro_count = tokens.shape[0]
+    x_own, x_full, y_own, y_full, c_own, norm_params, all_ids, all_tables = gather_inputs(
+        seqs,
+        tokens.reshape(micro_count, 1, 2, own, feat),
+        streams.reshape(micro_count, stream_count, 2, own, feat),
+        cotangent.reshape(micro_count, stream_count, 2, own, feat),
+        norm_params,
+        block_ids.reshape(8, -1),
+        table_pack,
+    )
+    x_full, y_full = x_full.reshape(length, D), y_full.reshape(stream_count * length, D)
+    segment = pick(pick(all_ids.reshape(rows, micro_count, length), seq, 0), y, 0)
     segq = segment[None]
     segk = jnp.broadcast_to(segment[:, None], (length, 128))
-    tables = lax.all_gather(jnp.stack([enc_table, cross_table]), "col", axis=0)
+    own_tables = pick(all_tables[:, 0].reshape(seqs, 2, table_heads, bucket_count), k, 2)
     slot_col = 2 * ((seq - jnp.arange(seqs)) % seqs) + half
-    own_tables = pick(jnp.take(tables, slot_col, axis=0), k, 2)
     reversed_ids = jnp.concatenate([jnp.full((1,), -1, jnp.int32), bucket_ids[::-1]])
     onehot = bucket_onehot(reversed_ids, bucket_count)
     offsets = jnp.einsum("htb,bo->tho", own_tables, onehot, precision=highest)[:, :, None, :]
-
-    def relayout(array):
-        count = array.shape[1]
-        both = jnp.concatenate([pick(array, y, 0), send(pick(array, 1 - y, 0), pairs["micro"])], axis=-1)
-        blocks = both.reshape(count, 2, own, 2, 1, feat)
-        other = send(pick(blocks, 1 - k, 1), pairs["core"])
-        return in_order(low_core, pick(blocks, k, 1), other, 3).reshape(count, own, D)
-
-    def relayout_back(array, link_type):
-        count = array.shape[0]
-        blocks = array.reshape(count, own, 2, 2, feat)
-        other = send(pick(blocks, 1 - k, 3), pairs["core"])
-        both = in_order(low_core, pick(blocks, k, 3), other, 1).reshape(count, tok, 2, feat)
-        other = send(both[:, :, 1].astype(link_type), pairs["micro"]).astype(F32)
-        return in_order(low_y, both[:, :, 0], other, 0, jnp.stack)
-
-    def gather_tokens(array):
-        count = array.shape[0]
-        pair = in_order(low_half, array, send(array, pairs["half"]), 1, jnp.stack)
-        return in_order(low_core, pair, send(pair, pairs["core"]), 2, jnp.stack).reshape(count, 2 * tok, D)
-
-    def scatter_tokens(partial):
-        count = partial.shape[0]
-        blocks = partial.reshape(count, 2, 2, own, D)
-        other = send(pick(blocks, 1 - k, 2).astype(BF), pairs["core"])
-        blocks = pick(blocks, k, 2) + other.astype(F32)
-        other = send(pick(blocks, 1 - half, 1).astype(BF), pairs["half"])
-        return pick(blocks, half, 1) + other.astype(F32)
 
     def gather_weights(shards):
         base = in_order(low_core, pick(shards, k, 0), send(pick(shards, 1 - k, 0), pairs["core"]), 1)
@@ -624,62 +1041,58 @@
     halves = lambda weight: weight.reshape(2, -1, feat)
     hd3, hd2 = 3 * head_dim, 2 * head_dim
     first = gather_weights(jnp.concatenate([columns(w_qkv, 3), halves(w_out)], axis=1))
-    x_own = relayout(tokens[:, None])
-    x_full = gather_tokens(x_own)[0]
     up = gather_weights(columns(w_up, 1))
     down = gather_weights(halves(w_down))
     last = gather_weights(jnp.concatenate([columns(w_keyval, 2), columns(w_query, 1), halves(w_cross_out)], axis=1))
-    y_own = relayout(streams)
-    y_full = gather_tokens(y_own).reshape(stream_count * length, D)
-    c_own = relayout(cotangent)
     m_qkv, m_out = first[:, :hd3], first[:, hd3:].reshape(-1, D)
     m_kv, m_q, m_co = last[:, :hd2], last[:, hd2:hd3], last[:, hd3:].reshape(-1, D)
     up, down = up.reshape(-1, D), down.reshape(-1, D)
+    blocked = lambda product: product.astype(BF).reshape(-1, 2, 2, own, D)
 
     qkv = dot_f32("snr,tr->snt", m_qkv, x_full).astype(BF)
     mix, lse, tiles = attention(offsets[0], segq, segk, qkv, qkv, qkv, (0, 1, 2), 1)
     mix_flat = mix.reshape(-1, length)
-    branch = scatter_tokens(dot_f32("et,er->tr", mix_flat, m_out)[None])[0]
-    hidden, normed1, inv1 = layer_norm(x_own[0].astype(F32) + branch, gain1, bias1)
-    hidden_full = gather_tokens(hidden.astype(BF)[None])[0]
+    hidden_full, hidden, normed1, inv1 = exchange(
+        "forward", 1, blocked(dot_f32("et,er->tr", mix_flat, m_out)), x_own, norm_params[0:2]
+    )
+    hidden_full = hidden_full.reshape(length, D)
     pre = dot_f32("fr,tr->ft", up, hidden_full)
     act, gelu_pull = jax.vjp(gelu_exact, pre)
     act = act.astype(BF)
-    branch = scatter_tokens(dot_f32("ft,fr->tr", act, down)[None])[0]
-    encoded, normed2, inv2 = layer_norm(hidden + branch, gain2, bias2)
-    enc_full = gather_tokens(encoded.astype(BF)[None])[0]
+    enc_full, _, normed2, inv2 = exchange(
+        "forward", 2, blocked(dot_f32("ft,fr->tr", act, down)), hidden, norm_params[2:4]
+    )
+    enc_full = enc_full.reshape(length, D)
     kv = dot_f32("snr,tr->snt", m_kv, enc_full).astype(BF)
     query = dot_f32("snr,tr->snt", m_q, y_full).astype(BF)
     cmix, clse, ctiles = attention(offsets[1], segq, segk, query, kv, kv, (0, 0, 1), stream_count)
     cmix_flat = cmix.reshape(-1, stream_count * length)
-    branch = scatter_tokens(dot_f32("et,er->tr", cmix_flat, m_co).reshape(stream_count, length, D))
-    result, normed3, inv3 = layer_norm(y_own.astype(F32) + branch, gain3, bias3)
-    output = relayout_back(result, BF)
-
-    d3, gain3_grad, bias3_grad = layer_norm_back(c_own.astype(F32), normed3, inv3, gain3)
-    d3_full = gather_tokens(d3.astype(BF)).reshape(stream_count * length, D)
+    d3_full, output, d3, sums3 = exchange(
+        "turn", 3, blocked(dot_f32("et,er->tr", cmix_flat, m_co)), y_own, norm_params[4:6], cot=c_own
+    )
+    d3_full = d3_full.reshape(stream_count * length, D)
+
     dcmix = dot_f32("er,tr->et", m_co, d3_full).astype(BF).reshape(cmix.shape)
     g_co = dot_f32("et,tr->er", cmix_flat, d3_full)
     dquery, dkc, dvc, doff_cross = attention_back(
         ctiles, segq, segk, query, kv, kv, (0, 0, 1), clse, dcmix, stream_count
     )
     dkv = jnp.concatenate([dkc, dvc], axis=1)
-    d_enc = scatter_tokens(dot_f32("snt,snr->tr", dkv, m_kv)[None])[0]
-    d2, gain2_grad, bias2_grad = layer_norm_back(d_enc, normed2, inv2, gain2)
-    d2_full = gather_tokens(d2.astype(BF)[None])[0]
+    d2_full, d2, sums2 = exchange(
+        "backward", 4, blocked(dot_f32("snt,snr->tr", dkv, m_kv)), norm_params[2:4][None], norm_params[2:4], normed=normed2, inv=inv2
+    )
+    d2_full = d2_full.reshape(length, D)
     g_q = dot_f32("snt,tr->snr", dquery, y_full)
     g_kv = dot_f32("snt,tr->snr", dkv, enc_full)
-    g_last = scatter_weights(
-        jnp.concatenate([g_kv, g_q, g_co.reshape(seqs, head_dim, D)], axis=1)
-    )
-    dy = scatter_tokens(dot_f32("snt,snr->tr", dquery, m_q).reshape(stream_count, length, D))
-    grad_streams = relayout_back(d3 + dy, BF)
+    g_last = scatter_weights(jnp.concatenate([g_kv, g_q, g_co.reshape(seqs, head_dim, D)], axis=1))
+    part_y = blocked(dot_f32("snt,snr->tr", dquery, m_q))
     dact = dot_f32("fr,tr->ft", down, d2_full)
     dpre = gelu_pull(dact)[0].astype(BF)
     g_down = scatter_weights(dot_f32("ft,tr->fr", act, d2_full).reshape(seqs, ff, D))
-    d_hid = d2 + scatter_tokens(dot_f32("ft,fr->tr", dpre, up)[None])[0]
-    d1, gain1_grad, bias1_grad = layer_norm_back(d_hid, normed1, inv1, gain1)
-    d1_full = gather_tokens(d1.astype(BF)[None])[0]
+    d1_full, d1, sums1 = exchange(
+        "backward", 5, blocked(dot_f32("ft,fr->tr", dpre, up)), d2, norm_params[0:2], normed=normed1, inv=inv1
+    )
+    d1_full = d1_full.reshape(length, D)
     g_up = scatter_weights(dot_f32("ft,tr->fr", dpre, hidden_full).reshape(seqs, ff, D))
     dmix = dot_f32("er,tr->et", m_out, d1_full).astype(BF).reshape(mix.shape)
     g_out = dot_f32("et,tr->er", mix_flat, d1_full)
@@ -687,10 +1100,9 @@
     dqkv = jnp.concatenate([dq, dk, dv], axis=1)
     g_qkv = dot_f32("snt,tr->snr", dqkv, x_full)
     g_first = scatter_weights(jnp.concatenate([g_qkv, g_out.reshape(seqs, head_dim, D)], axis=1))
-    dx = scatter_tokens(dot_f32("snt,snr->tr", dqkv, m_qkv)[None])[0]
-    grad_tokens = relayout_back((d1 + dx)[None], BF)[:, 0]
-
-    norm_grads = jnp.stack([gain1_grad, bias1_grad, gain2_grad, bias2_grad, gain3_grad, bias3_grad])
+    part_x = blocked(dot_f32("snt,snr->tr", dqkv, m_qkv))
+
+    norm_grads = jnp.concatenate([sums1[:2], sums2[:2], sums3[:2]])
     norm_grads = jnp.where(low_y, norm_grads, jnp.roll(norm_grads, D // 2, axis=1))
     table_grads = jnp.einsum(
         "tho,bo->thb", jnp.stack([doff_enc[:, 0], doff_cross[:, 0]]), onehot, precision=highest
@@ -699,7 +1111,9 @@
     spread = (heads[:, None] == jnp.arange(table_heads * cols)[None, :]).astype(F32)
     table_grads = jnp.einsum("thb,hg->tgb", table_grads, spread, precision=highest)
     small = jnp.concatenate([norm_grads.reshape(-1, 128), table_grads.reshape(-1, 128)])
-    small = lax.psum(small, ("row", "col"))
+    grad_tokens, grad_streams, small = scatter_outputs(seqs, 6, part_x, part_y, d1, d3, small)
+    output, grad_streams = output.reshape(streams.shape), grad_streams.reshape(streams.shape)
+    grad_tokens = grad_tokens.reshape(tokens.shape)
     count = norm_grads.size // 128
     norm_sums = lax.dynamic_slice_in_dim(small[:count].reshape(6, D), row * feat, feat, axis=1)
     table_sums = small[count:].reshape(2, table_heads * cols, bucket_count)
@@ -732,7 +1146,7 @@
 
     def run(tokens, *rest):
         micro_count = tokens.shape[0]
-        if whole_row == 2 * micro_count:
+        if whole_row == 4 and micro_count == 2 and half_col % 2 == 0:
             device_fn = functools.partial(on_device, whole_row, half_col)
         else:
             device_fn = on_device_general

time: 721 us -> 579 us (0.80)
  Pallas kernels: 50.9 us -> 267 us
  waiting for transfers between devices: 232 us -> 75.2 us
  blocking collectives: 73.9 us -> 0 us
  other arithmetic: 117 us -> 46 us
  local copies, waits for them, and re-layouts: 114 us -> 62 us
    pallas_call x0 -> x7, Pallas kernels: none -> 216 us  [the longest x5 112 us: exchange(): pl.pallas_call(functools.partial(exchange_kernel, kind, count, pieces), o...]
    ppermute x80 -> x40, waiting for transfers between devices: 232 us -> 75.2 us  [send(): return lax.ppermute(value, ('row', 'col'), pairs)]
    psum x1 -> x0, blocking collectives: 37.2 us -> none  [on_device(): small = lax.psum(small, ('row', 'col'))]
    all_gather x3 -> x0, blocking collectives: 36.7 us -> none  [the longest x1 26.3 us: on_device(): tables = lax.all_gather(jnp.stack([enc_table, cross_table]), 'col', axis=0)]
    select_n x39 -> x12, other arithmetic: 42 us -> 14.8 us  [in_order(): jnp.where(first, join([mine, other], axis=axis), join([other, mine], axis...]
    convert_element_type x20 -> x0, local copies, waits for them, and re-layouts: 18.8 us -> none  [the longest x2 6.06 us: on_device(): c_own.astype(F32)]
    add x11 -> x0, other arithmetic: 17.1 us -> none  [the longest x7 10.1 us: scatter_tokens(): blocks = pick(blocks, k, 2) + other.astype(F32)]
    convert_element_type x10 -> x0, other arithmetic: 15 us -> none  [the longest x1 5.82 us: on_device(): act = act.astype(BF)]
  transfers between devices with their start and end apart: 80 -> 40, of which waited for: 27 -> 11; matrix products, arithmetic and copies ran while one was open for 32% -> 19% of each run, Pallas kernels for 2% -> 29%
where the time goes in v2:
time: 579 us; the launch traced here: 572 us
  Pallas kernels  267 us (46%)
  starting transfers between devices  83.2 us (14%)
  waiting for transfers between devices  75.2 us (13%)
  local copies, waits for them, and re-layouts  62 us (11%)
  other arithmetic  46 us (8%)
  matrix products  36.7 us (6%)
    pallas_call x5, Pallas kernels, exchange(): pl.pallas_call(functools.partial(exchange_kernel, kind, count, pieces), o...  112 us
    ppermute x40, starting transfers between devices, send(): return lax.ppermute(value, ('row', 'col'), pairs)  83.2 us
    ppermute x40, waiting for transfers between devices, send(): return lax.ppermute(value, ('row', 'col'), pairs)  75.2 us
    pallas_call x1, Pallas kernels, scatter_outputs(): pl.pallas_call(functools.partial(outputs_kernel, seqs, count), out_shape=...  62.9 us
    pallas_call x1, Pallas kernels, gather_inputs(): pl.pallas_call(functools.partial(inputs_kernel, seqs), out_shape=outs, in...  40.7 us
    dot_general x21, matrix products, dot_f32(): return jnp.einsum(spec, left, right, preferred_element_type=F32)  36 us
    unnamed x208, local copies, waits for them, and re-layouts  33.1 us
    pallas_call x2, Pallas kernels, attention_back(): pl.pallas_call(functools.partial(bwd_kernel, streams, length, width), gri...  27.9 us
  transfers between devices with their start and end apart: 40, of which 11 were waited for; matrix products, arithmetic and copies ran while one was open for 19% of the time, Pallas kernels for 29%

profile of v2, /device:TPU:0, one launch (start us, length us, event | category | flops | bytes accessed | tf_op | source)
XLA Modules:
  0.0 572.4 jit_solution(11017038403924795222)
XLA Ops:
  7.3 40.7 %gather_inputs.1 = (bf16[1,128,1024]{2,1,0:T(8,128)(2,1)S(1)}, bf16[1,2,2,128,1024]{4,3,2,1,0:T(8,128)(2,1)}, bf16[3,128,1024]{2,1,0:T(8,128)(2,1)S(1)}, bf16[3,...) custom-call(bf16[2,1,2,128,256]{4,3,2,1,0:T(8,128)(2,1)S(1)} %bitcas, ...), custom_call_target="tpu_custom_call" | custom-call | tf_op jit(solution)/shard_map/gather_inputs/pallas_call | solution.py:823
  61.8 4.4 collective-permute-done.11
  66.2 11.2 %collective-permute-done.12 = bf16[256,512]{1,0:T(8,128)(2,1)S(1)} collective-permute-done((bf16[256,512]{1,0:T(8,128)(2,1)}, bf16[256,512]{1,0:T(8,128)(2,1)S(1)}, u32[]{:S(2)}, u32[]{:S(2)}) %collective-permute-start.12) | collective-permute-done | bytes 262176 | tf_op jit(solution)/shard_map/ppermute | solution.py:932
  79.1 9.7 %collective-permute-start.7 = (bf16[256,512]{1,0:T(8,128)(2,1)}, bf16[256,512]{1,0:T(8,128)(2,1)S(1)}, u32[]{:S(2)}, u32[]{:S(2)}) collective-permute-start(bf16[256,512]{1,0:T(8,128)(2,1)} %maximum_select_fusion.7), channel_id=1, source_target_pairs={{0,4},{1,5},{2,6},{3,7},{4,0},{5,1},{6,2},{7,3},{8,12},{9,13},{10,... | collective-permute-start | bytes 786440 | tf_op jit(solution)/shard_map/ppermute | solution.py:932
  88.7 3.3 collective-permute-start.8
  95.8 6.4 %collective-permute-done.7 = bf16[256,512]{1,0:T(8,128)(2,1)S(1)} collective-permute-done((bf16[256,512]{1,0:T(8,128)(2,1)}, bf16[256,512]{1,0:T(8,128)(2,1)S(1)}, u32[]{:S(2)}, u32[]{:S(2)}) %collective-permute-start.7) | collective-permute-done | bytes 262176 | tf_op jit(solution)/shard_map/ppermute | solution.py:932
  102.2 15.9 %collective-permute-start.18 = (bf16[256,512]{1,0:T(8,128)(2,1)S(1)}, bf16[256,512]{1,0:T(8,128)(2,1)S(1)}, u32[]{:S(2)}, u32[]{:S(2)}) collective-permute-start(bf16[256,512]{1,0:T(8,128)(2,1)S(1)} %maximum_select_fusion.11), channel_id=1, source_target_pairs={{0,6},{1,7},{2,0},{3,1},{4,2},{5,3},{6,4},{7,5},{8,14},{9,15},{10,... | collective-permute-start | bytes 786440 | tf_op jit(solution)/shard_map/ppermute | solution.py:932
  118.3 3.7 collective-permute-start.1
  122.0 4.7 collective-permute-start.2
  126.7 8.8 %collective-permute-done.17 = bf16[256,512]{1,0:T(8,128)(2,1)S(1)} collective-permute-done((bf16[256,512]{1,0:T(8,128)(2,1)S(1)}, bf16[256,512]{1,0:T(8,128)(2,1)S(1)}, u32[]{:S(2)}, u32[]{:S(2)}) %collective-permute-start.17) | collective-permute-done | bytes 262176 | tf_op jit(solution)/shard_map/ppermute | solution.py:932
  135.5 2.2 collective-permute-start.3
  142.1 4.6 collective-permute-done.2
  152.5 6.3 %attend.2 = (bf16[4,64,512]{2,1,0:T(8,128)(2,1)S(1)}, f32[4,1,512]{2,1,0:T(1,128)S(1)}, f32[4,896,128]{2,1,0:T(8,128)S(1)}) custom-call(f32[4,1,1024]{2,1,0:T(1,128)S(1)} %get-tuple-element.205.off_ref, s32[1,512]{1,0:T(1,128)S(1)} %fusion.102.segq_ref, s32[512,128]{1,0:T(8,128)S(1)} %broadcast_in_dim.7.segk_ref, ...), custom_call_target="tpu_custom_call" | custom-call | tf_op jit(solution)/shard_map/attend/pallas_call | solution.py:446
  161.1 16.8 %exchange_forward.2 = (bf16[1,2,2,128,1024]{4,3,2,1,0:T(8,128)(2,1)S(1)}, f32[1,128,1024]{2,1,0:T(8,128)S(1)}, f32[1,128,1024]{2,1,0:T(8,128)S(1)}, f32[1,128,1]{2,1,0:T(8,128)S(1)}) custom-call(bf16[1,2,2,128,1024]{4,3,2,1,0:T(8,128)(2,1)S(1)} %bitcast.299, bf16[1,128,1024]{2,1,0:T(8,128)(2,1)S(1)} %copy-done.14, f32[2,1024]{1,0:T(2,128)S(1)} %get-tuple-element.204.refs_2_), custom_call_target="tpu_custom_call" | custom-call | tf_op jit(solution)/shard_map/exchange_forward/pallas_call | solution.py:724
  179.6 7.1 %multiply_convert_fusion = (bf16[1024,512]{1,0:T(8,128)(2,1)S(1)}, f32[1024,512]{1,0:T(8,128)}, f32[1024,512]{1,0:T(8,128)}) fusion(bf16[1024,1024]{1,0:T(8,128)(2,1)S(1)} %bitcast.314, bf16[512,1024]{1,0:T(8,128)(2,1)S(1)} %bitcast.301), kind=kOutput, calls=%fused_computation.27 | convolution fusion | flops 1107820544 | bytes 8388608 | tf_op jit(solution)/shard_map/fr,tr->ft/dot_general | solution.py:957
  190.4 17.6 %exchange_forward.3 = (bf16[1,2,2,128,1024]{4,3,2,1,0:T(8,128)(2,1)S(1)}, f32[1,128,1024]{2,1,0:T(8,128)}, f32[1,128,1024]{2,1,0:T(8,128)S(1)}, f32[1,128,1]{2,1,0:T(8,128)S(1)}) custom-call(bf16[1,2,2,128,1024]{4,3,2,1,0:T(8,128)(2,1)S(1)} %bitcast.293, f32[1,128,1024]{2,1,0:T(8,128)S(1)} %get-tuple-element.80.refs_1_, f32[2,1024]{1,0:T(2,128)S(1)} %get-tuple-element.203.refs_2_), custom_call_target="tpu_custom_call" | custom-call | tf_op jit(solution)/shard_map/exchange_forward/pallas_call | solution.py:724
  212.7 17.1 %attend.3 = (bf16[4,64,1536]{2,1,0:T(8,128)(2,1)S(1)}, f32[4,1,1536]{2,1,0:T(1,128)S(1)}, f32[4,896,128]{2,1,0:T(8,128)S(1)}) custom-call(f32[4,1,1024]{2,1,0:T(1,128)S(1)} %get-tuple-element.206.off_ref, s32[1,512]{1,0:T(1,128)S(1)} %fusion.102.segq_ref, s32[512,128]{1,0:T(8,128)S(1)} %broadcast_in_dim.7.segk_ref, ...), custom_call_target="tpu_custom_call" | custom-call | tf_op jit(solution)/shard_map/attend/pallas_call | solution.py:446
  229.8 2.7 bitcast_convert_fusion.1
  232.6 44.3 %exchange_turn.1 = (bf16[3,2,2,128,1024]{4,3,2,1,0:T(8,128)(2,1)}, f32[2,3,2,128,256]{4,3,2,1,0:T(8,128)S(1)}, f32[3,128,1024]{2,1,0:T(8,128)}, f32[8,1024]{1,0:T(8,128)S(1)}) custom-call(bf16[3,2,2,128,1024]{4,3,2,1,0:T(8,128)(2,1)} %bitcast.320, bf16[3,128,1024]{2,1,0:T(8,128)(2,1)S(1)} %get-tuple-element.83.refs_1_, ...), custom_call_target="tpu_custom_call" | custom-call | tf_op jit(solution)/shard_map/exchange_turn/pallas_call | solution.py:724
  276.8 2.9 convolution_convert_fusion
  279.7 20.2 %attend_back.2 = (bf16[4,64,1536]{2,1,0:T(8,128)(2,1)S(1)}, bf16[4,64,512]{2,1,0:T(8,128)(2,1)S(1)}, bf16[4,64,512]{2,1,0:T(8,128)(2,1)S(1)}, f32[4,1,1024]{2,1,0:T(1,128)S(1)}) custom-call(f32[4,896,128]{2,1,0:T(8,128)S(1)} %get-tuple-element.88.t_ref, s32[1,512]{1,0:T(1,128)S(1)} %fusion.102.segq_ref, s32[512,128]{1,0:T(8,128)S(1)} %broadcast_in_dim.7.segk_ref, ...), custom_call_target="tpu_custom_call" | custom-call | tf_op jit(solution)/shard_map/attend_back/pallas_call | solution.py:461
  302.0 2.1 fusion.60
  304.1 16.7 %exchange_backward.2 = (bf16[1,2,2,128,1024]{4,3,2,1,0:T(8,128)(2,1)S(1)}, f32[1,128,1024]{2,1,0:T(8,128)S(1)}, f32[8,1024]{1,0:T(8,128)S(1)}) custom-call(bf16[1,2,2,128,1024]{4,3,2,1,0:T(8,128)(2,1)S(1)} %bitcast.300, f32[1,2,1024]{2,1,0:T(2,128)S(1)} %get-tuple-element.201.refs_1_, f32[2,1024]{1,0:T(2,128)S(1)} %get-tuple-element.203.refs_2_, ...), custom_call_target="tpu_custom_call" | custom-call | tf_op jit(solution)/shard_map/exchange_backward/pallas_call | solution.py:724
  336.8 16.7 %exchange_backward.3 = (bf16[1,2,2,128,1024]{4,3,2,1,0:T(8,128)(2,1)S(1)}, f32[1,128,1024]{2,1,0:T(8,128)S(1)}, f32[8,1024]{1,0:T(8,128)S(1)}) custom-call(bf16[1,2,2,128,1024]{4,3,2,1,0:T(8,128)(2,1)S(1)} %bitcast.292, f32[1,128,1024]{2,1,0:T(8,128)S(1)} %get-tuple-element.96.refs_1_, f32[2,1024]{1,0:T(2,128)S(1)} %get-tuple-element.204.refs_2_, ...), custom_call_target="tpu_custom_call" | custom-call | tf_op jit(solution)/shard_map/exchange_backward/pallas_call | solution.py:724
  354.6 7.7 %attend_back.3 = (bf16[4,64,512]{2,1,0:T(8,128)(2,1)S(1)}, bf16[4,64,512]{2,1,0:T(8,128)(2,1)S(1)}, bf16[4,64,512]{2,1,0:T(8,128)(2,1)S(1)}, f32[4,1,1024]{2,1,0:T(1,128)S(1)}) custom-call(f32[4,896,128]{2,1,0:T(8,128)S(1)} %get-tuple-element.86.t_ref, s32[1,512]{1,0:T(1,128)S(1)} %fusion.102.segq_ref, s32[512,128]{1,0:T(8,128)S(1)} %broadcast_in_dim.7.segk_ref, ...), custom_call_target="tpu_custom_call" | custom-call | tf_op jit(solution)/shard_map/attend_back/pallas_call | solution.py:461
  370.5 2.5 bitcast_convert_fusion.2
  373.0 2.7 bitcast_convert_fusion
  375.7 62.9 %scatter_outputs.1 = (f32[2,2,128,256]{3,2,1,0:T(8,128)S(1)}, f32[2,3,2,128,256]{4,3,2,1,0:T(8,128)S(1)}, f32[56,128]{1,0:T(8,128)S(1)}) custom-call(bf16[1,2,2,128,1024]{4,3,2,1,0:T(8,128)(2,1)S(1)} %bitcast.305, bf16[3,2,2,128,1024]{4,3,2,1,0:T(8,128)(2,1)} %bitcast.321, f32[1,128,1024]{2,1,0:T(8,128)S(1)} %copy-done.11, ...), custom_call_target="tpu_custom_call" | custom-call | tf_op jit(solution)/shard_map/scatter_outputs/pallas_call | solution.py:908
  439.5 2.6 fusion.48
  446.2 3.6 collective-permute-start.36
  449.7 3.0 fusion.50
  453.5 3.0 fusion.49
  458.3 4.5 collective-permute-start.38
  462.8 16.3 %collective-permute-done.32 = bf16[256,512]{1,0:T(8,128)(2,1)S(1)} collective-permute-done((bf16[256,512]{1,0:T(8,128)(2,1)S(1)}, bf16[256,512]{1,0:T(8,128)(2,1)S(1)}, u32[]{:S(2)}, u32[]{:S(2)}) %collective-permute-start.32) | collective-permute-done | bytes 262176 | tf_op jit(solution)/shard_map/ppermute | solution.py:932
  481.4 15.1 %collective-permute-start.23 = (bf16[256,512]{1,0:T(8,128)(2,1)}, bf16[256,512]{1,0:T(8,128)(2,1)}, u32[]{:S(2)}, u32[]{:S(2)}) collective-permute-start(bf16[256,512]{1,0:T(8,128)(2,1)} %get-tuple-element.172), channel_id=1, source_target_pairs={{0,2},{1,3},{2,4},{3,5},{4,6},{5,7},{6,0},{7,1},{8,10},{9,11},{10,... | collective-permute-start | bytes 786440 | tf_op jit(solution)/shard_map/ppermute | solution.py:932
  496.5 5.1 collective-permute-done.37
  503.7 2.2 reshape.599
  505.9 2.2 reshape.600
  508.0 3.5 constant_dynamic-slice_fusion.3
  513.3 10.9 %collective-permute-done.22 = bf16[256,512]{1,0:T(8,128)(2,1)} collective-permute-done((bf16[256,512]{1,0:T(8,128)(2,1)}, bf16[256,512]{1,0:T(8,128)(2,1)}, u32[]{:S(2)}, u32[]{:S(2)}) %collective-permute-start.22) | collective-permute-done | bytes 262176 | tf_op jit(solution)/shard_map/ppermute | solution.py:932
  524.1 2.2 fusion.24
  526.3 2.2 reshape.592
  528.5 6.5 %collective-permute-done.27 = bf16[256,512]{1,0:T(8,128)(2,1)} collective-permute-done((bf16[256,512]{1,0:T(8,128)(2,1)}, bf16[256,512]{1,0:T(8,128)(2,1)}, u32[]{:S(2)}, u32[]{:S(2)}) %collective-permute-start.27) | collective-permute-done | bytes 262176 | tf_op jit(solution)/shard_map/ppermute | solution.py:932
  535.0 2.2 fusion.21
  537.2 2.2 reshape.598
  539.4 3.4 constant_dynamic-slice_fusion.7
  560.2 2.0 maximum_select_fusion.1
  566.9 2.1 maximum_select_fusion.2
  (366 shorter events, 113.7 us)
Async XLA Ops:
  2.1 46.9 %copy-start.79 = (s32[1023]{0:T(1024)S(1)}, s32[1023]{0:T(1024)}, u32[]{:S(2)}) copy-start(s32[1023]{0:T(1024)} %param.26) | copy-start | bytes 12280
  3.6 49.4 %collective-permute-start.10 = (bf16[256,256]{1,0:T(8,128)(2,1)}, bf16[256,256]{1,0:T(8,128)(2,1)}, u32[]{:S(2)}, u32[]{:S(2)}) collective-permute-start(bf16[256,256]{1,0:T(8,128)(2,1)} %get-tuple-element.187), channel_id=1, source_target_pairs={{0,8},{1,9},{2,10},{3,11},{4,12},{5,13},{6,14},{7,15},{8,0},{9,1},... | collective-permute-start | bytes 393224 | tf_op jit(solution)/shard_map/ppermute | solution.py:932
  5.9 53.9 %collective-permute-start.5 = (bf16[256,256]{1,0:T(8,128)(2,1)}, bf16[256,256]{1,0:T(8,128)(2,1)}, u32[]{:S(2)}, u32[]{:S(2)}) collective-permute-start(bf16[256,256]{1,0:T(8,128)(2,1)} %get-tuple-element.189), channel_id=1, source_target_pairs={{0,8},{1,9},{2,10},{3,11},{4,12},{5,13},{6,14},{7,15},{8,0},{9,1},... | collective-permute-start | bytes 393224 | tf_op jit(solution)/shard_map/ppermute | solution.py:932
  6.7 82.1 %collective-permute-start.15 = (bf16[256,256]{1,0:T(8,128)(2,1)}, bf16[256,256]{1,0:T(8,128)(2,1)}, u32[]{:S(2)}, u32[]{:S(2)}) collective-permute-start(bf16[256,256]{1,0:T(8,128)(2,1)} %get-tuple-element.185), channel_id=1, source_target_pairs={{0,8},{1,9},{2,10},{3,11},{4,12},{5,13},{6,14},{7,15},{8,0},{9,1},... | collective-permute-start | bytes 393224 | tf_op jit(solution)/shard_map/ppermute | solution.py:932
  48.8 29.7 %copy-start.2 = (bf16[3,128,1024]{2,1,0:T(8,128)(2,1)}, bf16[3,128,1024]{2,1,0:T(8,128)(2,1)S(1)}, u32[]{:S(2)}) copy-start(bf16[3,128,1024]{2,1,0:T(8,128)(2,1)S(1)} %get-tuple-element.84.refs_3_) | copy-start | bytes 2359300
  52.3 39.7 %copy-start.58 = (bf16[1,256,256]{2,1,0:T(8,128)(2,1)S(1)}, bf16[1,256,256]{2,1,0:T(8,128)(2,1)}, u32[]{:S(2)}) copy-start(bf16[1,256,256]{2,1,0:T(8,128)(2,1)} %get-tuple-element.184) | copy-start | bytes 393220
  54.9 11.3 %collective-permute-start.11 = (bf16[256,512]{1,0:T(8,128)(2,1)}, bf16[256,512]{1,0:T(8,128)(2,1)S(1)}, u32[]{:S(2)}, u32[]{:S(2)}) collective-permute-start(bf16[256,512]{1,0:T(8,128)(2,1)} %maximum_select_fusion.9), channel_id=1, source_target_pairs={{0,2},{1,3},{2,4},{3,5},{4,6},{5,7},{6,0},{7,1},{8,10},{9,11},{10,... | collective-permute-start | bytes 786440 | tf_op jit(solution)/shard_map/ppermute | solution.py:932
  55.5 21.9 %collective-permute-start.12 = (bf16[256,512]{1,0:T(8,128)(2,1)}, bf16[256,512]{1,0:T(8,128)(2,1)S(1)}, u32[]{:S(2)}, u32[]{:S(2)}) collective-permute-start(bf16[256,512]{1,0:T(8,128)(2,1)} %maximum_select_fusion.9), channel_id=1, source_target_pairs={{0,4},{1,5},{2,6},{3,7},{4,0},{5,1},{6,2},{7,3},{8,12},{9,13},{10,... | collective-permute-start | bytes 786440 | tf_op jit(solution)/shard_map/ppermute | solution.py:932
  56.9 20.5 %collective-permute-start.13 = (bf16[256,512]{1,0:T(8,128)(2,1)}, bf16[256,512]{1,0:T(8,128)(2,1)S(1)}, u32[]{:S(2)}, u32[]{:S(2)}) collective-permute-start(bf16[256,512]{1,0:T(8,128)(2,1)} %maximum_select_fusion.9), channel_id=1, source_target_pairs={{0,6},{1,7},{2,0},{3,1},{4,2},{5,3},{6,4},{7,5},{8,14},{9,15},{10,... | collective-permute-start | bytes 786440 | tf_op jit(solution)/shard_map/ppermute | solution.py:932
  58.7 36.0 %copy-start.74 = (bf16[1,256,256]{2,1,0:T(8,128)(2,1)S(1)}, bf16[1,256,256]{2,1,0:T(8,128)(2,1)}, u32[]{:S(2)}) copy-start(bf16[1,256,256]{2,1,0:T(8,128)(2,1)} %get-tuple-element.188) | copy-start | bytes 393220
  59.8 34.3 %collective-permute-start = (bf16[256,256]{1,0:T(8,128)(2,1)}, bf16[256,256]{1,0:T(8,128)(2,1)S(1)}, u32[]{:S(2)}, u32[]{:S(2)}) collective-permute-start(bf16[256,256]{1,0:T(8,128)(2,1)} %get-tuple-element.192), channel_id=1, source_target_pairs={{0,8},{1,9},{2,10},{3,11},{4,12},{5,13},{6,14},{7,15},{8,0},{9,1},... | collective-permute-start | bytes 393224 | tf_op jit(solution)/shard_map/ppermute | solution.py:932
  66.2 52.0 %copy-start.38 = (bf16[256,512]{1,0:T(8,128)(2,1)}, bf16[256,512]{1,0:T(8,128)(2,1)S(1)}, u32[]{:S(2)}) copy-start(bf16[256,512]{1,0:T(8,128)(2,1)S(1)} %collective-permute-done.11) | copy-start | bytes 786436
  66.2 28.0 %collective-permute-start.6 = (bf16[256,512]{1,0:T(8,128)(2,1)}, bf16[256,512]{1,0:T(8,128)(2,1)}, u32[]{:S(2)}, u32[]{:S(2)}) collective-permute-start(bf16[256,512]{1,0:T(8,128)(2,1)} %maximum_select_fusion.7), channel_id=1, source_target_pairs={{0,2},{1,3},{2,4},{3,5},{4,6},{5,7},{6,0},{7,1},{8,10},{9,11},{10,... | collective-permute-start | bytes 786440 | tf_op jit(solution)/shard_map/ppermute | solution.py:932
  77.4 40.8 %copy-start.40 = (bf16[256,512]{1,0:T(8,128)(2,1)}, bf16[256,512]{1,0:T(8,128)(2,1)S(1)}, u32[]{:S(2)}) copy-start(bf16[256,512]{1,0:T(8,128)(2,1)S(1)} %collective-permute-done.12) | copy-start | bytes 786436
  77.4 40.8 %copy-start.42 = (bf16[256,512]{1,0:T(8,128)(2,1)}, bf16[256,512]{1,0:T(8,128)(2,1)S(1)}, u32[]{:S(2)}) copy-start(bf16[256,512]{1,0:T(8,128)(2,1)S(1)} %collective-permute-done.13) | copy-start | bytes 786436
  78.5 71.0 %collective-permute-start.14 = (bf16[4,256,512]{2,1,0:T(8,128)(2,1)}, bf16[4,256,512]{2,1,0:T(8,128)(2,1)}, u32[]{:S(2)}, u32[]{:S(2)}) collective-permute-start(bf16[4,256,512]{2,1,0:T(8,128)(2,1)} %pad_maximum_fusion.8), channel_id=1, source_target_pairs={{0,16},{1,17},{2,18},{3,19},{4,20},{5,21},{6,22},{7,23},{8,24},{9,... | collective-permute-start | bytes 3145736 | tf_op jit(solution)/shard_map/ppermute | solution.py:932
  79.1 23.1 %collective-permute-start.7 = (bf16[256,512]{1,0:T(8,128)(2,1)}, bf16[256,512]{1,0:T(8,128)(2,1)S(1)}, u32[]{:S(2)}, u32[]{:S(2)}) collective-permute-start(bf16[256,512]{1,0:T(8,128)(2,1)} %maximum_select_fusion.7), channel_id=1, source_target_pairs={{0,4},{1,5},{2,6},{3,7},{4,0},{5,1},{6,2},{7,3},{8,12},{9,13},{10,... | collective-permute-start | bytes 786440 | tf_op jit(solution)/shard_map/ppermute | solution.py:932
  88.7 29.6 %collective-permute-start.8 = (bf16[256,512]{1,0:T(8,128)(2,1)}, bf16[256,512]{1,0:T(8,128)(2,1)S(1)}, u32[]{:S(2)}, u32[]{:S(2)}) collective-permute-start(bf16[256,512]{1,0:T(8,128)(2,1)} %maximum_select_fusion.7), channel_id=1, source_target_pairs={{0,6},{1,7},{2,0},{3,1},{4,2},{5,3},{6,4},{7,5},{8,14},{9,15},{10,... | collective-permute-start | bytes 786440 | tf_op jit(solution)/shard_map/ppermute | solution.py:932
  94.1 27.9 %collective-permute-start.16 = (bf16[256,512]{1,0:T(8,128)(2,1)S(1)}, bf16[256,512]{1,0:T(8,128)(2,1)S(1)}, u32[]{:S(2)}, u32[]{:S(2)}) collective-permute-start(bf16[256,512]{1,0:T(8,128)(2,1)S(1)} %maximum_select_fusion.11), channel_id=1, source_target_pairs={{0,2},{1,3},{2,4},{3,5},{4,6},{5,7},{6,0},{7,1},{8,10},{9,11},{10,... | collective-permute-start | bytes 786440 | tf_op jit(solution)/shard_map/ppermute | solution.py:932
  94.2 41.3 %collective-permute-start.17 = (bf16[256,512]{1,0:T(8,128)(2,1)S(1)}, bf16[256,512]{1,0:T(8,128)(2,1)S(1)}, u32[]{:S(2)}, u32[]{:S(2)}) collective-permute-start(bf16[256,512]{1,0:T(8,128)(2,1)S(1)} %maximum_select_fusion.11), channel_id=1, source_target_pairs={{0,4},{1,5},{2,6},{3,7},{4,0},{5,1},{6,2},{7,3},{8,12},{9,13},{10,... | collective-permute-start | bytes 786440 | tf_op jit(solution)/shard_map/ppermute | solution.py:932
  102.2 39.3 %copy-start.62 = (bf16[256,512]{1,0:T(8,128)(2,1)}, bf16[256,512]{1,0:T(8,128)(2,1)S(1)}, u32[]{:S(2)}) copy-start(bf16[256,512]{1,0:T(8,128)(2,1)S(1)} %collective-permute-done.7) | copy-start | bytes 786436
  102.2 36.6 %collective-permute-start.18 = (bf16[256,512]{1,0:T(8,128)(2,1)S(1)}, bf16[256,512]{1,0:T(8,128)(2,1)S(1)}, u32[]{:S(2)}, u32[]{:S(2)}) collective-permute-start(bf16[256,512]{1,0:T(8,128)(2,1)S(1)} %maximum_select_fusion.11), channel_id=1, source_target_pairs={{0,6},{1,7},{2,0},{3,1},{4,2},{5,3},{6,4},{7,5},{8,14},{9,15},{10,... | collective-permute-start | bytes 786440 | tf_op jit(solution)/shard_map/ppermute | solution.py:932
  118.3 23.2 %collective-permute-start.1 = (bf16[256,512]{1,0:T(8,128)(2,1)S(1)}, bf16[256,512]{1,0:T(8,128)(2,1)S(1)}, u32[]{:S(2)}, u32[]{:S(2)}) collective-permute-start(bf16[256,512]{1,0:T(8,128)(2,1)S(1)} %maximum_select_fusion.5), channel_id=1, source_target_pairs={{0,2},{1,3},{2,4},{3,5},{4,6},{5,7},{6,0},{7,1},{8,10},{9,11},{10,... | collective-permute-start | bytes 786440 | tf_op jit(solution)/shard_map/ppermute | solution.py:932
  122.0 24.8 %collective-permute-start.2 = (bf16[256,512]{1,0:T(8,128)(2,1)S(1)}, bf16[256,512]{1,0:T(8,128)(2,1)S(1)}, u32[]{:S(2)}, u32[]{:S(2)}) collective-permute-start(bf16[256,512]{1,0:T(8,128)(2,1)S(1)} %maximum_select_fusion.5), channel_id=1, source_target_pairs={{0,4},{1,5},{2,6},{3,7},{4,0},{5,1},{6,2},{7,3},{8,12},{9,13},{10,... | collective-permute-start | bytes 786440 | tf_op jit(solution)/shard_map/ppermute | solution.py:932
  135.5 11.4 %collective-permute-start.3 = (bf16[256,512]{1,0:T(8,128)(2,1)S(1)}, bf16[256,512]{1,0:T(8,128)(2,1)S(1)}, u32[]{:S(2)}, u32[]{:S(2)}) collective-permute-start(bf16[256,512]{1,0:T(8,128)(2,1)S(1)} %maximum_select_fusion.5), channel_id=1, source_target_pairs={{0,6},{1,7},{2,0},{3,1},{4,2},{5,3},{6,4},{7,5},{8,14},{9,15},{10,... | collective-permute-start | bytes 786440 | tf_op jit(solution)/shard_map/ppermute | solution.py:932
  138.8 39.1 %collective-permute-start.9 = (bf16[4,256,512]{2,1,0:T(8,128)(2,1)S(1)}, bf16[4,256,512]{2,1,0:T(8,128)(2,1)}, u32[]{:S(2)}, u32[]{:S(2)}) collective-permute-start(bf16[4,256,512]{2,1,0:T(8,128)(2,1)S(1)} %pad_maximum_fusion.7), channel_id=1, source_target_pairs={{0,16},{1,17},{2,18},{3,19},{4,20},{5,21},{6,22},{7,23},{8,24},{9,... | collective-permute-start | bytes 3145736 | tf_op jit(solution)/shard_map/ppermute | solution.py:932
  141.5 46.0 %collective-permute-start.19 = (bf16[4,256,512]{2,1,0:T(8,128)(2,1)}, bf16[4,256,512]{2,1,0:T(8,128)(2,1)}, u32[]{:S(2)}, u32[]{:S(2)}) collective-permute-start(bf16[4,256,512]{2,1,0:T(8,128)(2,1)} %pad_maximum_fusion.9), channel_id=1, source_target_pairs={{0,16},{1,17},{2,18},{3,19},{4,20},{5,21},{6,22},{7,23},{8,24},{9,... | collective-permute-start | bytes 3145736 | tf_op jit(solution)/shard_map/ppermute | solution.py:932
  148.0 60.0 %collective-permute-start.4 = (bf16[4,256,512]{2,1,0:T(8,128)(2,1)}, bf16[4,256,512]{2,1,0:T(8,128)(2,1)S(1)}, u32[]{:S(2)}, u32[]{:S(2)}) collective-permute-start(bf16[4,256,512]{2,1,0:T(8,128)(2,1)} %pad_maximum_fusion.6), channel_id=1, source_target_pairs={{0,16},{1,17},{2,18},{3,19},{4,20},{5,21},{6,22},{7,23},{8,24},{9,... | collective-permute-start | bytes 3145736 | tf_op jit(solution)/shard_map/ppermute | solution.py:932
  323.3 116.2 %collective-permute-start.30 = (bf16[4,256,512]{2,1,0:T(8,128)(2,1)}, bf16[4,256,512]{2,1,0:T(8,128)(2,1)}, u32[]{:S(2)}, u32[]{:S(2)}) collective-permute-start(bf16[4,256,512]{2,1,0:T(8,128)(2,1)} %slice.348), channel_id=1, source_target_pairs={{0,16},{1,17},{2,18},{3,19},{4,20},{5,21},{6,22},{7,23},{8,24},{9,... | collective-permute-start | bytes 3145736 | tf_op jit(solution)/shard_map/ppermute | solution.py:932
  329.5 114.4 %collective-permute-start.35 = (bf16[4,256,512]{2,1,0:T(8,128)(2,1)}, bf16[4,256,512]{2,1,0:T(8,128)(2,1)}, u32[]{:S(2)}, u32[]{:S(2)}) collective-permute-start(bf16[4,256,512]{2,1,0:T(8,128)(2,1)} %slice.347), channel_id=1, source_target_pairs={{0,16},{1,17},{2,18},{3,19},{4,20},{5,21},{6,22},{7,23},{8,24},{9,... | collective-permute-start | bytes 3145736 | tf_op jit(solution)/shard_map/ppermute | solution.py:932
  365.3 80.8 %collective-permute-start.20 = (bf16[4,256,512]{2,1,0:T(8,128)(2,1)}, bf16[4,256,512]{2,1,0:T(8,128)(2,1)}, u32[]{:S(2)}, u32[]{:S(2)}) collective-permute-start(bf16[4,256,512]{2,1,0:T(8,128)(2,1)} %fusion.3), channel_id=1, source_target_pairs={{0,16},{1,17},{2,18},{3,19},{4,20},{5,21},{6,22},{7,23},{8,24},{9,... | collective-permute-start | bytes 3145736 | tf_op jit(solution)/shard_map/ppermute | solution.py:932
  368.7 84.1 %collective-permute-start.25 = (bf16[4,256,512]{2,1,0:T(8,128)(2,1)}, bf16[4,256,512]{2,1,0:T(8,128)(2,1)}, u32[]{:S(2)}, u32[]{:S(2)}) collective-permute-start(bf16[4,256,512]{2,1,0:T(8,128)(2,1)} %slice.349), channel_id=1, source_target_pairs={{0,16},{1,17},{2,18},{3,19},{4,20},{5,21},{6,22},{7,23},{8,24},{9,... | collective-permute-start | bytes 3145736 | tf_op jit(solution)/shard_map/ppermute | solution.py:932
  442.1 16.2 %collective-permute-start.31 = (bf16[256,512]{1,0:T(8,128)(2,1)S(1)}, bf16[256,512]{1,0:T(8,128)(2,1)S(1)}, u32[]{:S(2)}, u32[]{:S(2)}) collective-permute-start(bf16[256,512]{1,0:T(8,128)(2,1)S(1)} %get-tuple-element.165), channel_id=1, source_target_pairs={{0,6},{1,7},{2,0},{3,1},{4,2},{5,3},{6,4},{7,5},{8,14},{9,15},{10,... | collective-permute-start | bytes 786440 | tf_op jit(solution)/shard_map/ppermute | solution.py:932
  442.2 36.9 %collective-permute-start.32 = (bf16[256,512]{1,0:T(8,128)(2,1)S(1)}, bf16[256,512]{1,0:T(8,128)(2,1)S(1)}, u32[]{:S(2)}, u32[]{:S(2)}) collective-permute-start(bf16[256,512]{1,0:T(8,128)(2,1)S(1)} %get-tuple-element.167), channel_id=1, source_target_pairs={{0,4},{1,5},{2,6},{3,7},{4,0},{5,1},{6,2},{7,3},{8,12},{9,13},{10,... | collective-permute-start | bytes 786440 | tf_op jit(solution)/shard_map/ppermute | solution.py:932
  443.9 35.2 %collective-permute-start.33 = (bf16[256,512]{1,0:T(8,128)(2,1)S(1)}, bf16[256,512]{1,0:T(8,128)(2,1)S(1)}, u32[]{:S(2)}, u32[]{:S(2)}) collective-permute-start(bf16[256,512]{1,0:T(8,128)(2,1)S(1)} %get-tuple-element.166), channel_id=1, source_target_pairs={{0,2},{1,3},{2,4},{3,5},{4,6},{5,7},{6,0},{7,1},{8,10},{9,11},{10,... | collective-permute-start | bytes 786440 | tf_op jit(solution)/shard_map/ppermute | solution.py:932
  446.2 35.2 %collective-permute-start.36 = (bf16[256,512]{1,0:T(8,128)(2,1)S(1)}, bf16[256,512]{1,0:T(8,128)(2,1)S(1)}, u32[]{:S(2)}, u32[]{:S(2)}) collective-permute-start(bf16[256,512]{1,0:T(8,128)(2,1)S(1)} %get-tuple-element.162), channel_id=1, source_target_pairs={{0,6},{1,7},{2,0},{3,1},{4,2},{5,3},{6,4},{7,5},{8,14},{9,15},{10,... | collective-permute-start | bytes 786440 | tf_op jit(solution)/shard_map/ppermute | solution.py:932
  452.8 48.8 %collective-permute-start.37 = (bf16[256,512]{1,0:T(8,128)(2,1)S(1)}, bf16[256,512]{1,0:T(8,128)(2,1)S(1)}, u32[]{:S(2)}, u32[]{:S(2)}) collective-permute-start(bf16[256,512]{1,0:T(8,128)(2,1)S(1)} %get-tuple-element.164), channel_id=1, source_target_pairs={{0,4},{1,5},{2,6},{3,7},{4,0},{5,1},{6,2},{7,3},{8,12},{9,13},{10,... | collective-permute-start | bytes 786440 | tf_op jit(solution)/shard_map/ppermute | solution.py:932
  458.3 43.3 %collective-permute-start.38 = (bf16[256,512]{1,0:T(8,128)(2,1)S(1)}, bf16[256,512]{1,0:T(8,128)(2,1)S(1)}, u32[]{:S(2)}, u32[]{:S(2)}) collective-permute-start(bf16[256,512]{1,0:T(8,128)(2,1)S(1)} %get-tuple-element.163), channel_id=1, source_target_pairs={{0,2},{1,3},{2,4},{3,5},{4,6},{5,7},{6,0},{7,1},{8,10},{9,11},{10,... | collective-permute-start | bytes 786440 | tf_op jit(solution)/shard_map/ppermute | solution.py:932
  479.1 33.2 %collective-permute-start.21 = (bf16[256,512]{1,0:T(8,128)(2,1)}, bf16[256,512]{1,0:T(8,128)(2,1)}, u32[]{:S(2)}, u32[]{:S(2)}) collective-permute-start(bf16[256,512]{1,0:T(8,128)(2,1)} %get-tuple-element.171), channel_id=1, source_target_pairs={{0,6},{1,7},{2,0},{3,1},{4,2},{5,3},{6,4},{7,5},{8,14},{9,15},{10,... | collective-permute-start | bytes 786440 | tf_op jit(solution)/shard_map/ppermute | solution.py:932
  479.1 45.0 %collective-permute-start.22 = (bf16[256,512]{1,0:T(8,128)(2,1)}, bf16[256,512]{1,0:T(8,128)(2,1)}, u32[]{:S(2)}, u32[]{:S(2)}) collective-permute-start(bf16[256,512]{1,0:T(8,128)(2,1)} %get-tuple-element.173), channel_id=1, source_target_pairs={{0,4},{1,5},{2,6},{3,7},{4,0},{5,1},{6,2},{7,3},{8,12},{9,13},{10,... | collective-permute-start | bytes 786440 | tf_op jit(solution)/shard_map/ppermute | solution.py:932
  481.4 42.8 %collective-permute-start.23 = (bf16[256,512]{1,0:T(8,128)(2,1)}, bf16[256,512]{1,0:T(8,128)(2,1)}, u32[]{:S(2)}, u32[]{:S(2)}) collective-permute-start(bf16[256,512]{1,0:T(8,128)(2,1)} %get-tuple-element.172), channel_id=1, source_target_pairs={{0,2},{1,3},{2,4},{3,5},{4,6},{5,7},{6,0},{7,1},{8,10},{9,11},{10,... | collective-permute-start | bytes 786440 | tf_op jit(solution)/shard_map/ppermute | solution.py:932
  501.6 26.9 %collective-permute-start.26 = (bf16[256,512]{1,0:T(8,128)(2,1)}, bf16[256,512]{1,0:T(8,128)(2,1)}, u32[]{:S(2)}, u32[]{:S(2)}) collective-permute-start(bf16[256,512]{1,0:T(8,128)(2,1)} %get-tuple-element.168), channel_id=1, source_target_pairs={{0,6},{1,7},{2,0},{3,1},{4,2},{5,3},{6,4},{7,5},{8,14},{9,15},{10,... | collective-permute-start | bytes 786440 | tf_op jit(solution)/shard_map/ppermute | solution.py:932
  501.6 33.4 %collective-permute-start.27 = (bf16[256,512]{1,0:T(8,128)(2,1)}, bf16[256,512]{1,0:T(8,128)(2,1)}, u32[]{:S(2)}, u32[]{:S(2)}) collective-permute-start(bf16[256,512]{1,0:T(8,128)(2,1)} %get-tuple-element.170), channel_id=1, source_target_pairs={{0,4},{1,5},{2,6},{3,7},{4,0},{5,1},{6,2},{7,3},{8,12},{9,13},{10,... | collective-permute-start | bytes 786440 | tf_op jit(solution)/shard_map/ppermute | solution.py:932
  512.3 22.7 %collective-permute-start.28 = (bf16[256,512]{1,0:T(8,128)(2,1)}, bf16[256,512]{1,0:T(8,128)(2,1)}, u32[]{:S(2)}, u32[]{:S(2)}) collective-permute-start(bf16[256,512]{1,0:T(8,128)(2,1)} %get-tuple-element.169), channel_id=1, source_target_pairs={{0,2},{1,3},{2,4},{3,5},{4,6},{5,7},{6,0},{7,1},{8,10},{9,11},{10,... | collective-permute-start | bytes 786440 | tf_op jit(solution)/shard_map/ppermute | solution.py:932
  524.1 26.9 %collective-permute-start.39 = (f32[256,256]{1,0:T(8,128)}, f32[256,256]{1,0:T(8,128)}, u32[]{:S(2)}, u32[]{:S(2)}) collective-permute-start(f32[256,256]{1,0:T(8,128)} %bitcast.284), channel_id=1, source_target_pairs={{0,8},{1,9},{2,10},{3,11},{4,12},{5,13},{6,14},{7,15},{8,0},{9,1},... | collective-permute-start | bytes 786440 | tf_op jit(solution)/shard_map/ppermute | solution.py:932
  543.4 8.7 %collective-permute-start.24 = (f32[256,256]{1,0:T(8,128)}, f32[256,256]{1,0:T(8,128)}, u32[]{:S(2)}, u32[]{:S(2)}) collective-permute-start(f32[256,256]{1,0:T(8,128)} %bitcast.288), channel_id=1, source_target_pairs={{0,8},{1,9},{2,10},{3,11},{4,12},{5,13},{6,14},{7,15},{8,0},{9,1},... | collective-permute-start | bytes 786440 | tf_op jit(solution)/shard_map/ppermute | solution.py:932
  547.4 19.6 %collective-permute-start.34 = (f32[256,256]{1,0:T(8,128)}, f32[256,256]{1,0:T(8,128)}, u32[]{:S(2)}, u32[]{:S(2)}) collective-permute-start(f32[256,256]{1,0:T(8,128)} %bitcast.286), channel_id=1, source_target_pairs={{0,8},{1,9},{2,10},{3,11},{4,12},{5,13},{6,14},{7,15},{8,0},{9,1},... | collective-permute-start | bytes 786440 | tf_op jit(solution)/shard_map/ppermute | solution.py:932
  550.3 9.9 %collective-permute-start.29 = (f32[256,256]{1,0:T(8,128)}, f32[256,256]{1,0:T(8,128)}, u32[]{:S(2)}, u32[]{:S(2)}) collective-permute-start(f32[256,256]{1,0:T(8,128)} %bitcast.282), channel_id=1, source_target_pairs={{0,8},{1,9},{2,10},{3,11},{4,12},{5,13},{6,14},{7,15},{8,0},{9,1},... | collective-permute-start | bytes 786440 | tf_op jit(solution)/shard_map/ppermute | solution.py:932
  (85 other events, 538.4 us)

commit v3 on v2

--- a/solution.py
+++ b/solution.py
@@ -1,4 +1,5 @@
 import functools
+import types
 import jax
 import jax.numpy as jnp
 from jax import lax
@@ -9,6 +10,7 @@
 D = 1024
 F32 = jnp.float32
 BF = jnp.bfloat16
+ROW, COL = "row", "col"
 
 
 epsilon = 1e-05
@@ -17,11 +19,11 @@
 
 
 def gather_cols(local_rows):
-    return lax.all_gather(local_rows, "col", axis=1, tiled=True)
+    return lax.all_gather(local_rows, COL, axis=1, tiled=True)
 
 
 def gather_rows(local_rows):
-    return lax.all_gather(local_rows, "row", axis=1, tiled=True)
+    return lax.all_gather(local_rows, ROW, axis=1, tiled=True)
 
 
 def product(matmul_operand, weight_matrix):
@@ -31,11 +33,11 @@
 
 
 def rows_product(operand_full, matrix):
-    return lax.psum_scatter(product(operand_full, matrix), "row", scatter_dimension=1, tiled=True)
+    return lax.psum_scatter(product(operand_full, matrix), ROW, scatter_dimension=1, tiled=True)
 
 
 def cols_product(operand_full, matrix):
-    return lax.psum_scatter(product(operand_full, matrix), "col", scatter_dimension=1, tiled=True)
+    return lax.psum_scatter(product(operand_full, matrix), COL, scatter_dimension=1, tiled=True)
 
 
 def weight_grad(matmul_operand, upstream_gradient):
@@ -50,9 +52,9 @@
 
 def norm_forward(residual, gain_vec, bias_vec):
     local_sum = jnp.sum(residual, axis=-1)
-    average = lax.psum(local_sum, "row") / D
+    average = lax.psum(local_sum, ROW) / D
     centered = residual - average[..., None]
-    spread = lax.psum(jnp.sum(centered * centered, axis=-1), "row") / D
+    spread = lax.psum(jnp.sum(centered * centered, axis=-1), ROW) / D
     inv_std = lax.rsqrt(spread + epsilon)
     normed = centered * inv_std[..., None]
     return (normed * gain_vec + bias_vec, normed, inv_std)
@@ -61,7 +63,7 @@
 def norm_back(out_grad, normed, inv_std, gain_vec):
     scaled_grad = out_grad * gain_vec
     first_moment, second_moment = lax.psum(
-        (jnp.sum(scaled_grad, axis=-1), jnp.sum(scaled_grad * normed, axis=-1)), "row"
+        (jnp.sum(scaled_grad, axis=-1), jnp.sum(scaled_grad * normed, axis=-1)), ROW
     )
     resid_grad = inv_std[..., None] * (
         scaled_grad - first_moment[..., None] / D - normed * (second_moment[..., None] / D)
@@ -340,8 +342,8 @@
         token_grads.append((grad_one + cols_product(qkv_full, qkv_matrix.T))[0])
     norm_stack = jnp.stack(norm_accs)
     table_stack = jnp.stack([enc_table_acc, cross_table_acc])
-    norm_sums = lax.psum(norm_stack, "col")
-    table_sums = lax.psum(table_stack, "row")
+    norm_sums = lax.psum(norm_stack, COL)
+    table_sums = lax.psum(table_stack, ROW)
     return (
         jnp.stack(outputs),
         jnp.stack(token_grads),
@@ -473,10 +475,12 @@
 
 
 MESH = pl.DeviceIdType.MESH
+FORWARD, TURN, BACKWARD = range(3)
+ACROSS, THROUGH, ALONG, SUM_ACROSS, SUM_ALONG = range(5)
 
 
 def spot():
-    row, col = lax.axis_index("row"), lax.axis_index("col")
+    row, col = lax.axis_index(ROW), lax.axis_index(COL)
     return row // 2, row % 2, col // 2, col % 2
 
 
@@ -610,6 +614,171 @@
             copy.wait()
 
 
+class Freight:
+    def __init__(self, full_ref, z_sems, y_sems, place, seqs):
+        self.full, self.place, self.seqs = full_ref, place, seqs
+        self.z_sems, self.y_sems = z_sems, y_sems
+        self.wide = full_ref.shape[2] // 2
+        self.z, self.y = {}, {}
+        self.turn = seqs // 2
+
+    def along(self, d):
+        y, k, seq, half = self.place
+        up = d <= self.turn
+        source = d - 1 if up else (d + 1) % self.seqs
+        if source:
+            self.z[source].wait_recv()
+        target = lax.rem(seq + (1 if up else self.seqs - 1), self.seqs)
+        self.z[d] = remote(
+            self.full.at[source, :, : self.wide],
+            self.full.at[d, :, : self.wide],
+            self.z_sems.at[0, d - 1],
+            self.z_sems.at[1, d - 1],
+            device(y, k, target, half),
+        )
+
+    def first(self):
+        return [d for d in (1, self.seqs - 1) if d <= self.turn or d > self.turn][: min(2, self.seqs - 1)]
+
+    def later(self):
+        return list(range(2, self.turn + 1)) + list(range(self.seqs - 2, self.turn, -1))
+
+    def last(self):
+        return [d for d in range(1, self.seqs) if d == self.turn or d == self.turn + 1]
+
+    def across(self, d):
+        y, k, seq, half = self.place
+        self.y[d] = remote(
+            self.full.at[d, :, : self.wide],
+            self.full.at[d, :, self.wide :],
+            self.y_sems.at[0, d],
+            self.y_sems.at[1, d],
+            device(1 - y, k, seq, half),
+        )
+
+    def pass_along(self, cross):
+        for d in self.later():
+            self.along(d)
+            if cross:
+                self.across(d - 1 if d <= self.turn else d + 1)
+        for d in self.last():
+            self.z[d].wait_recv()
+            if cross:
+                self.across(d)
+
+    def finish(self):
+        for copy in self.z.values():
+            copy.wait_send()
+        for copy in self.y.values():
+            copy.wait()
+
+
+class Collect:
+    def __init__(self, source, place, seqs, y_refs=None, z_refs=None):
+        self.source, self.place, self.seqs = source, place, seqs
+        self.y_refs, self.z_refs = y_refs, z_refs
+        self.wide = source.shape[2] // 2 if y_refs else source.shape[2]
+        self.turn = seqs // 2
+        self.order = list(range(self.turn, seqs)) + list(range(self.turn - 1, -1, -1))
+        self.y, self.z, self.core = {}, {}, None
+
+    def across(self):
+        y, k, seq, half = self.place
+        buf, sems = self.y_refs
+        for d in self.order:
+            self.y[d] = remote(
+                self.source.at[d, :, self.wide :], buf.at[d], sems.at[0, d], sems.at[1, d], device(1 - y, k, seq, half)
+            )
+
+    def total(self, d):
+        if not self.y_refs:
+            return self.source[d].astype(F32)
+        self.y[d].wait_recv()
+        return self.source[d, :, : self.wide].astype(F32) + self.y_refs[0][d].astype(F32)
+
+    def store(self, out):
+        for d in self.order:
+            out[d] = self.total(d).astype(BF)
+
+    def along(self, d):
+        y, k, seq, half = self.place
+        out, z_send, z_buf, c_send, z_sems, c_sems = self.z_refs
+        left = d <= self.turn
+        before = d + 1 if left else d - 1
+        value = self.total(d)
+        if before in self.z and before not in (self.turn + 1 if left else self.turn,):
+            self.z[before].wait_recv()
+            value = value + z_buf[before - 1].astype(F32)
+        z_send[d - 1] = value.astype(BF)
+        target = lax.rem(seq + (self.seqs - 1 if left else 1), self.seqs)
+        self.z[d] = remote(
+            z_send.at[d - 1], z_buf.at[d - 1], z_sems.at[0, d - 1], z_sems.at[1, d - 1], device(y, k, target, half)
+        )
+
+    def close(self):
+        y, k, seq, half = self.place
+        out, z_send, z_buf, c_send, z_sems, c_sems = self.z_refs
+        total = self.total(0)
+        for d in sorted({1, self.seqs - 1}):
+            self.z[d].wait_recv()
+            total = total + z_buf[d - 1].astype(F32)
+        low, high = total[:, : self.wide // 2], total[:, self.wide // 2 :]
+        out[k] = jnp.where(k == 0, low, high)
+        c_send[...] = jnp.where(k == 0, high, low)
+        self.core = remote(c_send, out.at[k], c_sems.at[0], c_sems.at[1], device(y, 1 - k, seq, half))
+
+    def finish(self):
+        for copy in self.y.values():
+            copy.wait_send()
+        for copy in self.z.values():
+            copy.wait_send()
+        if self.core is not None:
+            self.core.wait()
+
+
+def freight_scratch(seqs):
+    dma = pltpu.SemaphoreType.DMA
+    return [dma((2, seqs - 1)), dma((2, seqs))]
+
+
+def across_scratch(seqs, n, wide):
+    return [pltpu.VMEM((seqs, n, wide), BF), pltpu.SemaphoreType.DMA((2, seqs))]
+
+
+def along_scratch(seqs, n, wide):
+    dma = pltpu.SemaphoreType.DMA
+    return [
+        pltpu.VMEM((seqs - 1, n, wide), BF),
+        pltpu.VMEM((seqs - 1, n, wide), BF),
+        pltpu.VMEM((n, wide // 2), F32),
+        dma((2, seqs - 1)),
+        dma((2,)),
+    ]
+
+
+def along_devices(place, seqs):
+    y, k, seq, half = place
+    return [device(y, k, lax.rem(seq + d, seqs), half) for d in sorted({1, seqs - 1})]
+
+
+def shuffle(source, target, n, index, place, sends, receives, local_sems):
+    y, k, seq, half = place
+    feat = source.shape[-1]
+    copies = [pltpu.make_async_copy(source.at[y, n, k], target.at[n, :, lanes(k * feat, feat)], local_sems.at[index])]
+    copies[0].start()
+    for i, (dy, dk, ty, tk) in enumerate(rows_of(place)):
+        copies.append(
+            remote(
+                source.at[ty, n, tk],
+                target.at[n, :, lanes(k * feat + 2 * dy * feat, feat)],
+                sends.at[index, i],
+                receives.at[index, i],
+                device(ty, tk, seq, half),
+            )
+        )
+    return copies
+
+
 def normalize(residual):
     centered = residual - jnp.mean(residual, axis=-1, keepdims=True)
     inv_std = lax.rsqrt(jnp.mean(centered * centered, axis=-1, keepdims=True) + epsilon)
@@ -627,88 +796,154 @@
     return jnp.sum(value, axis=0, keepdims=True)
 
 
-def exchange_kernel(kind, count, pieces, *refs):
+def exchange_kernel(kind, count, pieces, seqs, rides, *refs):
     place = spot()
     y, k, seq, half = place
-    names = {
-        "forward": ("resid", "norm", "full", "out", "normed", "inv"),
-        "turn": ("resid", "norm", "cot", "full", "output", "grad", "sums", "own", "landing", "return_sems"),
-        "backward": ("resid", "norm", "normed", "inv", "full", "grad", "sums"),
-    }[kind]
-    partial, refs = refs[0], refs[1:]
-    r = dict(zip(names, refs))
-    core_buf, half_send, half_buf, rc, rh, gh, gc = refs[len(names) :]
+    refs = list(refs)
+    take = lambda amount: [refs.pop(0) for _ in range(amount)]
+    r = types.SimpleNamespace()
+    partial, r.resid, r.norm = take(3)
+    if kind == TURN:
+        (r.cot,) = take(1)
+    elif kind == BACKWARD:
+        r.normed, r.inv = take(2)
+    ride_in = take(len(rides))
+    (r.full,) = take(1)
+    if kind == FORWARD:
+        r.out, r.normed, r.inv = take(3)
+    elif kind == TURN:
+        r.output, r.grad, r.sums = take(3)
+    else:
+        r.grad, r.sums = take(2)
+    ride_out = take(len(rides))
+    if kind == TURN:
+        r.own, r.landing, r.return_sems, r.cot_own, r.cot_send, r.cot_recv, r.cot_local = take(7)
+    core_buf, half_send, half_buf, rc, rh, gh, gc = take(7)
     rows = partial.shape[3] // pieces
     peers = [device(y, 1 - k, seq, half), device(y, k, seq, 1 - half)]
-    if kind == "turn":
+    if kind == TURN:
         peers += [device(ty, tk, seq, half) for dy, dk, ty, tk in rows_of(place) if dy]
+    elif {ACROSS, THROUGH, SUM_ACROSS} & set(rides):
+        peers.append(device(1 - y, k, seq, half))
+    if {ALONG, THROUGH, SUM_ALONG} & set(rides):
+        peers += along_devices(place, seqs)
     greet(peers)
     units = [(n * pieces + p, n, p) for n in range(count) for p in range(pieces)]
     reduce = Reduce(partial, core_buf, half_send, half_buf, rc, rh, place, rows)
-    spread = Spread(r["full"], gh, gc, place, rows)
+    spread = Spread(r.full, gh, gc, place, rows)
     for unit, n, p in units:
         reduce.start(unit, n, p, True)
     for unit, n, p in units:
         reduce.start(unit, n, p, False)
-    if kind != "forward":
-        r["sums"][...] = jnp.zeros_like(r["sums"])
-    if kind == "turn":
-        back = Return(r["own"], r["landing"], r["return_sems"], place, partial.shape[4] // 4)
-    gain, bias = r["norm"][0:1], r["norm"][1:2]
+    moves, sums_along, sums_across = [], [], []
+    for ride, source, target in zip(rides, ride_in, ride_out):
+        if ride == SUM_ACROSS:
+            sums_across.append((Collect(source, place, seqs, y_refs=take(2)), target))
+            sums_across[-1][0].across()
+        elif ride == SUM_ALONG:
+            sums_along.append(Collect(source, place, seqs, z_refs=[target] + take(5)))
+            for d in sums_along[-1].order[:2]:
+                sums_along[-1].along(d)
+        else:
+            moves.append((ride, Freight(target, *take(2), place, seqs)))
+            if ride == ACROSS:
+                for d in range(seqs):
+                    moves[-1][1].across(d)
+            else:
+                if ride == THROUGH:
+                    moves[-1][1].across(0)
+                for d in moves[-1][1].first():
+                    moves[-1][1].along(d)
+    if kind != FORWARD:
+        r.sums[...] = jnp.zeros_like(r.sums)
+    if kind == TURN:
+        back = Return(r.own, r.landing, r.return_sems, place, partial.shape[4] // 4)
+        cots = [
+            shuffle(r.cot, r.cot_own, n, n, place, r.cot_send, r.cot_recv, r.cot_local) for n in range(count)
+        ]
+    gain, bias = r.norm[0:1], r.norm[1:2]
     for unit, n, p in units:
         reduce.pass_on(unit, n, p)
     for unit, n, p in units:
         here = pl.ds(p * rows, rows)
         branch = reduce.result(unit, n, p)
-        if kind == "forward":
-            normed, inv = normalize(r["resid"][n, here].astype(F32) + branch)
+        if kind == FORWARD:
+            normed, inv = normalize(r.resid[n, here].astype(F32) + branch)
             value = normed * gain + bias
-            r["out"][n, here] = value
-            r["normed"][n, here] = normed
-            r["inv"][n, here] = inv
-        elif kind == "turn":
-            normed, inv = normalize(r["resid"][n, here].astype(F32) + branch)
-            upstream = r["cot"][n, here].astype(F32)
+            r.out[n, here] = value
+            r.normed[n, here] = normed
+            r.inv[n, here] = inv
+        elif kind == TURN:
+            normed, inv = normalize(r.resid[n, here].astype(F32) + branch)
+            if p == 0:
+                for copy in cots[n]:
+                    copy.wait()
+            upstream = r.cot_own[n, here].astype(F32)
             value = normalize_back(upstream, normed, inv, gain)
-            r["grad"][n, here] = value
+            r.grad[n, here] = value
         else:
-            upstream = r["resid"][n, here] + branch if r["resid"].shape[1] == partial.shape[3] else branch
-            normed = r["normed"][n, here]
-            value = normalize_back(upstream, normed, r["inv"][n, here], gain)
-            r["grad"][n, here] = value
-        r["full"][n, half, k, here] = value.astype(BF)
+            upstream = r.resid[n, here] + branch if r.resid.shape[1] == partial.shape[3] else branch
+            normed = r.normed[n, here]
+            value = normalize_back(upstream, normed, r.inv[n, here], gain)
+            r.grad[n, here] = value
+        r.full[n, half, k, here] = value.astype(BF)
         spread.start(unit, n, p)
-        if kind != "forward":
-            r["sums"][0:1] += column_sum(upstream * normed)
-            r["sums"][1:2] += column_sum(upstream)
-        if kind == "turn":
+        if kind != FORWARD:
+            r.sums[0:1] += column_sum(upstream * normed)
+            r.sums[1:2] += column_sum(upstream)
+        if kind == TURN:
             back.start(unit, n, (normed * gain + bias).astype(BF))
+    for collect in sums_along:
+        for d in collect.order[2:-1]:
+            collect.along(d)
+    for ride, move in moves:
+        if ride != ACROSS:
+            move.pass_along(ride == THROUGH)
     for unit, n, p in units:
         spread.forward(unit, n, p)
+    for collect in sums_along:
+        collect.close()
     for unit, n, p in units:
         spread.finish(unit)
         reduce.finish(unit)
-    if kind == "turn":
+    if kind == TURN:
         back.finish()
-        r["output"][...] = r["landing"][...].astype(F32)
-
-
-def exchange(kind, collective_id, partial, resid, norm, cot=None, normed=None, inv=None):
+        r.output[...] = r.landing[...].astype(F32)
+    for ride, move in moves:
+        move.finish()
+    for collect, target in sums_across:
+        collect.store(target)
+        collect.finish()
+    for collect in sums_along:
+        collect.finish()
+
+
+def exchange(kind, collective_id, seqs, partial, resid, norm, cot=None, normed=None, inv=None, rides=()):
     count, _, _, own, depth = partial.shape
     pieces = 2 if count == 1 else 1
     units, rows = count * pieces, own // pieces
     dma = pltpu.SemaphoreType.DMA
     shape = jax.ShapeDtypeStruct
+    vmem = pl.BlockSpec(memory_space=pltpu.VMEM)
+    anywhere = pl.BlockSpec(memory_space=pl.ANY)
     full = shape((count, 2, 2, own, depth), BF)
     grad, sums = shape((count, own, depth), F32), shape((8, depth), F32)
     scratch = []
-    if kind == "forward":
+    if kind == FORWARD:
         args = (partial, resid, norm)
         outs = (full, grad, grad, shape((count, own, 1), F32))
-    elif kind == "turn":
+    elif kind == TURN:
         args = (partial, resid, norm, cot)
         outs = (full, shape((2, count, 2, own, depth // 4), F32), grad, sums)
-        scratch = [pltpu.VMEM((units, rows, depth), BF), pltpu.VMEM((2, count, 2, own, depth // 4), BF), dma((2, units, 3))]
+        scratch = [
+            pltpu.VMEM((units, rows, depth), BF),
+            pltpu.VMEM((2, count, 2, own, depth // 4), BF),
+            dma((2, units, 3)),
+            pltpu.VMEM((count, own, depth), BF),
+            dma((count, 3)),
+            dma((count, 3)),
+            dma((count,)),
+        ]
     else:
         args = (partial, resid, norm, normed, inv)
         outs = (full, grad, sums)
@@ -721,47 +956,61 @@
         dma((2, units)),
         dma((2, units, 2)),
     ]
+    in_specs, out_specs = [vmem] * len(args), [vmem] * len(outs)
+    aliases = {}
+    for ride, array in rides:
+        if ride == SUM_ACROSS or ride == SUM_ALONG:
+            n, wide = array.shape[1], depth // 2
+            scratch += (across_scratch if ride == SUM_ACROSS else along_scratch)(seqs, n, wide)
+            in_specs.append(vmem)
+            out_specs.append(vmem)
+            outs += (shape((seqs, n, wide), BF) if ride == SUM_ACROSS else shape((2, n, wide // 2), F32),)
+        else:
+            scratch += freight_scratch(seqs)
+            aliases[len(args)] = len(outs)
+            in_specs.append(anywhere)
+            out_specs.append(anywhere)
+            outs += (shape(array.shape, array.dtype),)
+        args += (array,)
     return pl.pallas_call(
-        functools.partial(exchange_kernel, kind, count, pieces),
+        functools.partial(exchange_kernel, kind, count, pieces, seqs, tuple(ride for ride, _ in rides)),
         out_shape=outs,
-        in_specs=[pl.BlockSpec(memory_space=pltpu.VMEM)] * len(args),
-        out_specs=tuple(pl.BlockSpec(memory_space=pltpu.VMEM) for _ in outs),
+        in_specs=in_specs,
+        out_specs=tuple(out_specs),
         scratch_shapes=scratch,
+        input_output_aliases=aliases,
         compiler_params=pltpu.CompilerParams(collective_id=collective_id, has_side_effects=True, vmem_limit_bytes=50 << 20),
-        name="exchange_" + kind,
+        name="exchange_%d" % collective_id,
     )(*args)
 
 
-def inputs_kernel(seqs, tok_ref, str_ref, cot_ref, norm_ref, ids_ref, tab_ref, x_own, x_full, y_own, y_full, c_own, norm_all, ids_all, tab_all, in_send, in_recv, self_sems, xh, xc, yh, yc, small_sems, tab_sems, small_self):
+def inputs_kernel(seqs, groups, tok_ref, str_ref, norm_ref, ids_ref, tab_ref, *refs):
+    refs = list(refs)
+    take = lambda amount: [refs.pop(0) for _ in range(amount)]
+    packs = take(groups)
+    x_own, x_full, y_own, y_full, norm_all, ids_all, tab_all = take(7)
+    fulls = take(groups)
+    in_send, in_recv, in_local, xh, xc, yh, yc, small_sems, tab_sems, small_self, pack_sems, pack_self = take(12)
     place = spot()
     y, k, seq, half = place
     feat = tok_ref.shape[-1]
     own = tok_ref.shape[-2]
     row_peers = rows_of(place)
-    rest = [lax.rem(seq + d, seqs) for d in range(1, seqs)]
-    greet(
-        [device(ty, tk, seq, half) for dy, dk, ty, tk in row_peers]
-        + [device(y, k, seq, 1 - half)]
-        + [device(y, k, s, half) for s in rest]
-    )
-
-    def shuffle(source, target, n, index):
-        copies = [pltpu.make_async_copy(source.at[y, n, k], target.at[n, :, lanes(k * feat, feat)], self_sems.at[index])]
-        copies[0].start()
-        for i, (dy, dk, ty, tk) in enumerate(row_peers):
-            copies.append(
-                remote(
-                    source.at[ty, n, tk],
-                    target.at[n, :, lanes(k * feat + 2 * dy * feat, feat)],
-                    in_send.at[index, i],
-                    in_recv.at[index, i],
-                    device(ty, tk, seq, half),
-                )
+    others = [device(y, k, lax.rem(seq + d, seqs), half) for d in range(1, seqs)]
+    greet([device(ty, tk, seq, half) for dy, dk, ty, tk in row_peers] + [device(y, k, seq, 1 - half)] + others)
+    count = str_ref.shape[1]
+    x_copies = shuffle(tok_ref, x_own, 0, 0, place, in_send, in_recv, in_local)
+    loads = []
+    for g in range(groups):
+        here = fulls[g].at[0, :, lanes(k * feat, feat)]
+        copy = pltpu.make_async_copy(packs[g].at[k], here, pack_self.at[g])
+        copy.start()
+        loads.append(
+            (
+                copy,
+                remote(packs[g].at[1 - k], here, pack_sems.at[0, g], pack_sems.at[1, g], device(y, 1 - k, seq, half)),
             )
-        return copies
-
-    count = str_ref.shape[1]
-    x_copies = shuffle(tok_ref, x_own, 0, 0)
+        )
     small = []
     for j, (source, target) in enumerate(((norm_ref, norm_all), (ids_ref, ids_all))):
         slot = (lambda dy: (slice(None), lanes(k * feat + 2 * dy * feat, feat))) if j == 0 else (lambda dy: (2 * y + k,))
@@ -776,83 +1025,108 @@
     copy.start()
     small.append(copy)
     for d in range(1, seqs):
-        small.append(
-            remote(tab_ref, tab_all.at[d], tab_sems.at[0, d - 1], tab_sems.at[1, d - 1], device(y, k, rest[d - 1], half))
-        )
+        small.append(remote(tab_ref, tab_all.at[d], tab_sems.at[0, d - 1], tab_sems.at[1, d - 1], others[d - 1]))
+    freights = [Freight(full, *take(2), place, seqs) for full in fulls]
+    for copy in loads[0]:
+        copy.wait()
+    for d in freights[0].first():
+        freights[0].along(d)
+    freights[0].across(0)
     for copy in x_copies:
         copy.wait()
     x_full[0, half, k] = x_own[0]
     x_spread = Spread(x_full, xh, xc, place, own)
     x_spread.start(0, 0, 0)
-    y_copies = [shuffle(str_ref, y_own, n, 1 + n) for n in range(count)]
+    y_copies = [shuffle(str_ref, y_own, n, 1 + n, place, in_send, in_recv, in_local) for n in range(count)]
     y_spread = Spread(y_full, yh, yc, place, own)
+    for g in range(1, groups):
+        for copy in loads[g]:
+            copy.wait()
     x_spread.forward(0, 0, 0)
     for n in range(count):
         for copy in y_copies[n]:
             copy.wait()
         y_full[n, half, k] = y_own[n]
         y_spread.start(n, n, 0)
-    c_copies = [shuffle(cot_ref, c_own, n, 1 + count + n) for n in range(count)]
+    freights[0].pass_along(True)
+    for d in freights[1].first():
+        freights[1].along(d)
+    freights[1].across(0)
     for n in range(count):
         y_spread.forward(n, n, 0)
+    for copy in small:
+        copy.wait()
+    freights[1].pass_along(True)
+    for d in freights[2].first():
+        freights[2].along(d)
+    freights[2].pass_along(False)
     x_spread.finish(0)
     for n in range(count):
         y_spread.finish(n)
-        for copy in c_copies[n]:
-            copy.wait()
-    for copy in small:
-        copy.wait()
-
-
-def gather_inputs(seqs, tokens, streams, cotangent, norm, ids, table):
+    for freight in freights:
+        freight.finish()
+
+
+def gather_inputs(seqs, tokens, streams, norm, ids, table, packs):
     count, own, feat = streams.shape[1], streams.shape[-2], streams.shape[-1]
     depth = 4 * feat
     dma = pltpu.SemaphoreType.DMA
     shape = jax.ShapeDtypeStruct
+    vmem = pl.BlockSpec(memory_space=pltpu.VMEM)
     outs = (
         shape((1, own, depth), BF),
         shape((1, 2, 2, own, depth), BF),
         shape((count, own, depth), BF),
         shape((count, 2, 2, own, depth), BF),
-        shape((count, own, depth), BF),
         shape((norm.shape[0], depth), F32),
         shape((4,) + ids.shape, jnp.int32),
         shape((seqs,) + table.shape, F32),
     )
-    moves = 1 + 2 * count
+    specs = [vmem] * len(outs)
+    for pack in packs:
+        outs += (shape((seqs, pack.shape[1], depth), BF),)
+        specs.append(pl.BlockSpec(memory_space=pl.ANY))
+    moves = 1 + count
+    scratch = [
+        dma((moves, 3)),
+        dma((moves, 3)),
+        dma((moves,)),
+        dma((2, 1)),
+        dma((2, 1, 2)),
+        dma((2, count)),
+        dma((2, count, 2)),
+        dma((2, 2, 3)),
+        dma((2, seqs - 1)),
+        dma((3,)),
+        dma((2, len(packs))),
+        dma((len(packs),)),
+    ]
+    for _ in packs:
+        scratch += freight_scratch(seqs)
     return pl.pallas_call(
-        functools.partial(inputs_kernel, seqs),
+        functools.partial(inputs_kernel, seqs, len(packs)),
         out_shape=outs,
-        in_specs=[pl.BlockSpec(memory_space=pltpu.VMEM)] * 6,
-        out_specs=tuple(pl.BlockSpec(memory_space=pltpu.VMEM) for _ in outs),
-        scratch_shapes=[
-            dma((moves, 3)),
-            dma((moves, 3)),
-            dma((moves,)),
-            dma((2, 1)),
-            dma((2, 1, 2)),
-            dma((2, count)),
-            dma((2, count, 2)),
-            dma((2, 2, 3)),
-            dma((2, seqs - 1)),
-            dma((3,)),
-        ],
+        in_specs=[vmem] * (5 + len(packs)),
+        out_specs=tuple(specs),
+        scratch_shapes=scratch,
         compiler_params=pltpu.CompilerParams(collective_id=0, has_side_effects=True, vmem_limit_bytes=50 << 20),
         name="gather_inputs",
-    )(tokens, streams, cotangent, norm, ids, table)
-
-
-def outputs_kernel(seqs, count, part_x, part_y, d1, d3, small, tok_out, str_out, small_out, core_buf, half_send, half_buf, own, land_x, land_y, rc, rh, rs, small_buf, ss):
+    )(tokens, streams, norm, ids, table, *packs)
+
+
+def outputs_kernel(seqs, count, part_x, part_y, d1, d3, small, down, up, first, tok_out, str_out, small_out, down_out, up_out, first_out, core_buf, half_send, half_buf, own, land_x, land_y, rc, rh, rs, small_buf, ss, *refs):
+    refs = list(refs)
+    take = lambda amount: [refs.pop(0) for _ in range(amount)]
     place = spot()
     y, k, seq, half = place
     rows = part_x.shape[3]
     feat = part_x.shape[4] // 4
-    bits = []
-    while 1 << len(bits) < seqs:
-        bits.append(1 << len(bits))
+    bits = [1 << b for b in range((seqs - 1).bit_length())]
     flips = [device(y, k, seq + b - 2 * b * ((seq // b) % 2), half) for b in bits]
-    partners = [device(y, 1 - k, seq, half), device(y, k, seq, 1 - half), device(1 - y, k, seq, half)] + flips
-    greet(partners + [device(1 - y, 1 - k, seq, half)])
+    others = [device(y, k, lax.rem(seq + d, seqs), half) for d in range(1, seqs)]
+    partners = [device(y, 1 - k, seq, half), device(y, k, seq, 1 - half), device(1 - y, k, seq, half)]
+    greet(partners + [device(1 - y, 1 - k, seq, half)] + others)
+    partners += flips
     small_out[...] = small[...]
 
     def add_small(stage):
@@ -874,83 +1148,90 @@
 
     reduce = Reduce(Both(), core_buf, half_send, half_buf, rc, rh, place, rows)
     units = range(count + 1)
-    for unit in units:
+    down = Collect(down, place, seqs, z_refs=[down_out] + take(5))
+    up = Collect(up, place, seqs, y_refs=take(2), z_refs=[up_out] + take(5))
+    first = Collect(first, place, seqs, y_refs=take(2), z_refs=[first_out] + take(5))
+    reduce.start(0, 0, 0, True)
+    reduce.start(0, 0, 0, False)
+    add_small(2)
+    up.across()
+    add_small(1)
+    reduce.pass_on(0, 0, 0)
+    for stage in range(3, len(partners)):
+        add_small(stage)
+    for d in down.order[:2]:
+        down.along(d)
+    add_small(0)
+    for unit in units[1:]:
         reduce.start(unit, unit, 0, True)
         reduce.start(unit, unit, 0, False)
-    for unit in units:
-        reduce.pass_on(unit, unit, 0)
-    for stage in range(len(partners)):
-        add_small(stage)
     x_back = Return(own, land_x, rs, place, feat)
     y_back = Return(own, land_y, rs, place, feat)
-    for unit in units:
-        branch = reduce.result(unit, unit, 0)
-        if unit == 0:
-            x_back.start(unit, 0, (d1[0] + branch).astype(BF))
-        else:
-            y_back.start(unit, unit - 1, (d3[unit - 1] + branch).astype(BF))
+    x_back.start(0, 0, (d1[0] + reduce.result(0, 0, 0)).astype(BF))
+    first.across()
+    for unit in units[1:]:
+        reduce.pass_on(unit, unit, 0)
+    for d in down.order[2:-1]:
+        down.along(d)
+    for d in up.order[:1]:
+        up.along(d)
+    down.close()
+    for d in up.order[1:-1]:
+        up.along(d)
+    for unit in units[1:]:
+        y_back.start(unit, unit - 1, (d3[unit - 1] + reduce.result(unit, unit, 0)).astype(BF))
     for unit in units:
         reduce.finish(unit)
     x_back.finish()
     tok_out[...] = land_x[:, 0].astype(F32)
+    up.close()
+    for d in first.order[:-1]:
+        first.along(d)
     y_back.finish()
     str_out[...] = land_y[...].astype(F32)
-
-
-def scatter_outputs(seqs, collective_id, part_x, part_y, d1, d3, small):
+    first.close()
+    for collect in (down, up, first):
+        collect.finish()
+
+
+def scatter_outputs(seqs, collective_id, part_x, part_y, d1, d3, small, down, up, first):
     count, _, _, own, depth = part_y.shape
-    feat = depth // 4
+    feat, wide = depth // 4, depth // 2
     units = count + 1
     dma = pltpu.SemaphoreType.DMA
     shape = jax.ShapeDtypeStruct
     stages = 3 + (seqs - 1).bit_length()
     outs = (shape((2, 2, own, feat), F32), shape((2, count, 2, own, feat), F32), shape(small.shape, F32))
+    outs += tuple(shape((2, group.shape[1], feat), F32) for group in (down, up, first))
+    scratch = [
+        pltpu.VMEM((units, 2, own, depth), BF),
+        pltpu.VMEM((units, own, depth), BF),
+        pltpu.VMEM((units, own, depth), BF),
+        pltpu.VMEM((units, own, depth), BF),
+        pltpu.VMEM((2, 1, 2, own, feat), BF),
+        pltpu.VMEM((2, count, 2, own, feat), BF),
+        dma((2, units, 2)),
+        dma((2, units)),
+        dma((2, units, 3)),
+        pltpu.VMEM((stages,) + small.shape, F32),
+        dma((2, stages)),
+    ]
+    scratch += along_scratch(seqs, down.shape[1], wide)
+    for group in (up, first):
+        scratch += across_scratch(seqs, group.shape[1], wide) + along_scratch(seqs, group.shape[1], wide)
     return pl.pallas_call(
         functools.partial(outputs_kernel, seqs, count),
         out_shape=outs,
-        in_specs=[pl.BlockSpec(memory_space=pltpu.VMEM)] * 5,
+        in_specs=[pl.BlockSpec(memory_space=pltpu.VMEM)] * 8,
         out_specs=tuple(pl.BlockSpec(memory_space=pltpu.VMEM) for _ in outs),
-        scratch_shapes=[
-            pltpu.VMEM((units, 2, own, depth), BF),
-            pltpu.VMEM((units, own, depth), BF),
-            pltpu.VMEM((units, own, depth), BF),
-            pltpu.VMEM((units, own, depth), BF),
-            pltpu.VMEM((2, 1, 2, own, feat), BF),
-            pltpu.VMEM((2, count, 2, own, feat), BF),
-            dma((2, units, 2)),
-            dma((2, units)),
-            dma((2, units, 3)),
-            pltpu.VMEM((stages,) + small.shape, F32),
-            dma((2, stages)),
-        ],
+        scratch_shapes=scratch,
         compiler_params=pltpu.CompilerParams(collective_id=collective_id, has_side_effects=True, vmem_limit_bytes=50 << 20),
         name="scatter_outputs",
-    )(part_x, part_y, d1, d3, small)
-
-
-def send(value, pairs):
-    return lax.ppermute(value, ("row", "col"), pairs)
-
-
-def device_pairs(rows, cols):
-    seqs = cols // 2
-    place = lambda y, k, s, h: (2 * (y % (rows // 2)) + k % 2) * cols + 2 * (s % seqs) + h % 2
-    spots = [(y, k, s, h) for y in range(rows // 2) for k in range(2) for s in range(seqs) for h in range(2)]
-    move = lambda dy, dk, ds, dh: [(place(y, k, s, h), place(y + dy, k + dk, s + ds, h + dh)) for y, k, s, h in spots]
-    return {
-        "core": move(0, 1, 0, 0),
-        "half": move(0, 0, 0, 1),
-        "micro": move(1, 0, 0, 0),
-        "seq": [move(0, 0, d, 0) for d in range(seqs)],
-    }
+    )(part_x, part_y, d1, d3, small, down, up, first)
 
 
 def pick(array, index, axis):
     return lax.dynamic_index_in_dim(array, index, axis, keepdims=False)
-
-
-def in_order(first, mine, other, axis, join=jnp.concatenate):
-    return jnp.where(first, join([mine, other], axis=axis), join([other, mine], axis=axis))
 
 
 def dot_f32(spec, left, right):
@@ -981,11 +1262,10 @@
     cross_gain,
     cross_bias,
 ):
-    pairs = device_pairs(rows, cols)
     seqs = cols // 2
-    row, col = lax.axis_index("row"), lax.axis_index("col")
+    row, col = lax.axis_index(ROW), lax.axis_index(COL)
     y, k, seq, half = row // 2, row % 2, col // 2, col % 2
-    low_core, low_y = k == 0, y == 0
+    low_y = y == 0
     stream_count = streams.shape[1]
     tok = tokens.shape[1]
     own = tok // 2
@@ -995,17 +1275,31 @@
     ff = w_up.shape[1] // 2
     table_heads, bucket_count = enc_table.shape
 
+    def columns(weight, parts):
+        return weight.reshape(feat, parts, 2, -1).transpose(2, 1, 3, 0).reshape(2, -1, feat)
+
+    def columns_back(array, parts):
+        return array.reshape(2, parts, -1, feat).transpose(3, 1, 0, 2).reshape(feat, parts, -1)
+
+    halves = lambda weight: weight.reshape(2, -1, feat)
+    hd3, hd2 = 3 * head_dim, 2 * head_dim
+    packs = (
+        jnp.concatenate([columns(w_qkv, 3), halves(w_out)], axis=1),
+        columns(w_up, 1),
+        halves(w_down),
+        jnp.concatenate([columns(w_keyval, 2), columns(w_query, 1), halves(w_cross_out)], axis=1),
+    )
     norm_params = jnp.stack([attention_norm_gain, attn_bias, ffn_gain, ffn_bias, cross_gain, cross_bias] + [cross_bias] * 2)
     table_pack = jnp.zeros((8, 128), F32).at[0].set(jnp.stack([enc_table, cross_table]).reshape(-1))
     micro_count = tokens.shape[0]
-    x_own, x_full, y_own, y_full, c_own, norm_params, all_ids, all_tables = gather_inputs(
+    x_own, x_full, y_own, y_full, norm_params, all_ids, all_tables, first, up, down, last = gather_inputs(
         seqs,
         tokens.reshape(micro_count, 1, 2, own, feat),
         streams.reshape(micro_count, stream_count, 2, own, feat),
-        cotangent.reshape(micro_count, stream_count, 2, own, feat),
         norm_params,
         block_ids.reshape(8, -1),
         table_pack,
+        packs,
     )
     x_full, y_full = x_full.reshape(length, D), y_full.reshape(stream_count * length, D)
     segment = pick(pick(all_ids.reshape(rows, micro_count, length), seq, 0), y, 0)
@@ -1017,58 +1311,43 @@
     onehot = bucket_onehot(reversed_ids, bucket_count)
     offsets = jnp.einsum("htb,bo->tho", own_tables, onehot, precision=highest)[:, :, None, :]
 
-    def gather_weights(shards):
-        base = in_order(low_core, pick(shards, k, 0), send(pick(shards, 1 - k, 0), pairs["core"]), 1)
-        slots = jnp.stack([base] + [send(base, pairs["seq"][d]) for d in range(1, seqs)])
-        return jnp.concatenate([slots, send(slots, pairs["micro"])], axis=2)
-
-    def scatter_weights(grad):
-        part = grad[:, :, : D // 2] + send(grad[:, :, D // 2 :].astype(BF), pairs["micro"]).astype(F32)
-        low = part.astype(BF)
-        total = part[0]
-        for d in range(1, seqs):
-            total = total + send(low[d], pairs["seq"][seqs - d]).astype(F32)
-        blocks = total.reshape(-1, 2, feat)
-        other = send(pick(blocks, 1 - k, 1), pairs["core"])
-        return in_order(low_core, pick(blocks, k, 1), other, 0, jnp.stack)
-
-    def columns(weight, parts):
-        return weight.reshape(feat, parts, 2, -1).transpose(2, 1, 3, 0).reshape(2, -1, feat)
-
-    def columns_back(array, parts):
-        return array.reshape(2, parts, -1, feat).transpose(3, 1, 0, 2).reshape(feat, parts, -1)
-
-    halves = lambda weight: weight.reshape(2, -1, feat)
-    hd3, hd2 = 3 * head_dim, 2 * head_dim
-    first = gather_weights(jnp.concatenate([columns(w_qkv, 3), halves(w_out)], axis=1))
-    up = gather_weights(columns(w_up, 1))
-    down = gather_weights(halves(w_down))
-    last = gather_weights(jnp.concatenate([columns(w_keyval, 2), columns(w_query, 1), halves(w_cross_out)], axis=1))
     m_qkv, m_out = first[:, :hd3], first[:, hd3:].reshape(-1, D)
-    m_kv, m_q, m_co = last[:, :hd2], last[:, hd2:hd3], last[:, hd3:].reshape(-1, D)
-    up, down = up.reshape(-1, D), down.reshape(-1, D)
     blocked = lambda product: product.astype(BF).reshape(-1, 2, 2, own, D)
 
     qkv = dot_f32("snr,tr->snt", m_qkv, x_full).astype(BF)
     mix, lse, tiles = attention(offsets[0], segq, segk, qkv, qkv, qkv, (0, 1, 2), 1)
     mix_flat = mix.reshape(-1, length)
-    hidden_full, hidden, normed1, inv1 = exchange(
-        "forward", 1, blocked(dot_f32("et,er->tr", mix_flat, m_out)), x_own, norm_params[0:2]
-    )
+    hidden_full, hidden, normed1, inv1, down, last = exchange(
+        FORWARD,
+        1,
+        seqs,
+        blocked(dot_f32("et,er->tr", mix_flat, m_out)),
+        x_own,
+        norm_params[0:2],
+        rides=((ACROSS, down), (ALONG, last)),
+    )
+    up, down = up.reshape(-1, D), down.reshape(-1, D)
     hidden_full = hidden_full.reshape(length, D)
     pre = dot_f32("fr,tr->ft", up, hidden_full)
     act, gelu_pull = jax.vjp(gelu_exact, pre)
     act = act.astype(BF)
-    enc_full, _, normed2, inv2 = exchange(
-        "forward", 2, blocked(dot_f32("ft,fr->tr", act, down)), hidden, norm_params[2:4]
-    )
+    enc_full, _, normed2, inv2, last = exchange(
+        FORWARD,
+        2,
+        seqs,
+        blocked(dot_f32("ft,fr->tr", act, down)),
+        hidden,
+        norm_params[2:4],
+        rides=((ACROSS, last),),
+    )
+    m_kv, m_q, m_co = last[:, :hd2], last[:, hd2:hd3], last[:, hd3:].reshape(-1, D)
     enc_full = enc_full.reshape(length, D)
     kv = dot_f32("snr,tr->snt", m_kv, enc_full).astype(BF)
     query = dot_f32("snr,tr->snt", m_q, y_full).astype(BF)
     cmix, clse, ctiles = attention(offsets[1], segq, segk, query, kv, kv, (0, 0, 1), stream_count)
     cmix_flat = cmix.reshape(-1, stream_count * length)
     d3_full, output, d3, sums3 = exchange(
-        "turn", 3, blocked(dot_f32("et,er->tr", cmix_flat, m_co)), y_own, norm_params[4:6], cot=c_own
+        TURN, 3, seqs, blocked(dot_f32("et,er->tr", cmix_flat, m_co)), y_own, norm_params[4:6], cot=cotangent.reshape(micro_count, stream_count, 2, own, feat)
     )
     d3_full = d3_full.reshape(stream_count * length, D)
 
@@ -1078,28 +1357,44 @@
         ctiles, segq, segk, query, kv, kv, (0, 0, 1), clse, dcmix, stream_count
     )
     dkv = jnp.concatenate([dkc, dvc], axis=1)
-    d2_full, d2, sums2 = exchange(
-        "backward", 4, blocked(dot_f32("snt,snr->tr", dkv, m_kv)), norm_params[2:4][None], norm_params[2:4], normed=normed2, inv=inv2
-    )
-    d2_full = d2_full.reshape(length, D)
     g_q = dot_f32("snt,tr->snr", dquery, y_full)
     g_kv = dot_f32("snt,tr->snr", dkv, enc_full)
-    g_last = scatter_weights(jnp.concatenate([g_kv, g_q, g_co.reshape(seqs, head_dim, D)], axis=1))
+    g_last = jnp.concatenate([g_kv.astype(BF), g_q.astype(BF), g_co.astype(BF).reshape(seqs, head_dim, D)], axis=1)
+    d2_full, d2, sums2, g_last = exchange(
+        BACKWARD,
+        4,
+        seqs,
+        blocked(dot_f32("snt,snr->tr", dkv, m_kv)),
+        norm_params[2:4][None],
+        norm_params[2:4],
+        normed=normed2,
+        inv=inv2,
+        rides=((SUM_ACROSS, g_last),),
+    )
+    d2_full = d2_full.reshape(length, D)
     part_y = blocked(dot_f32("snt,snr->tr", dquery, m_q))
     dact = dot_f32("fr,tr->ft", down, d2_full)
     dpre = gelu_pull(dact)[0].astype(BF)
-    g_down = scatter_weights(dot_f32("ft,tr->fr", act, d2_full).reshape(seqs, ff, D))
-    d1_full, d1, sums1 = exchange(
-        "backward", 5, blocked(dot_f32("ft,fr->tr", dpre, up)), d2, norm_params[0:2], normed=normed1, inv=inv1
+    g_down = dot_f32("ft,tr->fr", act, d2_full).astype(BF).reshape(seqs, ff, D)
+    d1_full, d1, sums1, g_last, g_down = exchange(
+        BACKWARD,
+        5,
+        seqs,
+        blocked(dot_f32("ft,fr->tr", dpre, up)),
+        d2,
+        norm_params[0:2],
+        normed=normed1,
+        inv=inv1,
+        rides=((SUM_ALONG, g_last), (SUM_ACROSS, g_down)),
     )
     d1_full = d1_full.reshape(length, D)
-    g_up = scatter_weights(dot_f32("ft,tr->fr", dpre, hidden_full).reshape(seqs, ff, D))
+    g_up = dot_f32("ft,tr->fr", dpre, hidden_full).astype(BF).reshape(seqs, ff, D)
     dmix = dot_f32("er,tr->et", m_out, d1_full).astype(BF).reshape(mix.shape)
     g_out = dot_f32("et,tr->er", mix_flat, d1_full)
     dq, dk, dv, doff_enc = attention_back(tiles, segq, segk, qkv, qkv, qkv, (0, 1, 2), lse, dmix, 1)
     dqkv = jnp.concatenate([dq, dk, dv], axis=1)
     g_qkv = dot_f32("snt,tr->snr", dqkv, x_full)
-    g_first = scatter_weights(jnp.concatenate([g_qkv, g_out.reshape(seqs, head_dim, D)], axis=1))
+    g_first = jnp.concatenate([g_qkv.astype(BF), g_out.astype(BF).reshape(seqs, head_dim, D)], axis=1)
     part_x = blocked(dot_f32("snt,snr->tr", dqkv, m_qkv))
 
     norm_grads = jnp.concatenate([sums1[:2], sums2[:2], sums3[:2]])
@@ -1111,7 +1406,9 @@
     spread = (heads[:, None] == jnp.arange(table_heads * cols)[None, :]).astype(F32)
     table_grads = jnp.einsum("thb,hg->tgb", table_grads, spread, precision=highest)
     small = jnp.concatenate([norm_grads.reshape(-1, 128), table_grads.reshape(-1, 128)])
-    grad_tokens, grad_streams, small = scatter_outputs(seqs, 6, part_x, part_y, d1, d3, small)
+    grad_tokens, grad_streams, small, g_down, g_up, g_first = scatter_outputs(
+        seqs, 6, part_x, part_y, d1, d3, small, g_down, g_up, g_first
+    )
     output, grad_streams = output.reshape(streams.shape), grad_streams.reshape(streams.shape)
     grad_tokens = grad_tokens.reshape(tokens.shape)
     count = norm_grads.size // 128
@@ -1141,8 +1438,10 @@
 
 
 def solution(mesh):
-    whole_row, half_col = mesh.shape["row"], mesh.shape["col"]
-    weights = (P("row", None, "col"), P("col", None), P("col", "row"), P("row"), P("row"), P("row", "col"), P("col", "row"), P("row"), P("row"), P("row", "col"), P("row", None, "col"), P("col", None), P("col", "row"), P("row"), P("row"))
+    whole_row, half_col = mesh.shape[ROW], mesh.shape[COL]
+    wide, table, norm = P(ROW, None, COL), P(COL, None), P(ROW)
+    up, down = P(ROW, COL), P(COL, ROW)
+    weights = (wide, table, down, norm, norm, up, down, norm, norm, up, wide, table, down, norm, norm)
 
     def run(tokens, *rest):
         micro_count = tokens.shape[0]
@@ -1153,8 +1452,8 @@
         return jax.shard_map(
             device_fn,
             mesh=mesh,
-            in_specs=(P(None, "col", "row"), P(None, None, "col", "row"), P(None, None, "col", "row"), P(None, "row", None), P()) + weights,
-            out_specs=(P(None, None, "col", "row"), P(None, "col", "row"), P(None, None, "col", "row")) + weights,
+            in_specs=(P(None, COL, ROW), P(None, None, COL, ROW), P(None, None, COL, ROW), P(None, ROW, None), P()) + weights,
+            out_specs=(P(None, None, COL, ROW), P(None, COL, ROW), P(None, None, COL, ROW)) + weights,
             check_vma=False,
         )(tokens, *rest)
 

time: 579 us -> 435 us (0.75)
  Pallas kernels: 267 us -> 355 us
  starting transfers between devices: 83.2 us -> 0 us
  waiting for transfers between devices: 75.2 us -> 0 us
  other arithmetic: 46 us -> 4.1 us
  local copies, waits for them, and re-layouts: 62 us -> 23.2 us
  matrix products: 36.7 us -> 43 us
    ppermute x40 -> x0, starting transfers between devices: 83.2 us -> none  [send(): return lax.ppermute(value, ('row', 'col'), pairs)]
    pallas_call x6, Pallas kernels: 153 us -> 230 us  [the longest x5 154 us: exchange(): pl.pallas_call(functools.partial(exchange_kernel, kind, count, pieces, se...]
    ppermute x40 -> x0, waiting for transfers between devices: 75.2 us -> none  [send(): return lax.ppermute(value, ('row', 'col'), pairs)]
    unnamed x208 -> x109, local copies, waits for them, and re-layouts: 33.1 us -> 18 us
    select_n x12 -> x0, other arithmetic: 14.8 us -> none  [in_order(): jnp.where(first, join([mine, other], axis=axis), join([other, mine], axis...]
    pallas_call x1, Pallas kernels: 62.9 us -> 74 us  [scatter_outputs(): pl.pallas_call(functools.partial(outputs_kernel, seqs, count), out_shape=...]
    convert_element_type x4 -> x0, other arithmetic: 10.4 us -> none  [scatter_weights(): low = part.astype(BF)]
    reshape x4 -> x0, local copies, waits for them, and re-layouts: 8.64 us -> none  [scatter_weights(): blocks = total.reshape(-1, 2, feat)]
  transfers between devices with their start and end apart: 40 -> 0, of which waited for: 11 -> 0; matrix products, arithmetic and copies ran while one was open for 19% -> 0% of each run, Pallas kernels for 29% -> 0%
where the time goes in v3:
time: 435 us; the launch traced here: 427 us
  Pallas kernels  355 us (82%)
  matrix products  43 us (10%)
  local copies, waits for them, and re-layouts  23.2 us (5%)
    pallas_call x5, Pallas kernels, exchange(): pl.pallas_call(functools.partial(exchange_kernel, kind, count, pieces, se...  154 us
    pallas_call x1, Pallas kernels, gather_inputs(): pl.pallas_call(functools.partial(inputs_kernel, seqs, len(packs)), out_sh...  75.9 us
    pallas_call x1, Pallas kernels, scatter_outputs(): pl.pallas_call(functools.partial(outputs_kernel, seqs, count), out_shape=...  74 us
    dot_general x21, matrix products, dot_f32(): return jnp.einsum(spec, left, right, preferred_element_type=F32)  42.3 us
    pallas_call x2, Pallas kernels, attention_back(): pl.pallas_call(functools.partial(bwd_kernel, streams, length, width), gri...  27.6 us
    pallas_call x2, Pallas kernels, attention(): pl.pallas_call(functools.partial(fwd_kernel, streams, length, width), gri...  23.1 us
    unnamed x109, local copies, waits for them, and re-layouts  18 us

profile of v3, /device:TPU:0, one launch (start us, length us, event | category | flops | bytes accessed | tf_op | source)
XLA Modules:
  0.0 427.3 jit_solution(8981867103457249440)
XLA Ops:
  0.8 1.2 copy.52
  2.1 1.0 copy.55
  3.1 0.9 copy.57
  4.1 0.9 pad_maximum_fusion.2
  5.4 75.9 %gather_inputs.1 = (bf16[1,128,1024]{2,1,0:T(8,128)(2,1)S(1)}, bf16[1,2,2,128,1024]{4,3,2,1,0:T(8,128)(2,1)}, bf16[3,128,1024]{2,1,0:T(8,128)(2,1)S(1)}, bf16[3,...) custom-call(bf16[2,1,2,128,256]{4,3,2,1,0:T(8,128)(2,1)S(1)} %bitcas, ...), custom_call_target="tpu_custom_call" | custom-call | tf_op jit(solution)/shard_map/gather_inputs/pallas_call | solution.py:1106
  82.1 2.7 convolution_convert_fusion.8.q_ref.k_ref.v_ref
  84.8 6.1 %attend.2 = (bf16[4,64,512]{2,1,0:T(8,128)(2,1)S(1)}, f32[4,1,512]{2,1,0:T(1,128)S(1)}, f32[4,896,128]{2,1,0:T(8,128)S(1)}) custom-call(f32[4,1,1024]{2,1,0:T(1,128)S(1)} %get-tuple-element.190.off_ref, s32[1,512]{1,0:T(1,128)S(1)} %fusion.72.segq_ref, s32[512,128]{1,0:T(8,128)S(1)} %broadcast_in_dim.7.segk_ref, ...), custom_call_target="tpu_custom_call" | custom-call | tf_op jit(solution)/shard_map/attend/pallas_call | solution.py:448
  90.9 1.5 bitcast_convert_fusion.4
  92.5 26.1 %exchange_1.1 = (bf16[1,2,2,128,1024]{4,3,2,1,0:T(8,128)(2,1)S(1)}, f32[1,128,1024]{2,1,0:T(8,128)S(1)}, f32[1,128,1024]{2,1,0:T(8,128)S(1)}, f32[1,128,1]{2,1,0...) custom-call(bf16[1,2,2,128,1024]{4,3,2,1,0:T(8,128)(2,1)S(1)} %bitca, ...), custom_call_target="tpu_custom_call", output_to_operand_aliasing={{4}: (3, {}), {5}: (4, {})} | custom-call | tf_op jit(solution)/shard_map/exchange_1/pallas_call | solution.py:975
  118.6 7.1 %multiply_convert_fusion = (bf16[1024,512]{1,0:T(8,128)(2,1)S(1)}, f32[1024,512]{1,0:T(8,128)}, f32[1024,512]{1,0:T(8,128)}) fusion(bf16[1024,1024]{1,0:T(8,128)(2,1)S(1)} %bitcast.201, bf16[512,1024]{1,0:T(8,128)(2,1)S(1)} %bitcast.186), kind=kOutput, calls=%fused_computation.12 | convolution fusion | flops 1107820544 | bytes 8388608 | tf_op jit(solution)/shard_map/fr,tr->ft/dot_general | solution.py:1238
  125.7 1.3 convolution_convert_fusion.6
  126.9 26.0 %exchange_2.1 = (bf16[1,2,2,128,1024]{4,3,2,1,0:T(8,128)(2,1)S(1)}, f32[1,128,1024]{2,1,0:T(8,128)}, f32[1,128,1024]{2,1,0:T(8,128)S(1)}, f32[1,128,1]{2,1,0:T(8,128)S(1)}, bf16[4,256,1024]{2,1,0:T(8,128)(2,1)}) custom-call(bf16[1,2,2,128,1024]{4,3,2,1,0:T(8,128)(2,1)S(1)} %bitcast.170, ...), custom_call_target="tpu_custom_call", output_to_operand_aliasing={{4}: (3, {})} | custom-call | tf_op jit(solution)/shard_map/exchange_2/pallas_call | solution.py:975
  153.0 2.4 convolution_convert_fusion.12.k_ref.v_ref
  155.4 1.0 convolution_convert_fusion.1.q_ref
  156.5 17.0 %attend.3 = (bf16[4,64,1536]{2,1,0:T(8,128)(2,1)S(1)}, f32[4,1,1536]{2,1,0:T(1,128)S(1)}, f32[4,896,128]{2,1,0:T(8,128)S(1)}) custom-call(f32[4,1,1024]{2,1,0:T(1,128)S(1)} %get-tuple-element.191.off_ref, s32[1,512]{1,0:T(1,128)S(1)} %fusion.72.segq_ref, s32[512,128]{1,0:T(8,128)S(1)} %broadcast_in_dim.7.segk_ref, ...), custom_call_target="tpu_custom_call" | custom-call | tf_op jit(solution)/shard_map/attend/pallas_call | solution.py:448
  173.5 2.7 bitcast_convert_fusion.1
  176.2 44.9 %exchange_3.1 = (bf16[3,2,2,128,1024]{4,3,2,1,0:T(8,128)(2,1)}, f32[2,3,2,128,256]{4,3,2,1,0:T(8,128)S(1)}, f32[3,128,1024]{2,1,0:T(8,128)}, f32[8,1024]{1,0:T(8,128)S(1)}) custom-call(bf16[3,2,2,128,1024]{4,3,2,1,0:T(8,128)(2,1)} %bitcast.198, bf16[3,128,1024]{2,1,0:T(8,128)(2,1)S(1)} %get-tuple-element.102.refs_1_, ...), custom_call_target="tpu_custom_call" | custom-call | tf_op jit(solution)/shard_map/exchange_3/pallas_call | solution.py:975
  221.2 2.9 convolution_convert_fusion
  224.1 19.9 %attend_back.2 = (bf16[4,64,1536]{2,1,0:T(8,128)(2,1)S(1)}, bf16[4,64,512]{2,1,0:T(8,128)(2,1)S(1)}, bf16[4,64,512]{2,1,0:T(8,128)(2,1)S(1)}, f32[4,1,1024]{2,1,0:T(1,128)S(1)}) custom-call(f32[4,896,128]{2,1,0:T(8,128)S(1)} %get-tuple-element.106.t_ref, s32[1,512]{1,0:T(1,128)S(1)} %fusion.72.segq_ref, s32[512,128]{1,0:T(8,128)S(1)} %broadcast_in_dim.7.segk_ref, ...), custom_call_target="tpu_custom_call" | custom-call | tf_op jit(solution)/shard_map/attend_back/pallas_call | solution.py:463
  244.8 1.4 copy-done.41
  246.2 1.0 convolution_convert_fusion.11
  247.2 0.8 copy-done.42
  248.1 1.0 convolution_convert_fusion.10
  249.1 1.6 pad_maximum_fusion.refs_5_
  250.7 1.7 bitcast_convert_fusion.3
  252.4 27.8 %exchange_4.1 = (bf16[1,2,2,128,1024]{4,3,2,1,0:T(8,128)(2,1)S(1)}, f32[1,128,1024]{2,1,0:T(8,128)S(1)}, f32[8,1024]{1,0:T(8,128)S(1)}, bf16[4,256,512]{2,1,0:T(8,128)(2,1)S(1)}) custom-call(bf16[1,2,2,128,1024]{4,3,2,1,0:T(8,128)(2,1)} %bitcast.209, f32[1,2,1024]{2,1,0:T(2,128)S(1)} %get-tuple-element.186.refs_1_, ...), custom_call_target="tpu_custom_call" | custom-call | tf_op jit(solution)/shard_map/exchange_4/pallas_call | solution.py:975
  280.2 2.6 convolution_convert_fusion.3
  284.2 1.9 add_convert_fusion
  286.1 2.2 convolution_convert_fusion.5
  288.3 29.4 %exchange_5.1 = (bf16[1,2,2,128,1024]{4,3,2,1,0:T(8,128)(2,1)S(1)}, f32[1,128,1024]{2,1,0:T(8,128)S(1)}, f32[8,1024]{1,0:T(8,128)S(1)}, f32[2,256,256]{2,1,0:T(8,128)S(1)}, bf16[4,256,512]{2,1,0:T(8,128)(2,1)}) custom-call(bf16[1,2,2,128,1024]{4,3,2,1,0:T(8,128)(2,1)} %bitcast.197, f32[1,128,1024]{2,1,0:T(8,128)S(1)} %get-tuple-element.115.refs_1_, ...), custom_call_target="tpu_custom_call" | custom-call | tf_op jit(solution)/shard_map/exchange_5/pallas_call | solution.py:975
  317.7 1.1 slice.118
  319.3 7.7 %attend_back.3 = (bf16[4,64,512]{2,1,0:T(8,128)(2,1)S(1)}, bf16[4,64,512]{2,1,0:T(8,128)(2,1)S(1)}, bf16[4,64,512]{2,1,0:T(8,128)(2,1)S(1)}, f32[4,1,1024]{2,1,0:T(1,128)S(1)}) custom-call(f32[4,896,128]{2,1,0:T(8,128)S(1)} %get-tuple-element.104.t_ref, s32[1,512]{1,0:T(1,128)S(1)} %fusion.72.segq_ref, s32[512,128]{1,0:T(8,128)S(1)} %broadcast_in_dim.7.segk_ref, ...), custom_call_target="tpu_custom_call" | custom-call | tf_op jit(solution)/shard_map/attend_back/pallas_call | solution.py:463
  327.1 1.0 convolution_convert_fusion.4
  328.6 1.5 pad_maximum_fusion.1.first
  330.1 2.6 convolution_convert_fusion.2
  333.4 4.1 bitcast_convert_fusion
  337.5 1.0 bitcast_convert_fusion.2
  338.5 74.0 %scatter_outputs.1 = (f32[2,2,128,256]{3,2,1,0:T(8,128)S(1)}, f32[2,3,2,128,256]{4,3,2,1,0:T(8,128)}, f32[56,128]{1,0:T(8,128)S(1)}, f32[2,256,256]{2,1,0:T(8,12...) custom-call(bf16[1,2,2,128,1024]{4,3,2,1,0:T(8,128)(2,1)S(1)} %bitcast.172, ...), custom_call_target="tpu_custom_call" | custom-call | tf_op jit(solution)/shard_map/scatter_outputs/pallas_call | solution.py:1222
  412.5 0.8 copy-done.3
  413.3 0.8 copy-done.5
  414.1 0.8 copy-done.7
  415.7 1.9 copy.63
  417.6 1.0 copy.64
  420.7 0.8 copy.66
  422.9 1.1 copy.84
  424.1 0.8 copy.85
  424.9 1.1 copy.86
  426.1 0.8 copy.87
  (141 shorter events, 9.3 us)
Async XLA Ops:
  0.7 4.3 %copy-start.27 = (bf16[256,512]{1,0:T(8,128)(2,1)S(1)}, bf16[256,512]{1,0:T(8,128)(2,1)}, u32[]{:S(2)}) copy-start(bf16[256,512]{1,0:T(8,128)(2,1)} %param.32) | copy-start | bytes 786436
  0.7 4.5 %copy-start.33 = (f32[256]{0:T(256)S(1)}, f32[256]{0:T(256)}, u32[]{:S(2)}) copy-start(f32[256]{0:T(256)} %param.30) | copy-start | bytes 3076
  0.7 4.5 %copy-start.34 = (f32[256]{0:T(256)S(1)}, f32[256]{0:T(256)}, u32[]{:S(2)}) copy-start(f32[256]{0:T(256)} %param.31) | copy-start | bytes 3076
  0.7 4.5 %copy-start.35 = (f32[256]{0:T(256)S(1)}, f32[256]{0:T(256)}, u32[]{:S(2)}) copy-start(f32[256]{0:T(256)} %param.34) | copy-start | bytes 3076
  0.7 4.5 %copy-start.36 = (f32[256]{0:T(256)S(1)}, f32[256]{0:T(256)}, u32[]{:S(2)}) copy-start(f32[256]{0:T(256)} %param.35) | copy-start | bytes 3076
  0.7 4.5 %copy-start.37 = (f32[256]{0:T(256)S(1)}, f32[256]{0:T(256)}, u32[]{:S(2)}) copy-start(f32[256]{0:T(256)} %param.40) | copy-start | bytes 3076
  0.7 4.5 %copy-start.31 = (f32[256]{0:T(256)S(1)}, f32[256]{0:T(256)}, u32[]{:S(2)}) copy-start(f32[256]{0:T(256)} %param.41) | copy-start | bytes 3076
  0.7 4.5 %copy-start.39 = (f32[2,32]{1,0:T(2,128)S(1)}, f32[2,32]{1,0:T(2,128)}, u32[]{:S(2)}) copy-start(f32[2,32]{1,0:T(2,128)} %param.28) | copy-start | bytes 772
  0.7 4.5 %copy-start.38 = (f32[2,32]{1,0:T(2,128)S(1)}, f32[2,32]{1,0:T(2,128)}, u32[]{:S(2)}) copy-start(f32[2,32]{1,0:T(2,128)} %param.38) | copy-start | bytes 772
  0.8 4.6 %copy-start.11 = (bf16[2,256,256]{2,1,0:T(8,128)(2,1)S(1)}, bf16[2,256,256]{2,1,0:T(8,128)(2,1)}, u32[]{:S(2)}) copy-start(bf16[2,256,256]{2,1,0:T(8,128)(2,1)} %param.22) | copy-start | bytes 786436
  0.8 4.6 %copy-start.12 = (bf16[512,256]{1,0:T(8,128)(2,1)S(1)}, bf16[512,256]{1,0:T(8,128)(2,1)}, u32[]{:S(2)}) copy-start(bf16[512,256]{1,0:T(8,128)(2,1)} %param.33) | copy-start | bytes 786436
  0.8 4.6 %copy-start.2 = (bf16[2,3,256,256]{3,2,1,0:T(8,128)(2,1)S(1)}, bf16[2,3,256,256]{3,2,1,0:T(8,128)(2,1)}, u32[]{:S(2)}) copy-start(bf16[2,3,256,256]{3,2,1,0:T(8,128)(2,1)} %param.23) | copy-start | bytes 2359300
  0.8 4.6 %copy-start.13 = (s32[2,1,512]{2,1,0:T(1,128)S(1)}, s32[2,1,512]{2,1,0:T(1,128)}, u32[]{:S(2)}) copy-start(s32[2,1,512]{2,1,0:T(1,128)} %param.25) | copy-start | bytes 12292
  3.1 78.5 %copy-start.32 = (s32[1023]{0:T(1024)S(1)}, s32[1023]{0:T(1024)}, u32[]{:S(2)}) copy-start(s32[1023]{0:T(1024)} %param.26) | copy-start | bytes 12280
  92.5 26.1 %copy-start.22 = (bf16[4,256,1024]{2,1,0:T(8,128)(2,1)S(1)}, bf16[4,256,1024]{2,1,0:T(8,128)(2,1)}, u32[]{:S(2)}) copy-start(bf16[4,256,1024]{2,1,0:T(8,128)(2,1)} %get-tuple-element.86) | copy-start | bytes 6291460
  118.5 7.1 %copy-start.9 = (f32[1,128,1024]{2,1,0:T(8,128)}, f32[1,128,1024]{2,1,0:T(8,128)S(1)}, u32[]{:S(2)}) copy-start(f32[1,128,1024]{2,1,0:T(8,128)S(1)} %get-tuple-element.116.refs_3_) | copy-start | bytes 1572868
  118.6 7.1 %copy-start.14 = (bf16[1,2,2,128,1024]{4,3,2,1,0:T(8,128)(2,1)}, bf16[1,2,2,128,1024]{4,3,2,1,0:T(8,128)(2,1)S(1)}, u32[]{:S(2)}) copy-start(bf16[1,2,2,128,1024]{4,3,2,1,0:T(8,128)(2,1)S(1)} %get-tuple-element.94) | copy-start | bytes 3145732
  118.6 7.1 %copy-start.20 = (bf16[4,256,1024]{2,1,0:T(8,128)(2,1)S(1)}, bf16[4,256,1024]{2,1,0:T(8,128)(2,1)}, u32[]{:S(2)}) copy-start(bf16[4,256,1024]{2,1,0:T(8,128)(2,1)} %get-tuple-element.95) | copy-start | bytes 6291460
  125.6 1.3 copy-start.25
  126.9 28.5 %copy-start.40 = (bf16[3,2,2,128,1024]{4,3,2,1,0:T(8,128)(2,1)S(1)}, bf16[3,2,2,128,1024]{4,3,2,1,0:T(8,128)(2,1)}, u32[]{:S(2)}) copy-start(bf16[3,2,2,128,1024]{4,3,2,1,0:T(8,128)(2,1)} %get-tuple-element.99) | copy-start | bytes 9437188
  153.0 3.5 copy-start.16
  153.0 2.4 copy-start.19
  173.5 2.8 copy-start.1
  224.1 20.0 %copy-start.17 = (bf16[1,2,2,128,1024]{4,3,2,1,0:T(8,128)(2,1)S(1)}, bf16[1,2,2,128,1024]{4,3,2,1,0:T(8,128)(2,1)}, u32[]{:S(2)}) copy-start(bf16[1,2,2,128,1024]{4,3,2,1,0:T(8,128)(2,1)} %copy-done.16) | copy-start | bytes 3145732
  244.0 3.2 copy-start.18
  244.0 2.2 copy-start.41
  246.2 1.9 copy-start.42
  252.4 27.8 %copy-start.26 = (bf16[1024,512]{1,0:T(8,128)(2,1)S(1)}, bf16[1024,512]{1,0:T(8,128)(2,1)}, u32[]{:S(2)}) copy-start(bf16[1024,512]{1,0:T(8,128)(2,1)} %copy-done.25) | copy-start | bytes 3145732
  280.2 2.7 copy-start
  280.2 2.6 copy-start.21
  280.2 3.3 copy-start.44
  280.2 4.0 copy-start.45
  284.2 1.9 copy-start.23
  286.1 2.3 copy-start.10
  319.3 7.8 %copy-start.43 = (bf16[1,2,2,128,1024]{4,3,2,1,0:T(8,128)(2,1)S(1)}, bf16[1,2,2,128,1024]{4,3,2,1,0:T(8,128)(2,1)}, u32[]{:S(2)}) copy-start(bf16[1,2,2,128,1024]{4,3,2,1,0:T(8,128)(2,1)} %get-tuple-element.88) | copy-start | bytes 3145732
  327.1 1.0 copy-start.29
  328.6 1.5 copy-start.15
  333.4 4.1 copy-start.28
  333.4 4.1 copy-start.30
  412.5 0.8 copy-start.3
  413.3 0.8 copy-start.5
  414.1 0.8 copy-start.7
  414.9 2.7 copy-start.8
  421.5 2.6 copy-start.6
  422.9 2.0 copy-start.24
  424.1 2.0 copy-start.4
